TPU v7x, 128 devices: a whole 4x4x4 slice. The times are simulated.
128 devices in a mesh: branch: 16 (over z_lo, y, core), head: 8 (over z_hi, x).
Axes of the slice: x: 4, y: 4, z: 4 (z_hi: 2, z_lo: 2; z = z_hi * 2 + z_lo), core: 2. Of those that a mesh axis runs over, the one named last changes fastest.
Arguments:
- queries: bfloat16 [16, 64, 3, 8192], P('branch', None, None, 'head'), may hold values from -16 to 16
- new_keys: bfloat16 [16, 64, 3, 1024], P('branch', None, None, 'head'), may hold values from -8 to 8
- new_values: bfloat16 [16, 64, 3, 1024], P('branch', None, None, 'head'), may hold values from -6 to 6
- prompt_keys: bfloat16 [8192, 1024], P('branch', 'head'), may hold values from -16 to 16
- prompt_values: bfloat16 [8192, 1024], P('branch', 'head'), may hold values from -6 to 6
- span_keys: bfloat16 [16, 64, 64, 1024], P('branch', None, None, 'head'), may hold values from -8 to 8
- span_values: bfloat16 [16, 64, 64, 1024], P('branch', None, None, 'head'), may hold values from -6 to 6
- span_lengths: int32 [64, 16], replicated, may hold values from 1 to 64, as said below
- join_offsets: int32 [64, 16], replicated, may hold values from 8192 to 9152, as said below
- pattern: int32 [16, 4, 16], P('branch'), may hold values 0 or 1
- out_weight: bfloat16 [8192, 8192], P('head'), may hold values from -0.0625 to 0.0625
Outputs:
- mixed: bfloat16 [16, 64, 3, 8192], P('branch')
- joined_keys: bfloat16 [64, 1024, 1024], P('branch', None, 'head')
- joined_values: bfloat16 [64, 1024, 1024], P('branch', None, 'head')
Inputs may be any that keep to these rules, and one draw needn't show every extreme that they name: `span_lengths`: each problem has at least one branch whose cache is full, 64 live slots; all branches of problem 0 are full. `join_offsets`: for each problem the branches are taken in some order and their live slots laid end to end after the 8192 prompt positions: a branch's offset is 8192 plus the live slots of the branches before it in that order.
All inputs are finite; a program needn't handle non-finite values. No bound on the sum of `pattern` on one device may be relied on, other than what follows from the above.
Results may differ from a plain program's by a relative error of at most 0.02.
Values may be sent and summed in bfloat16 or wider, within the bound.
No kernel may reach another device: no remote copies, remote signals or barrier semaphores. Data moves between devices by JAX's collectives and lax.ppermute only.
A program may use at most 128 MiB of HBM per device.

v0:
```python
import functools
import math

import jax
import jax.numpy as jnp
import numpy as np
from jax import lax
from jax.experimental import pallas as pl
from jax.experimental.pallas import tpu as pltpu
from jax.sharding import PartitionSpec as P

HEADS = 64
KVH = 8
HD = 128
GROUP = HEADS // KVH
STEPS = 3
SPAN = 64
BRANCHES = 16
QBLOCKS = 4
PROBS = 64
QP = PROBS // QBLOCKS
PIECES = STEPS * GROUP
TILE = PIECES * QP
P_DEV = 512
CHUNK = 512

rope_base = 500000.0
masked_score = -1e30
SCALE2 = math.log2(math.e) / math.sqrt(HD)
VMEM = 60 * 1024 * 1024
PART = 46 * 1024 * 1024
LITTLE = 24 * 1024 * 1024
LIGHT = pl.CostEstimate(flops=0, bytes_accessed=0, transcendentals=0)


def params(limit=VMEM):
    return pltpu.CompilerParams(dimension_semantics=("arbitrary",), vmem_limit_bytes=limit)


def tables(position):
    half = HD // 2
    exponent = np.arange(half) * (2.0 / HD)
    frequency = np.tile(np.exp(-math.log(rope_base) * exponent), 2).astype(np.float32)
    sign = np.repeat(np.float32([-1.0, 1.0]), half)
    angle = position.astype(jnp.float32)[..., None] * frequency
    return jnp.cos(angle), jnp.sin(angle) * sign


def turn(values, cosine, sine):
    return values * cosine + pltpu.roll(values, HD // 2, values.ndim - 1) * sine


def with_ones(values):
    return jnp.concatenate([values, jnp.ones_like(values)], 1)


def dot(a, b):
    return jnp.dot(a, b, preferred_element_type=jnp.float32)


def span_kernel(
    len_ref, me_ref, q_ref, cos_ref, sin_ref, nk_ref, nv_ref, sk_ref, sv_ref,
    q_out, m_out, acc_out, sent_out,
):
    first = pl.program_id(0) * QP
    lane = lax.broadcasted_iota(jnp.int32, (1, QP * SPAN), 1)
    code = jnp.full((1, QP * SPAN), -1, jnp.int32)
    for p in range(QP):
        live = len_ref[me_ref[0], first + p]
        code = jnp.where((lane >= p * SPAN) & (lane < p * SPAN + live), p, code)
    rotated = {}
    for g in range(GROUP):
        for s in range(STEPS):
            lanes = slice(g * HD, (g + 1) * HD)
            raw = q_ref[s, :, lanes].astype(jnp.float32)
            rotated[g, s] = turn(raw, cos_ref[s], sin_ref[s])
            q_out[s, :, lanes] = rotated[g, s].astype(jnp.bfloat16)
    fresh = [
        turn(nk_ref[s].astype(jnp.float32), cos_ref[s], sin_ref[s]).astype(jnp.bfloat16)
        for s in range(STEPS)
    ]
    pad = jnp.zeros((HD - STEPS * QP, HD), jnp.bfloat16)
    fresh_keys = jnp.concatenate(fresh + [pad], 0).T
    fresh_vals = with_ones(jnp.concatenate([nv_ref[s] for s in range(STEPS)] + [pad], 0))
    few = QP // 2
    rows = few * PIECES
    keys_of = few * SPAN
    row = lax.broadcasted_iota(jnp.int32, (rows, 1), 0)
    piece = row >> 3
    step = piece - 3 * ((piece * 22) >> 6)
    fresh_lane = lax.broadcasted_iota(jnp.int32, (1, HD), 1)
    for part in range(2):
        low = part * few
        prob = (row & (few - 1)) + low
        q = jnp.concatenate(
            [rotated[g, s][low : low + few] for g in range(GROUP) for s in range(STEPS)], 0
        ).astype(jnp.bfloat16)
        span_keys = sk_ref[low : low + few].reshape(keys_of, HD).T
        span_vals = with_ones(sv_ref[low : low + few].reshape(keys_of, HD))
        s1 = jnp.where(
            code[:, part * keys_of : (part + 1) * keys_of] == prob, dot(q, span_keys), masked_score
        )
        ok = ((fresh_lane & (QP - 1)) == prob) & ((fresh_lane >> 4) <= step)
        s2 = jnp.where(ok, dot(q, fresh_keys), masked_score)
        top = jnp.maximum(s1.max(1, keepdims=True), s2.max(1, keepdims=True)) * SCALE2
        p1 = jnp.exp2(s1 * SCALE2 - top).astype(jnp.bfloat16)
        p2 = jnp.exp2(s2 * SCALE2 - top).astype(jnp.bfloat16)
        total = dot(p1, span_vals) + dot(p2, fresh_vals)
        wide = jnp.broadcast_to(top, (rows, HD))
        for k in range(PIECES):
            m_out[0, k * QP + low : k * QP + low + few, :] = wide[k * few : (k + 1) * few]
            acc_out[0, k * QP + low : k * QP + low + few, :] = total[k * few : (k + 1) * few]
    keys = sk_ref[...].astype(jnp.float32)
    kcos = cos_ref[STEPS][:, None, :]
    ksin = sin_ref[STEPS][:, None, :]
    sent_out[:, :, :HD] = turn(keys, kcos, ksin).astype(jnp.bfloat16)
    sent_out[:, :, HD:] = sv_ref[...]


def span_part(
    lengths, me, queries, cosine, sine, new_keys, new_values, span_keys, span_values
):
    three = lambda width: pl.BlockSpec((STEPS, QP, width), lambda i, *_: (0, i, 0))
    span = lambda width: pl.BlockSpec((QP, SPAN, width), lambda i, *_: (i, 0, 0))
    table = pl.BlockSpec((STEPS + 1, QP, HD), lambda i, *_: (0, i, 0))
    state = lambda width: pl.BlockSpec((1, TILE, width), lambda i, *_: (i, 0, 0))
    wide = GROUP * HD
    return pl.pallas_call(
        span_kernel,
        grid_spec=pltpu.PrefetchScalarGridSpec(
            num_scalar_prefetch=2,
            grid=(QBLOCKS,),
            in_specs=[
                three(wide), table, table, three(HD), three(HD), span(HD), span(HD),
            ],
            out_specs=[three(wide), state(HD), state(2 * HD), span(2 * HD)],
        ),
        out_shape=[
            jax.ShapeDtypeStruct((STEPS, PROBS, wide), jnp.bfloat16),
            jax.ShapeDtypeStruct((QBLOCKS, TILE, HD), jnp.float32),
            jax.ShapeDtypeStruct((QBLOCKS, TILE, 2 * HD), jnp.float32),
            jax.ShapeDtypeStruct((PROBS, SPAN, 2 * HD), jnp.bfloat16),
        ],
        compiler_params=params(),
        cost_estimate=LIGHT,
    )(lengths, me, queries, cosine, sine, new_keys, new_values, span_keys, span_values)


def pack_kernel(keys_ref, vals_ref, out):
    for c in range(0, P_DEV, HD):
        out[c : c + HD, :] = keys_ref[c : c + HD, :].T
    out[P_DEV:, :] = vals_ref[...]


def pack_block(keys, vals):
    return pl.pallas_call(
        pack_kernel,
        out_shape=jax.ShapeDtypeStruct((2 * P_DEV, HD), jnp.bfloat16),
        compiler_params=pltpu.CompilerParams(vmem_limit_bytes=VMEM),
        cost_estimate=LIGHT,
    )(keys, vals)


def attend(picks, valid, kv, qs, m_ref, acc_ref):
    rows = 128
    keys = []
    vals = []
    for k in picks:
        flat = jnp.concatenate([kv[k, c : c + HD, :] for c in range(0, P_DEV, HD)], 1)
        keys.append(jnp.concatenate([flat, flat], 0))
        vals.append(with_ones(kv[k, P_DEV:, :]))
    for r0 in range(0, TILE, rows):
        at = slice(r0, r0 + rows)
        query = qs[at, :]
        old = m_ref[at, :]
        scores = [jnp.dot(query, key, preferred_element_type=jnp.float32) for key in keys]
        top = old
        for value, ok in zip(scores, valid):
            best = value.max(1, keepdims=True)
            top = jnp.maximum(top, best if ok is None else jnp.where(ok, best, masked_score))
        factor = jnp.exp2(old - top)
        total = acc_ref[at, :] * jnp.concatenate([factor, factor], 1)
        for value, val, ok in zip(scores, vals, valid):
            base = top if ok is None else jnp.where(ok, top, -masked_score)
            weights = jnp.concatenate(
                [
                    jnp.exp2(value[:, c : c + HD] - base).astype(jnp.bfloat16)
                    for c in range(0, P_DEV, HD)
                ],
                1,
            )
            total = total + jnp.dot(weights, val, preferred_element_type=jnp.float32)
        m_ref[at, :] = top
        acc_ref[at, :] = total


def attend_active(places, pat_ref, me_ref, picked, kv, qs, m_ref, acc_ref):
    i = pl.program_id(0)
    me = me_ref[0]
    for k in range(len(places) + 4):
        picked[k] = 0
    count = jnp.int32(0)
    for k, (dz, dy, other) in enumerate(places):
        picked[count] = k
        owner = chip_of(me, dz, -dy) + ((me & 1) ^ other)
        count = count + jnp.where(pat_ref[i, owner] > 0, 1, 0)
    fours = (count + 1) // 4

    def four(t, carry):
        base = 4 * t
        attend(
            [picked[base + k] for k in range(4)],
            [None, None, None, base + 3 < count],
            kv, qs, m_ref, acc_ref,
        )
        return carry

    lax.fori_loop(0, fours, four, 0)

    @pl.when(4 * fours < count)
    def _():
        base = 4 * fours
        attend(
            [picked[base], picked[base + 1]], [None, base + 1 < count], kv, qs, m_ref, acc_ref
        )


def load_state(q_ref, m_in, acc_in, qs, m_ref, acc_ref):
    for g in range(GROUP):
        for s in range(STEPS):
            at = (g * STEPS + s) * QP
            scaled = q_ref[s, :, g * HD : (g + 1) * HD].astype(jnp.float32) * SCALE2
            high = scaled.astype(jnp.bfloat16)
            qs[at : at + QP, :HD] = high
            qs[at : at + QP, HD:] = (scaled - high.astype(jnp.float32)).astype(jnp.bfloat16)
    m_ref[...] = m_in[0]
    acc_ref[...] = acc_in[0]


def prompt_kernel(
    places, groups, stacks, pat_ref, me_ref, head_ref, q_ref, m_in, acc_in, *refs
):
    blocks, weight, refs = refs[:stacks], refs[stacks], refs[stacks + 1 :]
    outs, att = refs[: len(groups)], refs[len(groups)]
    qs, m_ref, acc_ref, kv, picked, w_s, o_s, sems, w_sems, o_sems = refs[len(groups) + 1 :]
    i = pl.program_id(0)
    sizes = [ref.shape[0] for ref in blocks]
    copies = [
        pltpu.make_async_copy(ref, kv.at[pl.ds(sum(sizes[:k]), sizes[k])], sems.at[k])
        for k, ref in enumerate(blocks)
    ]
    chunks = [(k, j, place) for k, group in enumerate(groups) for j, place in enumerate(group)]
    each = -(-len(chunks) // QBLOCKS)

    def weight_copy(n):
        return pltpu.make_async_copy(
            weight.at[:, chunk_at(head_ref, chunks[n][2])], w_s.at[n], w_sems.at[n]
        )

    def out_copy(n):
        k, j, _ = chunks[n]
        return pltpu.make_async_copy(o_s.at[n], outs[k].at[j], o_sems.at[n])

    @pl.when(i == 0)
    def _():
        for copy in copies:
            copy.start()

    load_state(q_ref, m_in, acc_in, qs, m_ref, acc_ref)

    @pl.when(i == 0)
    def _():
        for copy in copies:
            copy.wait()

    for step in range(QBLOCKS):

        @pl.when(i == step)
        def _(step=step):
            for n in range(step * each, min((step + 1) * each, len(chunks))):
                weight_copy(n).start()

    attend_active(places, pat_ref, me_ref, picked, kv, qs, m_ref, acc_ref)
    done = (acc_ref[:, :HD] / acc_ref[:, HD:]).astype(jnp.bfloat16)
    for g in range(GROUP):
        for s in range(STEPS):
            at = (g * STEPS + s) * QP
            row = pl.multiple_of(s * PROBS + i * QP, QP)
            att[pl.ds(row, QP), g * HD : (g + 1) * HD] = done[at : at + QP]

    @pl.when(i == QBLOCKS - 1)
    def _():
        for n in range(len(chunks)):
            weight_copy(n).wait()
            o_s[n] = dot(att[...], w_s[n]).astype(jnp.bfloat16)
            out_copy(n).start()
        for n in range(len(chunks)):
            out_copy(n).wait()


def prompt_part(pattern, me, head, places, groups, query, top, accum, stacks, weight):
    wide = GROUP * HD
    three = pl.BlockSpec((STEPS, QP, wide), lambda i, *_: (0, i, 0))
    state = lambda width: pl.BlockSpec((1, TILE, width), lambda i, *_: (i, 0, 0))
    anywhere = pl.BlockSpec(memory_space=pl.ANY)
    rows = STEPS * PROBS
    depth = weight.shape[0]
    chunks = sum(len(group) for group in groups)
    return pl.pallas_call(
        functools.partial(prompt_kernel, places, groups, len(stacks)),
        grid_spec=pltpu.PrefetchScalarGridSpec(
            num_scalar_prefetch=3,
            grid=(QBLOCKS,),
            in_specs=[three, state(HD), state(2 * HD)] + [anywhere] * (len(stacks) + 1),
            out_specs=[anywhere] * len(groups) + [pl.BlockSpec((rows, wide), lambda i, *_: (0, 0))],
            scratch_shapes=[
                pltpu.VMEM((TILE, 2 * HD), jnp.bfloat16),
                pltpu.VMEM((TILE, HD), jnp.float32),
                pltpu.VMEM((TILE, 2 * HD), jnp.float32),
                pltpu.VMEM((len(places), 2 * P_DEV, HD), jnp.bfloat16),
                pltpu.SMEM((len(places) + 4,), jnp.int32),
                pltpu.VMEM((chunks, depth, CHUNK), jnp.bfloat16),
                pltpu.VMEM((chunks, rows, CHUNK), jnp.bfloat16),
                pltpu.SemaphoreType.DMA((len(stacks),)),
                pltpu.SemaphoreType.DMA((chunks,)),
                pltpu.SemaphoreType.DMA((chunks,)),
            ],
        ),
        out_shape=[
            jax.ShapeDtypeStruct((len(group), rows, CHUNK), jnp.bfloat16) for group in groups
        ]
        + [jax.ShapeDtypeStruct((rows, wide), jnp.bfloat16)],
        compiler_params=params(),
        cost_estimate=LIGHT,
    )(pattern, me, head, query, top, accum, *stacks, weight)


def flip(r):
    return (0x36 >> (2 * r)) & 3


def column(head, base, far, r):
    return base + (((head // 4) ^ far) * 4) + ((head & 3) ^ flip(r))


def project_kernel(places, head_ref, a_ref, w_ref, out):
    out[0] = dot(a_ref[...], w_ref[...]).astype(jnp.bfloat16)


def project(attended, weight, head, places):
    rows, depth = attended.shape

    def chunk(i, head):
        found = jnp.int32(0)
        for k, place in enumerate(places):
            found = jnp.where(i == k, column(head[0], *place), found)
        return (0, found)

    return pl.pallas_call(
        functools.partial(project_kernel, places),
        grid_spec=pltpu.PrefetchScalarGridSpec(
            num_scalar_prefetch=1,
            grid=(len(places),),
            in_specs=[
                pl.BlockSpec((rows, depth), lambda i, head: (0, 0)),
                pl.BlockSpec((depth, CHUNK), chunk),
            ],
            out_specs=pl.BlockSpec((1, rows, CHUNK), lambda i, head: (i, 0, 0)),
        ),
        out_shape=jax.ShapeDtypeStruct((len(places), rows, CHUNK), jnp.bfloat16),
        compiler_params=params(PART),
        cost_estimate=LIGHT,
    )(head, attended, weight)


def chunk_at(head_ref, place):
    return pl.ds(pl.multiple_of(column(head_ref[0], *place) * CHUNK, CHUNK), CHUNK)


def row_starts(places, refs):
    starts = []
    for k, group in enumerate(places):
        starts.append(refs[k].shape[1] if k and group == places[k - 1] else 0)
    return starts


def assemble_kernel(places, head_ref, *refs):
    for ref, group, row in zip(refs[:-1], places, row_starts(places, refs)):
        for j, place in enumerate(group):
            refs[-1][row : row + ref.shape[1], chunk_at(head_ref, place)] = ref[j]


def assemble(head, places, sources):
    rows = STEPS * PROBS
    whole = lambda value: pl.BlockSpec(value.shape, lambda i, head: (0, 0, 0))
    return pl.pallas_call(
        functools.partial(assemble_kernel, places),
        grid_spec=pltpu.PrefetchScalarGridSpec(
            num_scalar_prefetch=1,
            grid=(1,),
            in_specs=[whole(value) for value in sources],
            out_specs=pl.BlockSpec((rows, 16 * CHUNK), lambda i, head: (0, 0)),
        ),
        out_shape=jax.ShapeDtypeStruct((rows, 16 * CHUNK), jnp.bfloat16),
        compiler_params=params(LITTLE),
        cost_estimate=LIGHT,
    )(head, *sources)


def complete_kernel(places, head_ref, earlier, *refs):
    sources, out, sems = refs[:-2], refs[-2], refs[-1]
    copies = []
    for ref, group, row in zip(sources, places, row_starts(places, sources)):
        for j, place in enumerate(group):
            goal = out.at[row : row + ref.shape[1], chunk_at(head_ref, place)]
            copies.append(pltpu.make_async_copy(ref.at[j], goal, sems.at[len(copies)]))
    for copy in copies:
        copy.start()
    for copy in copies:
        copy.wait()


def complete(head, places, earlier, sources):
    anywhere = pl.BlockSpec(memory_space=pl.ANY)
    return pl.pallas_call(
        functools.partial(complete_kernel, places),
        grid_spec=pltpu.PrefetchScalarGridSpec(
            num_scalar_prefetch=1,
            grid=(1,),
            in_specs=[anywhere]
            + [pl.BlockSpec(value.shape, lambda i, head: (0, 0, 0)) for value in sources],
            out_specs=anywhere,
            scratch_shapes=[pltpu.SemaphoreType.DMA((sum(len(g) for g in places),))],
        ),
        out_shape=jax.ShapeDtypeStruct(earlier.shape, earlier.dtype),
        input_output_aliases={1: 0},
        compiler_params=params(LITTLE),
        cost_estimate=LIGHT,
    )(head, earlier, *sources)


def join_kernel(first_ref, begin_ref, len_ref, source, keys_out, vals_out):
    problem = first_ref[0] + pl.program_id(0)
    total = BRANCHES * SPAN
    flat = source[:, 0].reshape(total, 2 * HD)
    lane = lax.broadcasted_iota(jnp.int32, (1, total), 1)
    target = jnp.full((1, total), -1, jnp.int32)
    for b in range(BRANCHES):
        live = (lane >= b * SPAN) & (lane < b * SPAN + len_ref[b, problem])
        begin = begin_ref[b, problem] - P_DEV * BRANCHES - b * SPAN
        target = jnp.where(live, lane + begin, target)
    rows = 256
    for r0 in range(0, total, rows):
        slot = lax.broadcasted_iota(jnp.int32, (rows, 1), 0) + r0
        pick = jnp.where(target == slot, 1.0, 0.0).astype(jnp.bfloat16)
        got = jnp.dot(pick, flat, preferred_element_type=jnp.float32).astype(jnp.bfloat16)
        keys_out[0, r0 : r0 + rows, :] = got[:, :HD]
        vals_out[0, r0 : r0 + rows, :] = got[:, HD:]


def join(first, begins, lengths, source):
    share = source.shape[1]
    total = BRANCHES * SPAN
    out = pl.BlockSpec((1, total, HD), lambda i, *_: (i, 0, 0))
    shape = jax.ShapeDtypeStruct((share, total, HD), jnp.bfloat16)
    return pl.pallas_call(
        join_kernel,
        grid_spec=pltpu.PrefetchScalarGridSpec(
            num_scalar_prefetch=3,
            grid=(share,),
            in_specs=[pl.BlockSpec((BRANCHES, 1, SPAN, 2 * HD), lambda i, *_: (0, i, 0, 0))],
            out_specs=[out, out],
        ),
        out_shape=[shape, shape],
        compiler_params=params(LITTLE),
        cost_estimate=LIGHT,
    )(first, begins, lengths, source)


def chip_of(branch, dz, dy):
    return ((branch // 8) ^ dz) * 8 + ((branch // 2 + dy) % 4) * 2


def move_chip(value, dz, dy):
    perm = [(b, chip_of(b, dz, dy) + b % 2) for b in range(BRANCHES)]
    return lax.ppermute(value, "branch", perm)


def swap_core(value):
    return lax.ppermute(value, "branch", [(b, b ^ 1) for b in range(BRANCHES)])


def move_x(value, flip):
    return lax.ppermute(value, "head", [(h, h ^ flip) for h in range(KVH)])


def move_roles(o, p, q):
    return move_x(p, 1), move_x(q, 3), move_x(o, 2)


def add(*values):
    total = values[0].astype(jnp.float32)
    for value in values[1:]:
        total = total + value.astype(jnp.float32)
    return total.astype(jnp.bfloat16)


def after(value, *others):
    return lax.optimization_barrier((value, others))[0]


def shards(
    queries, new_keys, new_values, prompt_keys, prompt_values, span_keys, span_values,
    span_lengths, join_offsets, pattern, out_weight,
):
    me = lax.axis_index("branch")
    one = me.reshape(1)
    head = lax.axis_index("head").reshape(1)
    prompt_len = P_DEV * BRANCHES
    share = PROBS // BRANCHES

    own = pack_block(prompt_keys, prompt_values)
    near_at = [(0, 0), (1, 0), (0, 1), (0, 3)]
    far_at = [(0, 2), (1, 1), (1, 3), (1, 2)]
    near = [own] + [move_chip(own, dz, dy) for dz, dy in near_at[1:]]
    far = [move_chip(own, 0, 2)] + [move_chip(near[1], 0, dy) for _, dy in far_at[1:]]

    lengths = span_lengths.T
    offsets = join_offsets.T
    live = lax.dynamic_slice_in_dim(lengths, me, 1, 0)
    shift = lax.dynamic_slice_in_dim(offsets, me, 1, 0) - prompt_len
    steps = jnp.arange(STEPS, dtype=jnp.int32)[:, None]
    cosine, sine = tables(jnp.concatenate([prompt_len + live + steps, shift]))
    query, top, accum, sent = span_part(
        lengths,
        one,
        jnp.transpose(queries[0], (1, 0, 2)),
        cosine,
        sine,
        jnp.transpose(new_keys[0], (1, 0, 2)),
        jnp.transpose(new_values[0], (1, 0, 2)),
        span_keys[0],
        span_values[0],
    )

    near, far = after((near, far), query)
    near_stack, far_stack = jnp.stack(near), jnp.stack(far)
    near_other, far_other = swap_core(near_stack), swap_core(far_stack)
    sent = after(sent, near_stack, far_stack).reshape(BRANCHES, share, SPAN, 2 * HD)
    gathered = lax.all_to_all(sent, "branch", 0, 0, tiled=True)
    places = [(dz, dy, c) for at in (near_at, far_at) for c in (0, 1) for dz, dy in at]
    stacks = [near_stack, near_other, far_stack, far_other]

    half = 8
    roles = range(4)
    both = [[(0, far, r) for far in (1, 0)] for r in roles]
    zhere = [(half, 0, r) for r in roles]
    zthere = [(half, 1, r) for r in roles]
    zsend, xo, xp, xq, attended = prompt_part(
        pattern[0], one, head, places, [zthere] + both[:3], query, top, accum, stacks, out_weight
    )
    got_z = move_x(zsend, 4)
    got_x = move_roles(xo, xp, xq)
    kept = project(attended, out_weight, head, zhere + both[3])
    got_z = after(got_z, got_x)
    rows = STEPS * PROBS // 2
    halves = [slice(k, k + rows) for k in (0, rows)]
    zpart = [[add(kept[r][h], got_z[r][h]) for r in roles] for h in halves]
    got_zx = [move_roles(*part[:3]) for part in zpart]
    got_x = after(got_x, zpart[1][3], gathered)
    xsum = add(kept[4:], *got_x)
    got_zx[1] = after(got_zx[1], xsum)
    zsum = [add(part[3], *got) for part, got in zip(zpart, got_zx)]

    pair = add(xsum, move_x(xsum, 4)[::-1])
    zback = [move_roles(part, part, part) for part in zsum]
    zback[1] = after(zback[1], pair)
    zfour = [jnp.stack([zo, zp, zq, part]) for (zp, zq, zo), part in zip(zback, zsum)]
    zother = [move_x(part, 4) for part in zfour]
    xp, xq, xo = move_roles(pair, pair, pair)
    joined_keys, joined_values = join(
        (me * share).reshape(1), offsets, lengths, after(gathered, zfour[1])
    )
    mixed = assemble(head, [both[3], zhere, zhere], after([pair] + zfour, joined_keys))
    mixed = complete(head, [zthere, zthere] + both[:3], mixed, zother + [xo, xp, xq])
    mixed = jnp.transpose(mixed.reshape(STEPS, PROBS, 16 * CHUNK), (1, 0, 2))[None]
    return mixed, joined_keys, joined_values


def solution(mesh):
    return jax.shard_map(
        shards,
        mesh=mesh,
        in_specs=(
            P("branch", None, None, "head"),
            P("branch", None, None, "head"),
            P("branch", None, None, "head"),
            P("branch", "head"),
            P("branch", "head"),
            P("branch", None, None, "head"),
            P("branch", None, None, "head"),
            P(),
            P(),
            P("branch", None, None),
            P("head", None),
        ),
        out_specs=(
            P("branch", None, None, None),
            P("branch", None, "head"),
            P("branch", None, "head"),
        ),
        check_vma=False,
    )
```

profile of v0, /device:TPU:8, one launch (start us, length us, event | category | flops | bytes accessed | tf_op | source)
XLA Modules:
  0.0 137.7 jit_solution(10838531295300571694)
XLA Ops:
  0.6 1.8 %shard_map.149 = bf16[1024,128]{1,0:T(8,128)(2,1)} custom-call(bf16[512,128]{1,0:T(8,128)(2,1)} %keys_ref.1, bf16[512,128]{1,0:T(8,128)(2,1)} %vals_ref.1), custom_call_target="tpu_custom_call" | custom-call | tf_op jit(solution)/shard_map/pallas_call | solution.py:156
  2.4 1.9 %collective-permute-start = (bf16[1024,128]{1,0:T(8,128)(2,1)}, bf16[1024,128]{1,0:T(8,128)(2,1)S(1)}, u32[]{:S(2)}, u32[]{:S(2)}) collective-permute-start(bf16[1024,128]{1,0:T(8,128)(2,1)} %shard_map.149), channel_id=1, source_target_pairs={{0,64},{8,72},{16,80},{24,88},{32,96},{40,104},{48,112},{56,120},{... | collective-permute-start | bytes 786440 | tf_op jit(solution)/shard_map/ppermute | solution.py:486
  4.3 1.6 %collective-permute-start.1 = (bf16[1024,128]{1,0:T(8,128)(2,1)}, bf16[1024,128]{1,0:T(8,128)(2,1)S(1)}, u32[]{:S(2)}, u32[]{:S(2)}) collective-permute-start(bf16[1024,128]{1,0:T(8,128)(2,1)} %shard_map.149), channel_id=1, source_target_pairs={{0,16},{8,24},{16,32},{24,40},{32,48},{40,56},{48,0},{56,8},{64,80... | collective-permute-start | bytes 786440 | tf_op jit(solution)/shard_map/ppermute | solution.py:486
  6.3 2.3 %collective-permute-start.3 = (bf16[1024,128]{1,0:T(8,128)(2,1)}, bf16[1024,128]{1,0:T(8,128)(2,1)S(1)}, u32[]{:S(2)}, u32[]{:S(2)}) collective-permute-start(bf16[1024,128]{1,0:T(8,128)(2,1)} %shard_map.149), channel_id=1, source_target_pairs={{0,32},{8,40},{16,48},{24,56},{32,0},{40,8},{48,16},{56,24},{64,96... | collective-permute-start | bytes 786440 | tf_op jit(solution)/shard_map/ppermute | solution.py:486
  8.6 0.7 add_bitcast_fusion.1
  9.3 0.7 add_bitcast_fusion
  10.0 0.8 collective-permute-done
  10.8 1.6 %collective-permute-start.4 = (bf16[1024,128]{1,0:T(8,128)(2,1)S(1)}, bf16[1024,128]{1,0:T(8,128)(2,1)S(1)}, u32[]{:S(2)}, u32[]{:S(2)}) collective-permute-start(bf16[1024,128]{1,0:T(8,128)(2,1)S(1)} %collective-permute-done), channel_id=1, source_target_pairs={{0,16},{8,24},{16,32},{24,40},{32,48},{40,56},{48,0},{56,8},{64,80... | collective-permute-start | bytes 786440 | tf_op jit(solution)/shard_map/ppermute | solution.py:486
  12.8 3.5 %collective-permute-done.1 = bf16[1024,128]{1,0:T(8,128)(2,1)S(1)} collective-permute-done((bf16[1024,128]{1,0:T(8,128)(2,1)}, bf16[1024,128]{1,0:T(8,128)(2,1)S(1)}, u32[]{:S(2)}, u32[]{:S(2)}) %collective-permute-start.1) | collective-permute-done | bytes 262176 | tf_op jit(solution)/shard_map/ppermute | solution.py:486
  16.4 1.9 %fusion.3 = (f32[4,64,128]{2,1,0:T(8,128)}, f32[4,64,128]{2,1,0:T(8,128)}) fusion(f32[128]{0:T(128)} %constant.24.clone, f32[128]{0:T(128)} %constant.23.clone, f32[4,64]{1,0:T(4,128)S(1)} %add_convert_fusion.11), kind=kLoop, calls=%fused_computation.21 | loop fusion | flops 65536 | bytes 264192 | tf_op jit(solution)/shard_map/mul | solution.py:46
  18.3 7.4 %shard_map.148 = (bf16[3,64,1024]{2,1,0:T(8,128)(2,1)}, f32[4,384,128]{2,1,0:T(8,128)}, f32[4,384,256]{2,1,0:T(8,128)}, bf16[64,64,256]{2,1,0:T(8,128)(2,1)}) custom-call(s32[16,64]{1,0:T(8,128)} %bitcast.62, s32[1]{0:T(128)} %bitcast.2.me_ref, bf16[3,64,1024]{2,1,0:T(8,128)(2,1)} %bitcast.70, f32[4,64,128]{2,1,0:T(8,128)} %get-tuple-element.79.cos_ref, ...), custom_call_target="tpu_custom_call" | custom-call | tf_op jit(solution)/shard_map/pallas_call | solution.py:128
  25.8 5.4 %collective-permute-done.6 = bf16[1024,128]{1,0:T(8,128)(2,1)S(1)} collective-permute-done((bf16[1024,128]{1,0:T(8,128)(2,1)S(1)}, bf16[1024,128]{1,0:T(8,128)(2,1)S(1)}, u32[]{:S(2)}, u32[]{:S(2)}) %collective-permute-start.6) | collective-permute-done | bytes 262176 | tf_op jit(solution)/shard_map/ppermute | solution.py:486
  31.5 1.2 pad_maximum_fusion.refs_0_
  33.0 4.4 %all-to-all-start = ((bf16[16,4,64,256]{3,2,1,0:T(8,128)(2,1)}), bf16[16,4,64,256]{3,2,1,0:T(8,128)(2,1)S(1)}, u32[]{:S(2)}, u32[]{:S(2)}) async-start(bf16[16,4,64,256]{3,2,1,0:T(8,128)(2,1)} %bitcast.66), calls=%async_computation | async-start | bytes 4194304 | tf_op jit(solution)/shard_map/all_to_all | solution.py:550
  37.5 23.7 %shard_map.150 = (bf16[4,192,512]{2,1,0:T(8,128)(2,1)}, bf16[2,192,512]{2,1,0:T(8,128)(2,1)}, bf16[2,192,512]{2,1,0:T(8,128)(2,1)}, bf16[2,192,512]{2,1,0:T(8,128)(2,1)}, bf16[192,1024]{1,0:T(8,128)(2,1)}) custom-call(s32[4,16]{1,0:T(4,128)} %bitcast.88, s32[1]{0:T(128)} %bitcast.2.me_ref, s32[1]{0:T(128)} %bitcast.head_ref, ...), custom_call_target="tpu_custom_call" | custom-call | tf_op jit(solution)/shard_map/pallas_call | solution.py:309
  61.2 3.7 %collective-permute-start.12 = (bf16[4,192,512]{2,1,0:T(8,128)(2,1)}, bf16[4,192,512]{2,1,0:T(8,128)(2,1)S(1)}, u32[]{:S(2)}, u32[]{:S(2)}) collective-permute-start(bf16[4,192,512]{2,1,0:T(8,128)(2,1)} %get-tuple-element.52), channel_id=1, source_target_pairs={{0,4},{1,5},{2,6},{3,7},{4,0},{5,1},{6,2},{7,3},{8,12},{9,13},{10,... | collective-permute-start | bytes 2359304 | tf_op jit(solution)/shard_map/ppermute | solution.py:494
  64.8 2.7 %collective-permute-start.10 = (bf16[2,192,512]{2,1,0:T(8,128)(2,1)}, bf16[2,192,512]{2,1,0:T(8,128)(2,1)S(1)}, u32[]{:S(2)}, u32[]{:S(2)}) collective-permute-start(bf16[2,192,512]{2,1,0:T(8,128)(2,1)} %get-tuple-element.50), channel_id=1, source_target_pairs={{0,3},{1,2},{2,1},{3,0},{4,7},{5,6},{6,5},{7,4},{8,11},{9,10},{10,... | collective-permute-start | bytes 1179656 | tf_op jit(solution)/shard_map/ppermute | solution.py:494
  67.6 0.8 collective-permute-start.11
  68.9 1.0 copy-done
  69.9 5.4 %shard_map.151 = bf16[6,192,512]{2,1,0:T(8,128)(2,1)S(1)} custom-call(s32[1]{0:T(128)} %bitcast.head_ref, bf16[192,1024]{1,0:T(8,128)(2,1)S(1)} %copy-done, bf16[1024,8192]{1,0:T(8,128)(2,1)} %w_ref.1), custom_call_target="tpu_custom_call" | custom-call | tf_op jit(solution)/shard_map/pallas_call | solution.py:359
  75.4 9.9 %collective-permute-done.10 = bf16[2,192,512]{2,1,0:T(8,128)(2,1)S(1)} collective-permute-done((bf16[2,192,512]{2,1,0:T(8,128)(2,1)}, bf16[2,192,512]{2,1,0:T(8,128)(2,1)S(1)}, u32[]{:S(2)}, u32[]{:S(2)}) %collective-permute-start.10) | collective-permute-done | bytes 393248 | tf_op jit(solution)/shard_map/ppermute | solution.py:494
  85.3 0.6 collective-permute-done.9
  85.9 1.1 fusion.11
  87.0 1.5 %collective-permute-start.20 = (bf16[96,512]{1,0:T(8,128)(2,1)}, bf16[96,512]{1,0:T(8,128)(2,1)}, u32[]{:S(2)}, u32[]{:S(2)}) collective-permute-start(bf16[96,512]{1,0:T(8,128)(2,1)} %get-tuple-element.73), channel_id=1, source_target_pairs={{0,1},{1,0},{2,3},{3,2},{4,5},{5,4},{6,7},{7,6},{8,9},{9,8},{10,11... | collective-permute-start | bytes 294920 | tf_op jit(solution)/shard_map/ppermute | solution.py:494
  88.5 2.1 %collective-permute-start.21 = (bf16[96,512]{1,0:T(8,128)(2,1)}, bf16[96,512]{1,0:T(8,128)(2,1)}, u32[]{:S(2)}, u32[]{:S(2)}) collective-permute-start(bf16[96,512]{1,0:T(8,128)(2,1)} %get-tuple-element.72), channel_id=1, source_target_pairs={{0,3},{1,2},{2,1},{3,0},{4,7},{5,6},{6,5},{7,4},{8,11},{9,10},{10,... | collective-permute-start | bytes 294920 | tf_op jit(solution)/shard_map/ppermute | solution.py:494
  91.2 0.6 collective-permute-start.15
  91.8 3.0 %collective-permute-start.16 = (bf16[96,512]{1,0:T(8,128)(2,1)}, bf16[96,512]{1,0:T(8,128)(2,1)}, u32[]{:S(2)}, u32[]{:S(2)}) collective-permute-start(bf16[96,512]{1,0:T(8,128)(2,1)} %get-tuple-element.74), channel_id=1, source_target_pairs={{0,2},{1,3},{2,0},{3,1},{4,6},{5,7},{6,4},{7,5},{8,10},{9,11},{10,... | collective-permute-start | bytes 294920 | tf_op jit(solution)/shard_map/ppermute | solution.py:494
  94.8 1.4 %add_convert_fusion.1 = bf16[2,192,512]{2,1,0:T(8,128)(2,1)S(1)} fusion(bf16[2,192,512]{2,1,0:T(8,128)(2,1)} %copy-done.7, bf16[2,192,512]{2,1,0:T(8,128)(2,1)} %copy-done.6, bf16[2,192,512]{2,1,0:T(8,128)(2,1)} %copy-done.8, bf16[6,192,512]{2,1,0:T(8,128)(2,1)S(1)} %shard_map.151), kind=kLoop, calls=%fused_computation.3 | loop fusion | flops 1572864 | bytes 1966080 | tf_op jit(solution)/shard_map/convert_element_type | solution.py:505
  96.3 0.7 collective-permute-start.22
  97.0 2.7 %collective-permute-done.15 = bf16[96,512]{1,0:T(8,128)(2,1)} collective-permute-done((bf16[96,512]{1,0:T(8,128)(2,1)}, bf16[96,512]{1,0:T(8,128)(2,1)}, u32[]{:S(2)}, u32[]{:S(2)}) %collective-permute-start.15) | collective-permute-done | bytes 98336 | tf_op jit(solution)/shard_map/ppermute | solution.py:494
  100.1 1.1 fusion.2
  101.2 1.2 collective-permute-start.17
  103.0 2.4 %collective-permute-start.19 = (bf16[96,512]{1,0:T(8,128)(2,1)S(1)}, bf16[96,512]{1,0:T(8,128)(2,1)S(1)}, u32[]{:S(2)}, u32[]{:S(2)}) collective-permute-start(bf16[96,512]{1,0:T(8,128)(2,1)S(1)} %fusion.2), channel_id=1, source_target_pairs={{0,3},{1,2},{2,1},{3,0},{4,7},{5,6},{6,5},{7,4},{8,11},{9,10},{10,... | collective-permute-start | bytes 294920 | tf_op jit(solution)/shard_map/ppermute | solution.py:494
  105.4 1.0 add_convert_fusion.2
  106.9 1.1 collective-permute-done.17
  108.0 1.1 collective-permute-start.24
  109.2 1.4 %collective-permute-start.25 = (bf16[96,512]{1,0:T(8,128)(2,1)S(1)}, bf16[96,512]{1,0:T(8,128)(2,1)S(1)}, u32[]{:S(2)}, u32[]{:S(2)}) collective-permute-start(bf16[96,512]{1,0:T(8,128)(2,1)S(1)} %add_convert_fusion.2), channel_id=1, source_target_pairs={{0,2},{1,3},{2,0},{3,1},{4,6},{5,7},{6,4},{7,5},{8,10},{9,11},{10,... | collective-permute-start | bytes 294920 | tf_op jit(solution)/shard_map/ppermute | solution.py:494
  111.0 2.8 %collective-permute-start.26 = (bf16[4,96,512]{2,1,0:T(8,128)(2,1)S(1)}, bf16[4,96,512]{2,1,0:T(8,128)(2,1)}, u32[]{:S(2)}, u32[]{:S(2)}) collective-permute-start(bf16[4,96,512]{2,1,0:T(8,128)(2,1)S(1)} %pad_maximum_fusion.2.refs_1_), channel_id=1, source_target_pairs={{0,4},{1,5},{2,6},{3,7},{4,0},{5,1},{6,2},{7,3},{8,12},{9,13},{10,... | collective-permute-start | bytes 1179656 | tf_op jit(solution)/shard_map/ppermute | solution.py:494
  113.9 1.3 collective-permute-done.25
  115.3 2.6 %collective-permute-start.27 = (bf16[4,96,512]{2,1,0:T(8,128)(2,1)S(1)}, bf16[4,96,512]{2,1,0:T(8,128)(2,1)}, u32[]{:S(2)}, u32[]{:S(2)}) collective-permute-start(bf16[4,96,512]{2,1,0:T(8,128)(2,1)S(1)} %pad_maximum_fusion.3.refs_2_), channel_id=1, source_target_pairs={{0,4},{1,5},{2,6},{3,7},{4,0},{5,1},{6,2},{7,3},{8,12},{9,13},{10,... | collective-permute-start | bytes 1179656 | tf_op jit(solution)/shard_map/ppermute | solution.py:494
  118.0 3.1 %collective-permute-start.28 = (bf16[2,192,512]{2,1,0:T(8,128)(2,1)S(1)}, bf16[2,192,512]{2,1,0:T(8,128)(2,1)}, u32[]{:S(2)}, u32[]{:S(2)}) collective-permute-start(bf16[2,192,512]{2,1,0:T(8,128)(2,1)S(1)} %add_convert_fusion.refs_0_), channel_id=1, source_target_pairs={{0,2},{1,3},{2,0},{3,1},{4,6},{5,7},{6,4},{7,5},{8,10},{9,11},{10,... | collective-permute-start | bytes 1179656 | tf_op jit(solution)/shard_map/ppermute | solution.py:494
  121.1 1.2 collective-permute-start.29
  122.3 4.7 %shard_map.152 = (bf16[4,1024,128]{2,1,0:T(8,128)(2,1)}, bf16[4,1024,128]{2,1,0:T(8,128)(2,1)}) custom-call(s32[1]{0:T(128)} %bitcast.39.first_ref, s32[16,64]{1,0:T(8,128)S(1)} %bitcast.64, s32[16,64]{1,0:T(8,128)S(1)} %bitcast.63, bf16[16,4,64,256]{3,2,1,0:T(8,128)(2,1)S(1)} %all-to-all-done.source), custom_call_target="tpu_custom_call" | custom-call | tf_op jit(solution)/shard_map/pallas_call | solution.py:466
  127.0 1.8 %shard_map.153.earlier = bf16[192,8192]{1,0:T(8,128)(2,1)} custom-call(s32[1]{0:T(128)} %bitcast.head_ref, bf16[2,192,512]{2,1,0:T(8,128)(2,1)S(1)} %add_convert_fusion.refs_0_, bf16[4,96,512]{2,1,0:T(8,128)(2,1)S(1)} %pad_maximum_fusion.2.refs_1_, bf16[4,96,512]{2,1,0:T(8,128)(2,1)S(1)} %pad_maximum_fusion.3.refs_2_), custom_call_target="tpu_custom_call" | custom-call | tf_op jit(solution)/shard_map/pallas_call | solution.py:396
  128.7 1.9 %collective-permute-done.28.refs_2_ = bf16[2,192,512]{2,1,0:T(8,128)(2,1)} collective-permute-done((bf16[2,192,512]{2,1,0:T(8,128)(2,1)S(1)}, bf16[2,192,512]{2,1,0:T(8,128)(2,1)}, u32[]{:S(2)}, u32[]{:S(2)}) %collective-permute-start.28) | collective-permute-done | bytes 393248 | tf_op jit(solution)/shard_map/ppermute | solution.py:494
  130.6 1.8 %collective-permute-done.29.refs_3_ = bf16[2,192,512]{2,1,0:T(8,128)(2,1)} collective-permute-done((bf16[2,192,512]{2,1,0:T(8,128)(2,1)S(1)}, bf16[2,192,512]{2,1,0:T(8,128)(2,1)}, u32[]{:S(2)}, u32[]{:S(2)}) %collective-permute-start.29) | collective-permute-done | bytes 393248 | tf_op jit(solution)/shard_map/ppermute | solution.py:494
  132.4 2.3 %collective-permute-done.30.refs_4_ = bf16[2,192,512]{2,1,0:T(8,128)(2,1)} collective-permute-done((bf16[2,192,512]{2,1,0:T(8,128)(2,1)S(1)}, bf16[2,192,512]{2,1,0:T(8,128)(2,1)}, u32[]{:S(2)}, u32[]{:S(2)}) %collective-permute-start.30) | collective-permute-done | bytes 393248 | tf_op jit(solution)/shard_map/ppermute | solution.py:494
  134.7 2.8 %shard_map.154 = bf16[192,8192]{1,0:T(8,128)(2,1)} custom-call(s32[1]{0:T(128)} %bitcast.head_ref, bf16[192,8192]{1,0:T(8,128)(2,1)} %shard_map.153.earlier, bf16[4,96,512]{2,1,0:T(8,128)(2,1)} %collective-permute-done.26.refs_0_, bf16[4,96,512]{2,1,0:T(8,128)(2,1)} %collective-permute-done.27.refs_1_, ...), custom_call_target="tpu_custom_call", output_to_operand_aliasing={{}: (1, {})} | custom-call | tf_op jit(solution)/shard_map/pallas_call | solution.py:425
  (55 shorter events, 4.9 us)
Async XLA Ops:
  2.4 8.4 %collective-permute-start = (bf16[1024,128]{1,0:T(8,128)(2,1)}, bf16[1024,128]{1,0:T(8,128)(2,1)S(1)}, u32[]{:S(2)}, u32[]{:S(2)}) collective-permute-start(bf16[1024,128]{1,0:T(8,128)(2,1)} %shard_map.149), channel_id=1, source_target_pairs={{0,64},{8,72},{16,80},{24,88},{32,96},{40,104},{48,112},{56,120},{... | collective-permute-start | bytes 786440 | tf_op jit(solution)/shard_map/ppermute | solution.py:486
  4.3 12.0 %collective-permute-start.1 = (bf16[1024,128]{1,0:T(8,128)(2,1)}, bf16[1024,128]{1,0:T(8,128)(2,1)S(1)}, u32[]{:S(2)}, u32[]{:S(2)}) collective-permute-start(bf16[1024,128]{1,0:T(8,128)(2,1)} %shard_map.149), channel_id=1, source_target_pairs={{0,16},{8,24},{16,32},{24,40},{32,48},{40,56},{48,0},{56,8},{64,80... | collective-permute-start | bytes 786440 | tf_op jit(solution)/shard_map/ppermute | solution.py:486
  5.9 19.8 %collective-permute-start.2 = (bf16[1024,128]{1,0:T(8,128)(2,1)}, bf16[1024,128]{1,0:T(8,128)(2,1)S(1)}, u32[]{:S(2)}, u32[]{:S(2)}) collective-permute-start(bf16[1024,128]{1,0:T(8,128)(2,1)} %shard_map.149), channel_id=1, source_target_pairs={{0,48},{8,56},{16,0},{24,8},{32,16},{40,24},{48,32},{56,40},{64,11... | collective-permute-start | bytes 786440 | tf_op jit(solution)/shard_map/ppermute | solution.py:486
  6.3 19.4 %collective-permute-start.3 = (bf16[1024,128]{1,0:T(8,128)(2,1)}, bf16[1024,128]{1,0:T(8,128)(2,1)S(1)}, u32[]{:S(2)}, u32[]{:S(2)}) collective-permute-start(bf16[1024,128]{1,0:T(8,128)(2,1)} %shard_map.149), channel_id=1, source_target_pairs={{0,32},{8,40},{16,48},{24,56},{32,0},{40,8},{48,16},{56,24},{64,96... | collective-permute-start | bytes 786440 | tf_op jit(solution)/shard_map/ppermute | solution.py:486
  10.8 14.9 %collective-permute-start.4 = (bf16[1024,128]{1,0:T(8,128)(2,1)S(1)}, bf16[1024,128]{1,0:T(8,128)(2,1)S(1)}, u32[]{:S(2)}, u32[]{:S(2)}) collective-permute-start(bf16[1024,128]{1,0:T(8,128)(2,1)S(1)} %collective-permute-done), channel_id=1, source_target_pairs={{0,16},{8,24},{16,32},{24,40},{32,48},{40,56},{48,0},{56,8},{64,80... | collective-permute-start | bytes 786440 | tf_op jit(solution)/shard_map/ppermute | solution.py:486
  12.4 13.4 %collective-permute-start.5 = (bf16[1024,128]{1,0:T(8,128)(2,1)S(1)}, bf16[1024,128]{1,0:T(8,128)(2,1)S(1)}, u32[]{:S(2)}, u32[]{:S(2)}) collective-permute-start(bf16[1024,128]{1,0:T(8,128)(2,1)S(1)} %collective-permute-done), channel_id=1, source_target_pairs={{0,48},{8,56},{16,0},{24,8},{32,16},{40,24},{48,32},{56,40},{64,11... | collective-permute-start | bytes 786440 | tf_op jit(solution)/shard_map/ppermute | solution.py:486
  16.4 14.8 %collective-permute-start.6 = (bf16[1024,128]{1,0:T(8,128)(2,1)S(1)}, bf16[1024,128]{1,0:T(8,128)(2,1)S(1)}, u32[]{:S(2)}, u32[]{:S(2)}) collective-permute-start(bf16[1024,128]{1,0:T(8,128)(2,1)S(1)} %collective-permute-done), channel_id=1, source_target_pairs={{0,32},{8,40},{16,48},{24,56},{32,0},{40,8},{48,16},{56,24},{64,96... | collective-permute-start | bytes 786440 | tf_op jit(solution)/shard_map/ppermute | solution.py:486
  18.3 13.2 %copy-start.4 = (bf16[1024,128]{1,0:T(8,128)(2,1)S(1)}, bf16[1024,128]{1,0:T(8,128)(2,1)}, u32[]{:S(2)}) copy-start(bf16[1024,128]{1,0:T(8,128)(2,1)} %shard_map.149) | copy-start | bytes 786436
  31.3 1.7 %copy-start.3 = (bf16[4,1024,128]{2,1,0:T(8,128)(2,1)}, bf16[4,1024,128]{2,1,0:T(8,128)(2,1)S(1)}, u32[]{:S(2)}) copy-start(bf16[4,1024,128]{2,1,0:T(8,128)(2,1)S(1)} %pad_maximum_fusion.1.refs_2_) | copy-start | bytes 3145732
  31.3 6.1 %collective-permute-start.8 = (bf16[4,1024,128]{2,1,0:T(8,128)(2,1)S(1)}, bf16[4,1024,128]{2,1,0:T(8,128)(2,1)}, u32[]{:S(2)}, u32[]{:S(2)}) collective-permute-start(bf16[4,1024,128]{2,1,0:T(8,128)(2,1)S(1)} %pad_maximum_fusion.1.refs_2_), channel_id=1, source_target_pairs={{0,8},{8,0},{16,24},{24,16},{32,40},{40,32},{48,56},{56,48},{64,72... | collective-permute-start | bytes 3145736 | tf_op jit(solution)/shard_map/ppermute | solution.py:490
  32.7 4.8 %collective-permute-start.7 = (bf16[4,1024,128]{2,1,0:T(8,128)(2,1)}, bf16[4,1024,128]{2,1,0:T(8,128)(2,1)}, u32[]{:S(2)}, u32[]{:S(2)}) collective-permute-start(bf16[4,1024,128]{2,1,0:T(8,128)(2,1)} %pad_maximum_fusion.refs_0_), channel_id=1, source_target_pairs={{0,8},{8,0},{16,24},{24,16},{32,40},{40,32},{48,56},{56,48},{64,72... | collective-permute-start | bytes 3145736 | tf_op jit(solution)/shard_map/ppermute | solution.py:490
  33.0 61.7 %all-to-all-start = ((bf16[16,4,64,256]{3,2,1,0:T(8,128)(2,1)}), bf16[16,4,64,256]{3,2,1,0:T(8,128)(2,1)S(1)}, u32[]{:S(2)}, u32[]{:S(2)}) async-start(bf16[16,4,64,256]{3,2,1,0:T(8,128)(2,1)} %bitcast.66), calls=%async_computation | async-start | bytes 4194304 | tf_op jit(solution)/shard_map/all_to_all | solution.py:550
  61.2 24.8 %collective-permute-start.12 = (bf16[4,192,512]{2,1,0:T(8,128)(2,1)}, bf16[4,192,512]{2,1,0:T(8,128)(2,1)S(1)}, u32[]{:S(2)}, u32[]{:S(2)}) collective-permute-start(bf16[4,192,512]{2,1,0:T(8,128)(2,1)} %get-tuple-element.52), channel_id=1, source_target_pairs={{0,4},{1,5},{2,6},{3,7},{4,0},{5,1},{6,2},{7,3},{8,12},{9,13},{10,... | collective-permute-start | bytes 2359304 | tf_op jit(solution)/shard_map/ppermute | solution.py:494
  64.8 20.5 %collective-permute-start.10 = (bf16[2,192,512]{2,1,0:T(8,128)(2,1)}, bf16[2,192,512]{2,1,0:T(8,128)(2,1)S(1)}, u32[]{:S(2)}, u32[]{:S(2)}) collective-permute-start(bf16[2,192,512]{2,1,0:T(8,128)(2,1)} %get-tuple-element.50), channel_id=1, source_target_pairs={{0,3},{1,2},{2,1},{3,0},{4,7},{5,6},{6,5},{7,4},{8,11},{9,10},{10,... | collective-permute-start | bytes 1179656 | tf_op jit(solution)/shard_map/ppermute | solution.py:494
  67.6 17.7 %collective-permute-start.11 = (bf16[2,192,512]{2,1,0:T(8,128)(2,1)}, bf16[2,192,512]{2,1,0:T(8,128)(2,1)S(1)}, u32[]{:S(2)}, u32[]{:S(2)}) collective-permute-start(bf16[2,192,512]{2,1,0:T(8,128)(2,1)} %get-tuple-element.51), channel_id=1, source_target_pairs={{0,2},{1,3},{2,0},{3,1},{4,6},{5,7},{6,4},{7,5},{8,10},{9,11},{10,... | collective-permute-start | bytes 1179656 | tf_op jit(solution)/shard_map/ppermute | solution.py:494
  68.4 17.5 %collective-permute-start.9 = (bf16[2,192,512]{2,1,0:T(8,128)(2,1)}, bf16[2,192,512]{2,1,0:T(8,128)(2,1)S(1)}, u32[]{:S(2)}, u32[]{:S(2)}) collective-permute-start(bf16[2,192,512]{2,1,0:T(8,128)(2,1)} %get-tuple-element.49), channel_id=1, source_target_pairs={{0,1},{1,0},{2,3},{3,2},{4,5},{5,4},{6,7},{7,6},{8,9},{9,8},{10,11... | collective-permute-start | bytes 1179656 | tf_op jit(solution)/shard_map/ppermute | solution.py:494
  68.9 1.0 copy-start
  85.3 6.5 %copy-start.6 = (bf16[2,192,512]{2,1,0:T(8,128)(2,1)}, bf16[2,192,512]{2,1,0:T(8,128)(2,1)S(1)}, u32[]{:S(2)}) copy-start(bf16[2,192,512]{2,1,0:T(8,128)(2,1)S(1)} %collective-permute-done.10) | copy-start | bytes 1179652
  85.3 6.5 %copy-start.7 = (bf16[2,192,512]{2,1,0:T(8,128)(2,1)}, bf16[2,192,512]{2,1,0:T(8,128)(2,1)S(1)}, u32[]{:S(2)}) copy-start(bf16[2,192,512]{2,1,0:T(8,128)(2,1)S(1)} %collective-permute-done.11) | copy-start | bytes 1179652
  85.9 5.9 %copy-start.8 = (bf16[2,192,512]{2,1,0:T(8,128)(2,1)}, bf16[2,192,512]{2,1,0:T(8,128)(2,1)S(1)}, u32[]{:S(2)}) copy-start(bf16[2,192,512]{2,1,0:T(8,128)(2,1)S(1)} %collective-permute-done.9) | copy-start | bytes 1179652
  85.9 5.9 %copy-start.5 = (bf16[4,192,512]{2,1,0:T(8,128)(2,1)}, bf16[4,192,512]{2,1,0:T(8,128)(2,1)S(1)}, u32[]{:S(2)}) copy-start(bf16[4,192,512]{2,1,0:T(8,128)(2,1)S(1)} %collective-permute-done.12) | copy-start | bytes 2359300
  87.0 15.4 %collective-permute-start.20 = (bf16[96,512]{1,0:T(8,128)(2,1)}, bf16[96,512]{1,0:T(8,128)(2,1)}, u32[]{:S(2)}, u32[]{:S(2)}) collective-permute-start(bf16[96,512]{1,0:T(8,128)(2,1)} %get-tuple-element.73), channel_id=1, source_target_pairs={{0,1},{1,0},{2,3},{3,2},{4,5},{5,4},{6,7},{7,6},{8,9},{9,8},{10,11... | collective-permute-start | bytes 294920 | tf_op jit(solution)/shard_map/ppermute | solution.py:494
  88.5 14.5 %collective-permute-start.21 = (bf16[96,512]{1,0:T(8,128)(2,1)}, bf16[96,512]{1,0:T(8,128)(2,1)}, u32[]{:S(2)}, u32[]{:S(2)}) collective-permute-start(bf16[96,512]{1,0:T(8,128)(2,1)} %get-tuple-element.72), channel_id=1, source_target_pairs={{0,3},{1,2},{2,1},{3,0},{4,7},{5,6},{6,5},{7,4},{8,11},{9,10},{10,... | collective-permute-start | bytes 294920 | tf_op jit(solution)/shard_map/ppermute | solution.py:494
  90.6 5.7 %collective-permute-start.14 = (bf16[96,512]{1,0:T(8,128)(2,1)}, bf16[96,512]{1,0:T(8,128)(2,1)}, u32[]{:S(2)}, u32[]{:S(2)}) collective-permute-start(bf16[96,512]{1,0:T(8,128)(2,1)} %get-tuple-element.76), channel_id=1, source_target_pairs={{0,1},{1,0},{2,3},{3,2},{4,5},{5,4},{6,7},{7,6},{8,9},{9,8},{10,11... | collective-permute-start | bytes 294920 | tf_op jit(solution)/shard_map/ppermute | solution.py:494
  91.2 8.5 %collective-permute-start.15 = (bf16[96,512]{1,0:T(8,128)(2,1)}, bf16[96,512]{1,0:T(8,128)(2,1)}, u32[]{:S(2)}, u32[]{:S(2)}) collective-permute-start(bf16[96,512]{1,0:T(8,128)(2,1)} %get-tuple-element.75), channel_id=1, source_target_pairs={{0,3},{1,2},{2,1},{3,0},{4,7},{5,6},{6,5},{7,4},{8,11},{9,10},{10,... | collective-permute-start | bytes 294920 | tf_op jit(solution)/shard_map/ppermute | solution.py:494
  91.8 8.3 %collective-permute-start.16 = (bf16[96,512]{1,0:T(8,128)(2,1)}, bf16[96,512]{1,0:T(8,128)(2,1)}, u32[]{:S(2)}, u32[]{:S(2)}) collective-permute-start(bf16[96,512]{1,0:T(8,128)(2,1)} %get-tuple-element.74), channel_id=1, source_target_pairs={{0,2},{1,3},{2,0},{3,1},{4,6},{5,7},{6,4},{7,5},{8,10},{9,11},{10,... | collective-permute-start | bytes 294920 | tf_op jit(solution)/shard_map/ppermute | solution.py:494
  96.2 26.0 %copy-start.1 = (s32[64,16]{0,1:T(8,128)S(1)}, s32[64,16]{0,1:T(8,128)}, u32[]{:S(2)}) copy-start(s32[64,16]{0,1:T(8,128)} %param.20) | copy-start | bytes 12292
  96.2 26.0 %copy-start.2 = (s32[64,16]{0,1:T(8,128)S(1)}, s32[64,16]{0,1:T(8,128)}, u32[]{:S(2)}) copy-start(s32[64,16]{0,1:T(8,128)} %param.21) | copy-start | bytes 12292
  96.3 9.1 %collective-permute-start.22 = (bf16[96,512]{1,0:T(8,128)(2,1)S(1)}, bf16[96,512]{1,0:T(8,128)(2,1)S(1)}, u32[]{:S(2)}, u32[]{:S(2)}) collective-permute-start(bf16[96,512]{1,0:T(8,128)(2,1)S(1)} %get-tuple-element.71), channel_id=1, source_target_pairs={{0,2},{1,3},{2,0},{3,1},{4,6},{5,7},{6,4},{7,5},{8,10},{9,11},{10,... | collective-permute-start | bytes 294920 | tf_op jit(solution)/shard_map/ppermute | solution.py:494
  99.7 14.1 %collective-permute-start.13 = (bf16[2,192,512]{2,1,0:T(8,128)(2,1)S(1)}, bf16[2,192,512]{2,1,0:T(8,128)(2,1)S(1)}, u32[]{:S(2)}, u32[]{:S(2)}) collective-permute-start(bf16[2,192,512]{2,1,0:T(8,128)(2,1)S(1)} %add_convert_fusion.1), channel_id=1, source_target_pairs={{0,4},{1,5},{2,6},{3,7},{4,0},{5,1},{6,2},{7,3},{8,12},{9,13},{10,... | collective-permute-start | bytes 1179656 | tf_op jit(solution)/shard_map/ppermute | solution.py:494
  101.2 6.8 %collective-permute-start.17 = (bf16[96,512]{1,0:T(8,128)(2,1)S(1)}, bf16[96,512]{1,0:T(8,128)(2,1)S(1)}, u32[]{:S(2)}, u32[]{:S(2)}) collective-permute-start(bf16[96,512]{1,0:T(8,128)(2,1)S(1)} %fusion.2), channel_id=1, source_target_pairs={{0,2},{1,3},{2,0},{3,1},{4,6},{5,7},{6,4},{7,5},{8,10},{9,11},{10,... | collective-permute-start | bytes 294920 | tf_op jit(solution)/shard_map/ppermute | solution.py:494
  102.4 6.7 %collective-permute-start.18 = (bf16[96,512]{1,0:T(8,128)(2,1)S(1)}, bf16[96,512]{1,0:T(8,128)(2,1)S(1)}, u32[]{:S(2)}, u32[]{:S(2)}) collective-permute-start(bf16[96,512]{1,0:T(8,128)(2,1)S(1)} %fusion.2), channel_id=1, source_target_pairs={{0,1},{1,0},{2,3},{3,2},{4,5},{5,4},{6,7},{7,6},{8,9},{9,8},{10,11... | collective-permute-start | bytes 294920 | tf_op jit(solution)/shard_map/ppermute | solution.py:494
  103.0 7.9 %collective-permute-start.19 = (bf16[96,512]{1,0:T(8,128)(2,1)S(1)}, bf16[96,512]{1,0:T(8,128)(2,1)S(1)}, u32[]{:S(2)}, u32[]{:S(2)}) collective-permute-start(bf16[96,512]{1,0:T(8,128)(2,1)S(1)} %fusion.2), channel_id=1, source_target_pairs={{0,3},{1,2},{2,1},{3,0},{4,7},{5,6},{6,5},{7,4},{8,11},{9,10},{10,... | collective-permute-start | bytes 294920 | tf_op jit(solution)/shard_map/ppermute | solution.py:494
  106.4 7.5 %collective-permute-start.23 = (bf16[96,512]{1,0:T(8,128)(2,1)S(1)}, bf16[96,512]{1,0:T(8,128)(2,1)S(1)}, u32[]{:S(2)}, u32[]{:S(2)}) collective-permute-start(bf16[96,512]{1,0:T(8,128)(2,1)S(1)} %add_convert_fusion.2), channel_id=1, source_target_pairs={{0,1},{1,0},{2,3},{3,2},{4,5},{5,4},{6,7},{7,6},{8,9},{9,8},{10,11... | collective-permute-start | bytes 294920 | tf_op jit(solution)/shard_map/ppermute | solution.py:494
  108.0 5.9 %collective-permute-start.24 = (bf16[96,512]{1,0:T(8,128)(2,1)S(1)}, bf16[96,512]{1,0:T(8,128)(2,1)S(1)}, u32[]{:S(2)}, u32[]{:S(2)}) collective-permute-start(bf16[96,512]{1,0:T(8,128)(2,1)S(1)} %add_convert_fusion.2), channel_id=1, source_target_pairs={{0,3},{1,2},{2,1},{3,0},{4,7},{5,6},{6,5},{7,4},{8,11},{9,10},{10,... | collective-permute-start | bytes 294920 | tf_op jit(solution)/shard_map/ppermute | solution.py:494
  109.2 6.1 %collective-permute-start.25 = (bf16[96,512]{1,0:T(8,128)(2,1)S(1)}, bf16[96,512]{1,0:T(8,128)(2,1)S(1)}, u32[]{:S(2)}, u32[]{:S(2)}) collective-permute-start(bf16[96,512]{1,0:T(8,128)(2,1)S(1)} %add_convert_fusion.2), channel_id=1, source_target_pairs={{0,2},{1,3},{2,0},{3,1},{4,6},{5,7},{6,4},{7,5},{8,10},{9,11},{10,... | collective-permute-start | bytes 294920 | tf_op jit(solution)/shard_map/ppermute | solution.py:494
  111.0 17.8 %collective-permute-start.26 = (bf16[4,96,512]{2,1,0:T(8,128)(2,1)S(1)}, bf16[4,96,512]{2,1,0:T(8,128)(2,1)}, u32[]{:S(2)}, u32[]{:S(2)}) collective-permute-start(bf16[4,96,512]{2,1,0:T(8,128)(2,1)S(1)} %pad_maximum_fusion.2.refs_1_), channel_id=1, source_target_pairs={{0,4},{1,5},{2,6},{3,7},{4,0},{5,1},{6,2},{7,3},{8,12},{9,13},{10,... | collective-permute-start | bytes 1179656 | tf_op jit(solution)/shard_map/ppermute | solution.py:494
  115.3 13.4 %collective-permute-start.27 = (bf16[4,96,512]{2,1,0:T(8,128)(2,1)S(1)}, bf16[4,96,512]{2,1,0:T(8,128)(2,1)}, u32[]{:S(2)}, u32[]{:S(2)}) collective-permute-start(bf16[4,96,512]{2,1,0:T(8,128)(2,1)S(1)} %pad_maximum_fusion.3.refs_2_), channel_id=1, source_target_pairs={{0,4},{1,5},{2,6},{3,7},{4,0},{5,1},{6,2},{7,3},{8,12},{9,13},{10,... | collective-permute-start | bytes 1179656 | tf_op jit(solution)/shard_map/ppermute | solution.py:494
  118.0 12.6 %collective-permute-start.28 = (bf16[2,192,512]{2,1,0:T(8,128)(2,1)S(1)}, bf16[2,192,512]{2,1,0:T(8,128)(2,1)}, u32[]{:S(2)}, u32[]{:S(2)}) collective-permute-start(bf16[2,192,512]{2,1,0:T(8,128)(2,1)S(1)} %add_convert_fusion.refs_0_), channel_id=1, source_target_pairs={{0,2},{1,3},{2,0},{3,1},{4,6},{5,7},{6,4},{7,5},{8,10},{9,11},{10,... | collective-permute-start | bytes 1179656 | tf_op jit(solution)/shard_map/ppermute | solution.py:494
  121.1 11.3 %collective-permute-start.29 = (bf16[2,192,512]{2,1,0:T(8,128)(2,1)S(1)}, bf16[2,192,512]{2,1,0:T(8,128)(2,1)}, u32[]{:S(2)}, u32[]{:S(2)}) collective-permute-start(bf16[2,192,512]{2,1,0:T(8,128)(2,1)S(1)} %add_convert_fusion.refs_0_), channel_id=1, source_target_pairs={{0,1},{1,0},{2,3},{3,2},{4,5},{5,4},{6,7},{7,6},{8,9},{9,8},{10,11... | collective-permute-start | bytes 1179656 | tf_op jit(solution)/shard_map/ppermute | solution.py:494
  122.3 12.4 %collective-permute-start.30 = (bf16[2,192,512]{2,1,0:T(8,128)(2,1)S(1)}, bf16[2,192,512]{2,1,0:T(8,128)(2,1)}, u32[]{:S(2)}, u32[]{:S(2)}) collective-permute-start(bf16[2,192,512]{2,1,0:T(8,128)(2,1)S(1)} %add_convert_fusion.refs_0_), channel_id=1, source_target_pairs={{0,3},{1,2},{2,1},{3,0},{4,7},{5,6},{6,5},{7,4},{8,11},{9,10},{10,... | collective-permute-start | bytes 1179656 | tf_op jit(solution)/shard_map/ppermute | solution.py:494
where the time goes:
time: 140 us; the launch traced here: 138 us
  Pallas kernels  47.6 us (34%)
  starting transfers between devices  46.8 us (33%)
  waiting for transfers between devices  31.7 us (23%)
  other arithmetic  9.46 us (7%)
    ppermute x22, starting transfers between devices, move_x(): return lax.ppermute(value, 'head', [(h, h ^ flip) for h in range(KVH)])  33.7 us
    pallas_call x1, Pallas kernels, prompt_part(): pl.pallas_call(functools.partial(prompt_kernel, places, groups, len(stack...  23.7 us
    ppermute x22, waiting for transfers between devices, move_x(): return lax.ppermute(value, 'head', [(h, h ^ flip) for h in range(KVH)])  22 us
    ppermute x7, waiting for transfers between devices, move_chip(): return lax.ppermute(value, 'branch', perm)  9.76 us
    ppermute x7, starting transfers between devices, move_chip(): return lax.ppermute(value, 'branch', perm)  8.27 us
    pallas_call x1, Pallas kernels, span_part(): pl.pallas_call(span_kernel, grid_spec=pltpu.PrefetchScalarGridSpec(num_sc...  7.44 us
    pallas_call x1, Pallas kernels, project(): pl.pallas_call(functools.partial(project_kernel, places), grid_spec=pltpu...  5.44 us
    convert_element_type x5, other arithmetic, add(): return total.astype(jnp.bfloat16)  4.71 us
  transfers between devices with their start and end apart: 32, of which 13 were waited for; matrix products, arithmetic and copies ran while one was open for 7% of the time, Pallas kernels for 31%

commit v1 on v0

--- a/solution.py
+++ b/solution.py
@@ -523,7 +523,7 @@
     near_at = [(0, 0), (1, 0), (0, 1), (0, 3)]
     far_at = [(0, 2), (1, 1), (1, 3), (1, 2)]
     near = [own] + [move_chip(own, dz, dy) for dz, dy in near_at[1:]]
-    far = [move_chip(own, 0, 2)] + [move_chip(near[1], 0, dy) for _, dy in far_at[1:]]
+    far = [move_chip(own, 0, 2)] + [move_chip(near[1], 0, dy) for dy in (1, 3)]
 
     lengths = span_lengths.T
     offsets = join_offsets.T
@@ -531,6 +531,7 @@
     shift = lax.dynamic_slice_in_dim(offsets, me, 1, 0) - prompt_len
     steps = jnp.arange(STEPS, dtype=jnp.int32)[:, None]
     cosine, sine = tables(jnp.concatenate([prompt_len + live + steps, shift]))
+    far.append(move_chip(after(far[0], cosine), 1, 0))
     query, top, accum, sent = span_part(
         lengths,
         one,

time: 140 us -> 134 us (0.957); the launches traced: 138 us -> 133 us
  waiting for transfers between devices: 31.7 us -> 25.2 us
    ppermute x7, waiting for transfers between devices: 9.76 us -> 1.41 us  [move_chip(): return lax.ppermute(value, 'branch', perm)]
    ppermute x7, starting transfers between devices: 8.27 us -> 10.2 us  [move_chip(): return lax.ppermute(value, 'branch', perm)]
    ppermute x22, waiting for transfers between devices: 22 us -> 23.8 us  [move_x(): return lax.ppermute(value, 'head', [(h, h ^ flip) for h in range(KVH)])]
    ppermute x22, starting transfers between devices: 33.7 us -> 32.1 us  [move_x(): return lax.ppermute(value, 'head', [(h, h ^ flip) for h in range(KVH)])]
  transfers between devices with their start and end apart: 32 -> 32, of which waited for: 13 -> 11; matrix products, arithmetic and copies ran while one was open for 7% -> 7% of each run, Pallas kernels for 31% -> 33%
where the time goes in v1:
time: 134 us; the launch traced here: 133 us
  Pallas kernels  48.8 us (36%)
  starting transfers between devices  47.9 us (36%)
  waiting for transfers between devices  25.2 us (19%)
  other arithmetic  9.48 us (7%)
    ppermute x22, starting transfers between devices, move_x(): return lax.ppermute(value, 'head', [(h, h ^ flip) for h in range(KVH)])  32.1 us
    pallas_call x1, Pallas kernels, prompt_part(): pl.pallas_call(functools.partial(prompt_kernel, places, groups, len(stack...  24.9 us
    ppermute x22, waiting for transfers between devices, move_x(): return lax.ppermute(value, 'head', [(h, h ^ flip) for h in range(KVH)])  23.8 us
    ppermute x7, starting transfers between devices, move_chip(): return lax.ppermute(value, 'branch', perm)  10.2 us
    pallas_call x1, Pallas kernels, span_part(): pl.pallas_call(span_kernel, grid_spec=pltpu.PrefetchScalarGridSpec(num_sc...  7.44 us
    pallas_call x1, Pallas kernels, project(): pl.pallas_call(functools.partial(project_kernel, places), grid_spec=pltpu...  5.44 us
    all_to_all x1, starting transfers between devices, shards(): gathered = lax.all_to_all(sent, 'branch', 0, 0, tiled=True)  5.17 us
    convert_element_type x5, other arithmetic, add(): return total.astype(jnp.bfloat16)  4.73 us
  transfers between devices with their start and end apart: 32, of which 11 were waited for; matrix products, arithmetic and copies ran while one was open for 7% of the time, Pallas kernels for 33%

profile of v1, /device:TPU:8, one launch (start us, length us, event | category | flops | bytes accessed | tf_op | source)
XLA Modules:
  0.0 133.4 jit_solution(1032439341904631735)
XLA Ops:
  0.6 1.8 %shard_map.149 = bf16[1024,128]{1,0:T(8,128)(2,1)} custom-call(bf16[512,128]{1,0:T(8,128)(2,1)} %keys_ref.1, bf16[512,128]{1,0:T(8,128)(2,1)} %vals_ref.1), custom_call_target="tpu_custom_call" | custom-call | tf_op jit(solution)/shard_map/pallas_call | solution.py:156
  2.4 2.3 %collective-permute-start.3 = (bf16[1024,128]{1,0:T(8,128)(2,1)}, bf16[1024,128]{1,0:T(8,128)(2,1)S(1)}, u32[]{:S(2)}, u32[]{:S(2)}) collective-permute-start(bf16[1024,128]{1,0:T(8,128)(2,1)} %shard_map.149), channel_id=1, source_target_pairs={{0,32},{8,40},{16,48},{24,56},{32,0},{40,8},{48,16},{56,24},{64,96... | collective-permute-start | bytes 786440 | tf_op jit(solution)/shard_map/ppermute | solution.py:486
  4.7 1.9 %collective-permute-start = (bf16[1024,128]{1,0:T(8,128)(2,1)}, bf16[1024,128]{1,0:T(8,128)(2,1)S(1)}, u32[]{:S(2)}, u32[]{:S(2)}) collective-permute-start(bf16[1024,128]{1,0:T(8,128)(2,1)} %shard_map.149), channel_id=1, source_target_pairs={{0,64},{8,72},{16,80},{24,88},{32,96},{40,104},{48,112},{56,120},{... | collective-permute-start | bytes 786440 | tf_op jit(solution)/shard_map/ppermute | solution.py:486
  6.6 2.0 %collective-permute-start.2 = (bf16[1024,128]{1,0:T(8,128)(2,1)}, bf16[1024,128]{1,0:T(8,128)(2,1)S(1)}, u32[]{:S(2)}, u32[]{:S(2)}) collective-permute-start(bf16[1024,128]{1,0:T(8,128)(2,1)} %shard_map.149), channel_id=1, source_target_pairs={{0,48},{8,56},{16,0},{24,8},{32,16},{40,24},{48,32},{56,40},{64,11... | collective-permute-start | bytes 786440 | tf_op jit(solution)/shard_map/ppermute | solution.py:486
  8.6 0.7 add_bitcast_fusion.1
  9.3 0.7 add_bitcast_fusion
  10.0 1.9 %fusion.3 = (f32[4,64,128]{2,1,0:T(8,128)}, f32[4,64,128]{2,1,0:T(8,128)}) fusion(f32[128]{0:T(128)} %constant.24.clone, f32[128]{0:T(128)} %constant.23.clone, f32[4,64]{1,0:T(4,128)S(1)} %add_convert_fusion.11), kind=kLoop, calls=%fused_computation.21 | loop fusion | flops 65536 | bytes 264192 | tf_op jit(solution)/shard_map/mul | solution.py:46
  11.9 1.4 %collective-permute-done.3 = bf16[1024,128]{1,0:T(8,128)(2,1)S(1)} collective-permute-done((bf16[1024,128]{1,0:T(8,128)(2,1)}, bf16[1024,128]{1,0:T(8,128)(2,1)S(1)}, u32[]{:S(2)}, u32[]{:S(2)}) %collective-permute-start.3) | collective-permute-done | bytes 262176 | tf_op jit(solution)/shard_map/ppermute | solution.py:486
  13.3 1.9 %collective-permute-start.6 = (bf16[1024,128]{1,0:T(8,128)(2,1)S(1)}, bf16[1024,128]{1,0:T(8,128)(2,1)S(1)}, u32[]{:S(2)}, u32[]{:S(2)}) collective-permute-start(bf16[1024,128]{1,0:T(8,128)(2,1)S(1)} %collective-permute-done.3), channel_id=1, source_target_pairs={{0,64},{8,72},{16,80},{24,88},{32,96},{40,104},{48,112},{56,120},{... | collective-permute-start | bytes 786440 | tf_op jit(solution)/shard_map/ppermute | solution.py:486
  15.3 1.5 %collective-permute-start.4 = (bf16[1024,128]{1,0:T(8,128)(2,1)S(1)}, bf16[1024,128]{1,0:T(8,128)(2,1)S(1)}, u32[]{:S(2)}, u32[]{:S(2)}) collective-permute-start(bf16[1024,128]{1,0:T(8,128)(2,1)S(1)} %collective-permute-done), channel_id=1, source_target_pairs={{0,16},{8,24},{16,32},{24,40},{32,48},{40,56},{48,0},{56,8},{64,80... | collective-permute-start | bytes 786440 | tf_op jit(solution)/shard_map/ppermute | solution.py:486
  17.3 7.4 %shard_map.148 = (bf16[3,64,1024]{2,1,0:T(8,128)(2,1)}, f32[4,384,128]{2,1,0:T(8,128)}, f32[4,384,256]{2,1,0:T(8,128)}, bf16[64,64,256]{2,1,0:T(8,128)(2,1)}) custom-call(s32[16,64]{1,0:T(8,128)} %bitcast.62, s32[1]{0:T(128)} %bitcast.2.me_ref, bf16[3,64,1024]{2,1,0:T(8,128)(2,1)} %bitcast.70, f32[4,64,128]{2,1,0:T(8,128)} %get-tuple-element.81.cos_ref, ...), custom_call_target="tpu_custom_call" | custom-call | tf_op jit(solution)/shard_map/pallas_call | solution.py:128
  25.0 1.2 pad_maximum_fusion.refs_0_
  26.6 5.2 %all-to-all-start = ((bf16[16,4,64,256]{3,2,1,0:T(8,128)(2,1)}), bf16[16,4,64,256]{3,2,1,0:T(8,128)(2,1)S(1)}, u32[]{:S(2)}, u32[]{:S(2)}) async-start(bf16[16,4,64,256]{3,2,1,0:T(8,128)(2,1)} %bitcast.66), calls=%async_computation | async-start | bytes 4194304 | tf_op jit(solution)/shard_map/all_to_all | solution.py:551
  31.8 24.9 %shard_map.150 = (bf16[4,192,512]{2,1,0:T(8,128)(2,1)}, bf16[2,192,512]{2,1,0:T(8,128)(2,1)}, bf16[2,192,512]{2,1,0:T(8,128)(2,1)}, bf16[2,192,512]{2,1,0:T(8,128)(2,1)}, bf16[192,1024]{1,0:T(8,128)(2,1)}) custom-call(s32[4,16]{1,0:T(4,128)} %bitcast.88, s32[1]{0:T(128)} %bitcast.2.me_ref, s32[1]{0:T(128)} %bitcast.head_ref, ...), custom_call_target="tpu_custom_call" | custom-call | tf_op jit(solution)/shard_map/pallas_call | solution.py:309
  56.7 3.7 %collective-permute-start.12 = (bf16[4,192,512]{2,1,0:T(8,128)(2,1)}, bf16[4,192,512]{2,1,0:T(8,128)(2,1)S(1)}, u32[]{:S(2)}, u32[]{:S(2)}) collective-permute-start(bf16[4,192,512]{2,1,0:T(8,128)(2,1)} %get-tuple-element.54), channel_id=1, source_target_pairs={{0,4},{1,5},{2,6},{3,7},{4,0},{5,1},{6,2},{7,3},{8,12},{9,13},{10,... | collective-permute-start | bytes 2359304 | tf_op jit(solution)/shard_map/ppermute | solution.py:494
  60.4 2.8 %collective-permute-start.10 = (bf16[2,192,512]{2,1,0:T(8,128)(2,1)}, bf16[2,192,512]{2,1,0:T(8,128)(2,1)S(1)}, u32[]{:S(2)}, u32[]{:S(2)}) collective-permute-start(bf16[2,192,512]{2,1,0:T(8,128)(2,1)} %get-tuple-element.52), channel_id=1, source_target_pairs={{0,3},{1,2},{2,1},{3,0},{4,7},{5,6},{6,5},{7,4},{8,11},{9,10},{10,... | collective-permute-start | bytes 1179656 | tf_op jit(solution)/shard_map/ppermute | solution.py:494
  63.1 0.8 collective-permute-start.11
  64.5 1.0 copy-done
  65.5 5.4 %shard_map.151 = bf16[6,192,512]{2,1,0:T(8,128)(2,1)S(1)} custom-call(s32[1]{0:T(128)} %bitcast.head_ref, bf16[192,1024]{1,0:T(8,128)(2,1)S(1)} %copy-done, bf16[1024,8192]{1,0:T(8,128)(2,1)} %w_ref.1), custom_call_target="tpu_custom_call" | custom-call | tf_op jit(solution)/shard_map/pallas_call | solution.py:359
  70.9 11.1 %collective-permute-done.10 = bf16[2,192,512]{2,1,0:T(8,128)(2,1)S(1)} collective-permute-done((bf16[2,192,512]{2,1,0:T(8,128)(2,1)}, bf16[2,192,512]{2,1,0:T(8,128)(2,1)S(1)}, u32[]{:S(2)}, u32[]{:S(2)}) %collective-permute-start.10) | collective-permute-done | bytes 393248 | tf_op jit(solution)/shard_map/ppermute | solution.py:494
  82.0 0.6 collective-permute-done.9
  82.6 1.1 fusion.11
  83.7 1.5 %collective-permute-start.20 = (bf16[96,512]{1,0:T(8,128)(2,1)}, bf16[96,512]{1,0:T(8,128)(2,1)}, u32[]{:S(2)}, u32[]{:S(2)}) collective-permute-start(bf16[96,512]{1,0:T(8,128)(2,1)} %get-tuple-element.75), channel_id=1, source_target_pairs={{0,1},{1,0},{2,3},{3,2},{4,5},{5,4},{6,7},{7,6},{8,9},{9,8},{10,11... | collective-permute-start | bytes 294920 | tf_op jit(solution)/shard_map/ppermute | solution.py:494
  85.2 2.1 %collective-permute-start.21 = (bf16[96,512]{1,0:T(8,128)(2,1)}, bf16[96,512]{1,0:T(8,128)(2,1)}, u32[]{:S(2)}, u32[]{:S(2)}) collective-permute-start(bf16[96,512]{1,0:T(8,128)(2,1)} %get-tuple-element.74), channel_id=1, source_target_pairs={{0,3},{1,2},{2,1},{3,0},{4,7},{5,6},{6,5},{7,4},{8,11},{9,10},{10,... | collective-permute-start | bytes 294920 | tf_op jit(solution)/shard_map/ppermute | solution.py:494
  87.3 0.6 collective-permute-start.14
  87.9 0.6 collective-permute-start.15
  88.5 3.0 %collective-permute-start.16 = (bf16[96,512]{1,0:T(8,128)(2,1)}, bf16[96,512]{1,0:T(8,128)(2,1)}, u32[]{:S(2)}, u32[]{:S(2)}) collective-permute-start(bf16[96,512]{1,0:T(8,128)(2,1)} %get-tuple-element.76), channel_id=1, source_target_pairs={{0,2},{1,3},{2,0},{3,1},{4,6},{5,7},{6,4},{7,5},{8,10},{9,11},{10,... | collective-permute-start | bytes 294920 | tf_op jit(solution)/shard_map/ppermute | solution.py:494
  91.5 1.4 %add_convert_fusion.1 = bf16[2,192,512]{2,1,0:T(8,128)(2,1)S(1)} fusion(bf16[2,192,512]{2,1,0:T(8,128)(2,1)} %copy-done.7, bf16[2,192,512]{2,1,0:T(8,128)(2,1)} %copy-done.6, bf16[2,192,512]{2,1,0:T(8,128)(2,1)} %copy-done.8, bf16[6,192,512]{2,1,0:T(8,128)(2,1)S(1)} %shard_map.151), kind=kLoop, calls=%fused_computation.3 | loop fusion | flops 1572864 | bytes 1966080 | tf_op jit(solution)/shard_map/convert_element_type | solution.py:505
  93.0 0.7 collective-permute-start.22
  93.7 3.0 %collective-permute-done.15 = bf16[96,512]{1,0:T(8,128)(2,1)} collective-permute-done((bf16[96,512]{1,0:T(8,128)(2,1)}, bf16[96,512]{1,0:T(8,128)(2,1)}, u32[]{:S(2)}, u32[]{:S(2)}) %collective-permute-start.15) | collective-permute-done | bytes 98336 | tf_op jit(solution)/shard_map/ppermute | solution.py:494
  96.7 1.1 fusion.2
  97.8 2.0 %collective-permute-start.17 = (bf16[96,512]{1,0:T(8,128)(2,1)S(1)}, bf16[96,512]{1,0:T(8,128)(2,1)S(1)}, u32[]{:S(2)}, u32[]{:S(2)}) collective-permute-start(bf16[96,512]{1,0:T(8,128)(2,1)S(1)} %fusion.2), channel_id=1, source_target_pairs={{0,2},{1,3},{2,0},{3,1},{4,6},{5,7},{6,4},{7,5},{8,10},{9,11},{10,... | collective-permute-start | bytes 294920 | tf_op jit(solution)/shard_map/ppermute | solution.py:494
  99.9 0.6 collective-permute-start.18
  100.5 1.6 %collective-permute-start.19 = (bf16[96,512]{1,0:T(8,128)(2,1)S(1)}, bf16[96,512]{1,0:T(8,128)(2,1)S(1)}, u32[]{:S(2)}, u32[]{:S(2)}) collective-permute-start(bf16[96,512]{1,0:T(8,128)(2,1)S(1)} %fusion.2), channel_id=1, source_target_pairs={{0,3},{1,2},{2,1},{3,0},{4,7},{5,6},{6,5},{7,4},{8,11},{9,10},{10,... | collective-permute-start | bytes 294920 | tf_op jit(solution)/shard_map/ppermute | solution.py:494
  102.0 1.0 add_convert_fusion.2
  103.1 1.7 %collective-permute-done.17 = bf16[96,512]{1,0:T(8,128)(2,1)S(1)} collective-permute-done((bf16[96,512]{1,0:T(8,128)(2,1)S(1)}, bf16[96,512]{1,0:T(8,128)(2,1)S(1)}, u32[]{:S(2)}, u32[]{:S(2)}) %collective-permute-start.17) | collective-permute-done | bytes 98336 | tf_op jit(solution)/shard_map/ppermute | solution.py:494
  104.8 1.9 %collective-permute-start.24 = (bf16[96,512]{1,0:T(8,128)(2,1)S(1)}, bf16[96,512]{1,0:T(8,128)(2,1)S(1)}, u32[]{:S(2)}, u32[]{:S(2)}) collective-permute-start(bf16[96,512]{1,0:T(8,128)(2,1)S(1)} %add_convert_fusion.2), channel_id=1, source_target_pairs={{0,3},{1,2},{2,1},{3,0},{4,7},{5,6},{6,5},{7,4},{8,11},{9,10},{10,... | collective-permute-start | bytes 294920 | tf_op jit(solution)/shard_map/ppermute | solution.py:494
  107.6 3.3 %collective-permute-start.26 = (bf16[4,96,512]{2,1,0:T(8,128)(2,1)S(1)}, bf16[4,96,512]{2,1,0:T(8,128)(2,1)}, u32[]{:S(2)}, u32[]{:S(2)}) collective-permute-start(bf16[4,96,512]{2,1,0:T(8,128)(2,1)S(1)} %pad_maximum_fusion.2.refs_1_), channel_id=1, source_target_pairs={{0,4},{1,5},{2,6},{3,7},{4,0},{5,1},{6,2},{7,3},{8,12},{9,13},{10,... | collective-permute-start | bytes 1179656 | tf_op jit(solution)/shard_map/ppermute | solution.py:494
  111.0 1.9 %collective-permute-done.25 = bf16[96,512]{1,0:T(8,128)(2,1)S(1)} collective-permute-done((bf16[96,512]{1,0:T(8,128)(2,1)S(1)}, bf16[96,512]{1,0:T(8,128)(2,1)S(1)}, u32[]{:S(2)}, u32[]{:S(2)}) %collective-permute-start.25) | collective-permute-done | bytes 98336 | tf_op jit(solution)/shard_map/ppermute | solution.py:494
  112.9 1.8 %collective-permute-start.27 = (bf16[4,96,512]{2,1,0:T(8,128)(2,1)S(1)}, bf16[4,96,512]{2,1,0:T(8,128)(2,1)}, u32[]{:S(2)}, u32[]{:S(2)}) collective-permute-start(bf16[4,96,512]{2,1,0:T(8,128)(2,1)S(1)} %pad_maximum_fusion.3.refs_2_), channel_id=1, source_target_pairs={{0,4},{1,5},{2,6},{3,7},{4,0},{5,1},{6,2},{7,3},{8,12},{9,13},{10,... | collective-permute-start | bytes 1179656 | tf_op jit(solution)/shard_map/ppermute | solution.py:494
  114.7 2.4 %collective-permute-start.28 = (bf16[2,192,512]{2,1,0:T(8,128)(2,1)S(1)}, bf16[2,192,512]{2,1,0:T(8,128)(2,1)}, u32[]{:S(2)}, u32[]{:S(2)}) collective-permute-start(bf16[2,192,512]{2,1,0:T(8,128)(2,1)S(1)} %add_convert_fusion.refs_0_), channel_id=1, source_target_pairs={{0,2},{1,3},{2,0},{3,1},{4,6},{5,7},{6,4},{7,5},{8,10},{9,11},{10,... | collective-permute-start | bytes 1179656 | tf_op jit(solution)/shard_map/ppermute | solution.py:494
  117.2 1.2 collective-permute-start.29
  118.8 4.7 %shard_map.152 = (bf16[4,1024,128]{2,1,0:T(8,128)(2,1)}, bf16[4,1024,128]{2,1,0:T(8,128)(2,1)}) custom-call(s32[1]{0:T(128)} %bitcast.39.first_ref, s32[16,64]{1,0:T(8,128)S(1)} %bitcast.64, s32[16,64]{1,0:T(8,128)S(1)} %bitcast.63, bf16[16,4,64,256]{3,2,1,0:T(8,128)(2,1)S(1)} %all-to-all-done.source), custom_call_target="tpu_custom_call" | custom-call | tf_op jit(solution)/shard_map/pallas_call | solution.py:466
  123.5 1.8 %shard_map.153.earlier = bf16[192,8192]{1,0:T(8,128)(2,1)} custom-call(s32[1]{0:T(128)} %bitcast.head_ref, bf16[2,192,512]{2,1,0:T(8,128)(2,1)S(1)} %add_convert_fusion.refs_0_, bf16[4,96,512]{2,1,0:T(8,128)(2,1)S(1)} %pad_maximum_fusion.2.refs_1_, bf16[4,96,512]{2,1,0:T(8,128)(2,1)S(1)} %pad_maximum_fusion.3.refs_2_), custom_call_target="tpu_custom_call" | custom-call | tf_op jit(solution)/shard_map/pallas_call | solution.py:396
  125.3 1.1 collective-permute-done.28.refs_2_
  126.3 2.2 %collective-permute-done.29.refs_3_ = bf16[2,192,512]{2,1,0:T(8,128)(2,1)} collective-permute-done((bf16[2,192,512]{2,1,0:T(8,128)(2,1)S(1)}, bf16[2,192,512]{2,1,0:T(8,128)(2,1)}, u32[]{:S(2)}, u32[]{:S(2)}) %collective-permute-start.29) | collective-permute-done | bytes 393248 | tf_op jit(solution)/shard_map/ppermute | solution.py:494
  128.5 1.9 %collective-permute-done.30.refs_4_ = bf16[2,192,512]{2,1,0:T(8,128)(2,1)} collective-permute-done((bf16[2,192,512]{2,1,0:T(8,128)(2,1)S(1)}, bf16[2,192,512]{2,1,0:T(8,128)(2,1)}, u32[]{:S(2)}, u32[]{:S(2)}) %collective-permute-start.30) | collective-permute-done | bytes 393248 | tf_op jit(solution)/shard_map/ppermute | solution.py:494
  130.4 2.8 %shard_map.154 = bf16[192,8192]{1,0:T(8,128)(2,1)} custom-call(s32[1]{0:T(128)} %bitcast.head_ref, bf16[192,8192]{1,0:T(8,128)(2,1)} %shard_map.153.earlier, bf16[4,96,512]{2,1,0:T(8,128)(2,1)} %collective-permute-done.26.refs_0_, bf16[4,96,512]{2,1,0:T(8,128)(2,1)} %collective-permute-done.27.refs_1_, ...), custom_call_target="tpu_custom_call", output_to_operand_aliasing={{}: (1, {})} | custom-call | tf_op jit(solution)/shard_map/pallas_call | solution.py:425
  (55 shorter events, 3.3 us)
Async XLA Ops:
  2.4 11.0 %collective-permute-start.3 = (bf16[1024,128]{1,0:T(8,128)(2,1)}, bf16[1024,128]{1,0:T(8,128)(2,1)S(1)}, u32[]{:S(2)}, u32[]{:S(2)}) collective-permute-start(bf16[1024,128]{1,0:T(8,128)(2,1)} %shard_map.149), channel_id=1, source_target_pairs={{0,32},{8,40},{16,48},{24,56},{32,0},{40,8},{48,16},{56,24},{64,96... | collective-permute-start | bytes 786440 | tf_op jit(solution)/shard_map/ppermute | solution.py:486
  4.7 10.6 %collective-permute-start = (bf16[1024,128]{1,0:T(8,128)(2,1)}, bf16[1024,128]{1,0:T(8,128)(2,1)S(1)}, u32[]{:S(2)}, u32[]{:S(2)}) collective-permute-start(bf16[1024,128]{1,0:T(8,128)(2,1)} %shard_map.149), channel_id=1, source_target_pairs={{0,64},{8,72},{16,80},{24,88},{32,96},{40,104},{48,112},{56,120},{... | collective-permute-start | bytes 786440 | tf_op jit(solution)/shard_map/ppermute | solution.py:486
  6.6 18.1 %collective-permute-start.1 = (bf16[1024,128]{1,0:T(8,128)(2,1)}, bf16[1024,128]{1,0:T(8,128)(2,1)S(1)}, u32[]{:S(2)}, u32[]{:S(2)}) collective-permute-start(bf16[1024,128]{1,0:T(8,128)(2,1)} %shard_map.149), channel_id=1, source_target_pairs={{0,16},{8,24},{16,32},{24,40},{32,48},{40,56},{48,0},{56,8},{64,80... | collective-permute-start | bytes 786440 | tf_op jit(solution)/shard_map/ppermute | solution.py:486
  6.6 18.1 %collective-permute-start.2 = (bf16[1024,128]{1,0:T(8,128)(2,1)}, bf16[1024,128]{1,0:T(8,128)(2,1)S(1)}, u32[]{:S(2)}, u32[]{:S(2)}) collective-permute-start(bf16[1024,128]{1,0:T(8,128)(2,1)} %shard_map.149), channel_id=1, source_target_pairs={{0,48},{8,56},{16,0},{24,8},{32,16},{40,24},{48,32},{56,40},{64,11... | collective-permute-start | bytes 786440 | tf_op jit(solution)/shard_map/ppermute | solution.py:486
  13.3 11.4 %collective-permute-start.6 = (bf16[1024,128]{1,0:T(8,128)(2,1)S(1)}, bf16[1024,128]{1,0:T(8,128)(2,1)S(1)}, u32[]{:S(2)}, u32[]{:S(2)}) collective-permute-start(bf16[1024,128]{1,0:T(8,128)(2,1)S(1)} %collective-permute-done.3), channel_id=1, source_target_pairs={{0,64},{8,72},{16,80},{24,88},{32,96},{40,104},{48,112},{56,120},{... | collective-permute-start | bytes 786440 | tf_op jit(solution)/shard_map/ppermute | solution.py:486
  15.3 9.5 %collective-permute-start.4 = (bf16[1024,128]{1,0:T(8,128)(2,1)S(1)}, bf16[1024,128]{1,0:T(8,128)(2,1)S(1)}, u32[]{:S(2)}, u32[]{:S(2)}) collective-permute-start(bf16[1024,128]{1,0:T(8,128)(2,1)S(1)} %collective-permute-done), channel_id=1, source_target_pairs={{0,16},{8,24},{16,32},{24,40},{32,48},{40,56},{48,0},{56,8},{64,80... | collective-permute-start | bytes 786440 | tf_op jit(solution)/shard_map/ppermute | solution.py:486
  16.8 8.0 %collective-permute-start.5 = (bf16[1024,128]{1,0:T(8,128)(2,1)S(1)}, bf16[1024,128]{1,0:T(8,128)(2,1)S(1)}, u32[]{:S(2)}, u32[]{:S(2)}) collective-permute-start(bf16[1024,128]{1,0:T(8,128)(2,1)S(1)} %collective-permute-done), channel_id=1, source_target_pairs={{0,48},{8,56},{16,0},{24,8},{32,16},{40,24},{48,32},{56,40},{64,11... | collective-permute-start | bytes 786440 | tf_op jit(solution)/shard_map/ppermute | solution.py:486
  17.3 7.7 %copy-start.4 = (bf16[1024,128]{1,0:T(8,128)(2,1)S(1)}, bf16[1024,128]{1,0:T(8,128)(2,1)}, u32[]{:S(2)}) copy-start(bf16[1024,128]{1,0:T(8,128)(2,1)} %shard_map.149) | copy-start | bytes 786436
  24.9 1.7 %copy-start.3 = (bf16[4,1024,128]{2,1,0:T(8,128)(2,1)}, bf16[4,1024,128]{2,1,0:T(8,128)(2,1)S(1)}, u32[]{:S(2)}) copy-start(bf16[4,1024,128]{2,1,0:T(8,128)(2,1)S(1)} %pad_maximum_fusion.1.refs_2_) | copy-start | bytes 3145732
  24.9 6.9 %collective-permute-start.8 = (bf16[4,1024,128]{2,1,0:T(8,128)(2,1)S(1)}, bf16[4,1024,128]{2,1,0:T(8,128)(2,1)}, u32[]{:S(2)}, u32[]{:S(2)}) collective-permute-start(bf16[4,1024,128]{2,1,0:T(8,128)(2,1)S(1)} %pad_maximum_fusion.1.refs_2_), channel_id=1, source_target_pairs={{0,8},{8,0},{16,24},{24,16},{32,40},{40,32},{48,56},{56,48},{64,72... | collective-permute-start | bytes 3145736 | tf_op jit(solution)/shard_map/ppermute | solution.py:490
  26.2 5.6 %collective-permute-start.7 = (bf16[4,1024,128]{2,1,0:T(8,128)(2,1)}, bf16[4,1024,128]{2,1,0:T(8,128)(2,1)}, u32[]{:S(2)}, u32[]{:S(2)}) collective-permute-start(bf16[4,1024,128]{2,1,0:T(8,128)(2,1)} %pad_maximum_fusion.refs_0_), channel_id=1, source_target_pairs={{0,8},{8,0},{16,24},{24,16},{32,40},{40,32},{48,56},{56,48},{64,72... | collective-permute-start | bytes 3145736 | tf_op jit(solution)/shard_map/ppermute | solution.py:490
  26.6 64.9 %all-to-all-start = ((bf16[16,4,64,256]{3,2,1,0:T(8,128)(2,1)}), bf16[16,4,64,256]{3,2,1,0:T(8,128)(2,1)S(1)}, u32[]{:S(2)}, u32[]{:S(2)}) async-start(bf16[16,4,64,256]{3,2,1,0:T(8,128)(2,1)} %bitcast.66), calls=%async_computation | async-start | bytes 4194304 | tf_op jit(solution)/shard_map/all_to_all | solution.py:551
  56.7 25.9 %collective-permute-start.12 = (bf16[4,192,512]{2,1,0:T(8,128)(2,1)}, bf16[4,192,512]{2,1,0:T(8,128)(2,1)S(1)}, u32[]{:S(2)}, u32[]{:S(2)}) collective-permute-start(bf16[4,192,512]{2,1,0:T(8,128)(2,1)} %get-tuple-element.54), channel_id=1, source_target_pairs={{0,4},{1,5},{2,6},{3,7},{4,0},{5,1},{6,2},{7,3},{8,12},{9,13},{10,... | collective-permute-start | bytes 2359304 | tf_op jit(solution)/shard_map/ppermute | solution.py:494
  60.4 21.6 %collective-permute-start.10 = (bf16[2,192,512]{2,1,0:T(8,128)(2,1)}, bf16[2,192,512]{2,1,0:T(8,128)(2,1)S(1)}, u32[]{:S(2)}, u32[]{:S(2)}) collective-permute-start(bf16[2,192,512]{2,1,0:T(8,128)(2,1)} %get-tuple-element.52), channel_id=1, source_target_pairs={{0,3},{1,2},{2,1},{3,0},{4,7},{5,6},{6,5},{7,4},{8,11},{9,10},{10,... | collective-permute-start | bytes 1179656 | tf_op jit(solution)/shard_map/ppermute | solution.py:494
  63.1 18.9 %collective-permute-start.11 = (bf16[2,192,512]{2,1,0:T(8,128)(2,1)}, bf16[2,192,512]{2,1,0:T(8,128)(2,1)S(1)}, u32[]{:S(2)}, u32[]{:S(2)}) collective-permute-start(bf16[2,192,512]{2,1,0:T(8,128)(2,1)} %get-tuple-element.53), channel_id=1, source_target_pairs={{0,2},{1,3},{2,0},{3,1},{4,6},{5,7},{6,4},{7,5},{8,10},{9,11},{10,... | collective-permute-start | bytes 1179656 | tf_op jit(solution)/shard_map/ppermute | solution.py:494
  63.9 18.7 %collective-permute-start.9 = (bf16[2,192,512]{2,1,0:T(8,128)(2,1)}, bf16[2,192,512]{2,1,0:T(8,128)(2,1)S(1)}, u32[]{:S(2)}, u32[]{:S(2)}) collective-permute-start(bf16[2,192,512]{2,1,0:T(8,128)(2,1)} %get-tuple-element.51), channel_id=1, source_target_pairs={{0,1},{1,0},{2,3},{3,2},{4,5},{5,4},{6,7},{7,6},{8,9},{9,8},{10,11... | collective-permute-start | bytes 1179656 | tf_op jit(solution)/shard_map/ppermute | solution.py:494
  64.5 1.0 copy-start
  82.0 6.5 %copy-start.6 = (bf16[2,192,512]{2,1,0:T(8,128)(2,1)}, bf16[2,192,512]{2,1,0:T(8,128)(2,1)S(1)}, u32[]{:S(2)}) copy-start(bf16[2,192,512]{2,1,0:T(8,128)(2,1)S(1)} %collective-permute-done.10) | copy-start | bytes 1179652
  82.0 6.5 %copy-start.7 = (bf16[2,192,512]{2,1,0:T(8,128)(2,1)}, bf16[2,192,512]{2,1,0:T(8,128)(2,1)S(1)}, u32[]{:S(2)}) copy-start(bf16[2,192,512]{2,1,0:T(8,128)(2,1)S(1)} %collective-permute-done.11) | copy-start | bytes 1179652
  82.6 5.9 %copy-start.8 = (bf16[2,192,512]{2,1,0:T(8,128)(2,1)}, bf16[2,192,512]{2,1,0:T(8,128)(2,1)S(1)}, u32[]{:S(2)}) copy-start(bf16[2,192,512]{2,1,0:T(8,128)(2,1)S(1)} %collective-permute-done.9) | copy-start | bytes 1179652
  82.6 5.9 %copy-start.5 = (bf16[4,192,512]{2,1,0:T(8,128)(2,1)}, bf16[4,192,512]{2,1,0:T(8,128)(2,1)S(1)}, u32[]{:S(2)}) copy-start(bf16[4,192,512]{2,1,0:T(8,128)(2,1)S(1)} %collective-permute-done.12) | copy-start | bytes 2359300
  83.7 16.1 %collective-permute-start.20 = (bf16[96,512]{1,0:T(8,128)(2,1)}, bf16[96,512]{1,0:T(8,128)(2,1)}, u32[]{:S(2)}, u32[]{:S(2)}) collective-permute-start(bf16[96,512]{1,0:T(8,128)(2,1)} %get-tuple-element.75), channel_id=1, source_target_pairs={{0,1},{1,0},{2,3},{3,2},{4,5},{5,4},{6,7},{7,6},{8,9},{9,8},{10,11... | collective-permute-start | bytes 294920 | tf_op jit(solution)/shard_map/ppermute | solution.py:494
  85.2 15.3 %collective-permute-start.21 = (bf16[96,512]{1,0:T(8,128)(2,1)}, bf16[96,512]{1,0:T(8,128)(2,1)}, u32[]{:S(2)}, u32[]{:S(2)}) collective-permute-start(bf16[96,512]{1,0:T(8,128)(2,1)} %get-tuple-element.74), channel_id=1, source_target_pairs={{0,3},{1,2},{2,1},{3,0},{4,7},{5,6},{6,5},{7,4},{8,11},{9,10},{10,... | collective-permute-start | bytes 294920 | tf_op jit(solution)/shard_map/ppermute | solution.py:494
  87.3 5.7 %collective-permute-start.14 = (bf16[96,512]{1,0:T(8,128)(2,1)}, bf16[96,512]{1,0:T(8,128)(2,1)}, u32[]{:S(2)}, u32[]{:S(2)}) collective-permute-start(bf16[96,512]{1,0:T(8,128)(2,1)} %get-tuple-element.78), channel_id=1, source_target_pairs={{0,1},{1,0},{2,3},{3,2},{4,5},{5,4},{6,7},{7,6},{8,9},{9,8},{10,11... | collective-permute-start | bytes 294920 | tf_op jit(solution)/shard_map/ppermute | solution.py:494
  87.9 8.8 %collective-permute-start.15 = (bf16[96,512]{1,0:T(8,128)(2,1)}, bf16[96,512]{1,0:T(8,128)(2,1)}, u32[]{:S(2)}, u32[]{:S(2)}) collective-permute-start(bf16[96,512]{1,0:T(8,128)(2,1)} %get-tuple-element.77), channel_id=1, source_target_pairs={{0,3},{1,2},{2,1},{3,0},{4,7},{5,6},{6,5},{7,4},{8,11},{9,10},{10,... | collective-permute-start | bytes 294920 | tf_op jit(solution)/shard_map/ppermute | solution.py:494
  88.5 8.2 %collective-permute-start.16 = (bf16[96,512]{1,0:T(8,128)(2,1)}, bf16[96,512]{1,0:T(8,128)(2,1)}, u32[]{:S(2)}, u32[]{:S(2)}) collective-permute-start(bf16[96,512]{1,0:T(8,128)(2,1)} %get-tuple-element.76), channel_id=1, source_target_pairs={{0,2},{1,3},{2,0},{3,1},{4,6},{5,7},{6,4},{7,5},{8,10},{9,11},{10,... | collective-permute-start | bytes 294920 | tf_op jit(solution)/shard_map/ppermute | solution.py:494
  92.9 25.9 %copy-start.1 = (s32[64,16]{0,1:T(8,128)S(1)}, s32[64,16]{0,1:T(8,128)}, u32[]{:S(2)}) copy-start(s32[64,16]{0,1:T(8,128)} %param.20) | copy-start | bytes 12292
  93.0 25.9 %copy-start.2 = (s32[64,16]{0,1:T(8,128)S(1)}, s32[64,16]{0,1:T(8,128)}, u32[]{:S(2)}) copy-start(s32[64,16]{0,1:T(8,128)} %param.21) | copy-start | bytes 12292
  93.0 9.0 %collective-permute-start.22 = (bf16[96,512]{1,0:T(8,128)(2,1)S(1)}, bf16[96,512]{1,0:T(8,128)(2,1)S(1)}, u32[]{:S(2)}, u32[]{:S(2)}) collective-permute-start(bf16[96,512]{1,0:T(8,128)(2,1)S(1)} %get-tuple-element.73), channel_id=1, source_target_pairs={{0,2},{1,3},{2,0},{3,1},{4,6},{5,7},{6,4},{7,5},{8,10},{9,11},{10,... | collective-permute-start | bytes 294920 | tf_op jit(solution)/shard_map/ppermute | solution.py:494
  96.7 14.1 %collective-permute-start.13 = (bf16[2,192,512]{2,1,0:T(8,128)(2,1)S(1)}, bf16[2,192,512]{2,1,0:T(8,128)(2,1)S(1)}, u32[]{:S(2)}, u32[]{:S(2)}) collective-permute-start(bf16[2,192,512]{2,1,0:T(8,128)(2,1)S(1)} %add_convert_fusion.1), channel_id=1, source_target_pairs={{0,4},{1,5},{2,6},{3,7},{4,0},{5,1},{6,2},{7,3},{8,12},{9,13},{10,... | collective-permute-start | bytes 1179656 | tf_op jit(solution)/shard_map/ppermute | solution.py:494
  97.8 7.0 %collective-permute-start.17 = (bf16[96,512]{1,0:T(8,128)(2,1)S(1)}, bf16[96,512]{1,0:T(8,128)(2,1)S(1)}, u32[]{:S(2)}, u32[]{:S(2)}) collective-permute-start(bf16[96,512]{1,0:T(8,128)(2,1)S(1)} %fusion.2), channel_id=1, source_target_pairs={{0,2},{1,3},{2,0},{3,1},{4,6},{5,7},{6,4},{7,5},{8,10},{9,11},{10,... | collective-permute-start | bytes 294920 | tf_op jit(solution)/shard_map/ppermute | solution.py:494
  99.9 6.9 %collective-permute-start.18 = (bf16[96,512]{1,0:T(8,128)(2,1)S(1)}, bf16[96,512]{1,0:T(8,128)(2,1)S(1)}, u32[]{:S(2)}, u32[]{:S(2)}) collective-permute-start(bf16[96,512]{1,0:T(8,128)(2,1)S(1)} %fusion.2), channel_id=1, source_target_pairs={{0,1},{1,0},{2,3},{3,2},{4,5},{5,4},{6,7},{7,6},{8,9},{9,8},{10,11... | collective-permute-start | bytes 294920 | tf_op jit(solution)/shard_map/ppermute | solution.py:494
  100.5 7.0 %collective-permute-start.19 = (bf16[96,512]{1,0:T(8,128)(2,1)S(1)}, bf16[96,512]{1,0:T(8,128)(2,1)S(1)}, u32[]{:S(2)}, u32[]{:S(2)}) collective-permute-start(bf16[96,512]{1,0:T(8,128)(2,1)S(1)} %fusion.2), channel_id=1, source_target_pairs={{0,3},{1,2},{2,1},{3,0},{4,7},{5,6},{6,5},{7,4},{8,11},{9,10},{10,... | collective-permute-start | bytes 294920 | tf_op jit(solution)/shard_map/ppermute | solution.py:494
  103.0 8.0 %collective-permute-start.23 = (bf16[96,512]{1,0:T(8,128)(2,1)S(1)}, bf16[96,512]{1,0:T(8,128)(2,1)S(1)}, u32[]{:S(2)}, u32[]{:S(2)}) collective-permute-start(bf16[96,512]{1,0:T(8,128)(2,1)S(1)} %add_convert_fusion.2), channel_id=1, source_target_pairs={{0,1},{1,0},{2,3},{3,2},{4,5},{5,4},{6,7},{7,6},{8,9},{9,8},{10,11... | collective-permute-start | bytes 294920 | tf_op jit(solution)/shard_map/ppermute | solution.py:494
  104.8 6.2 %collective-permute-start.24 = (bf16[96,512]{1,0:T(8,128)(2,1)S(1)}, bf16[96,512]{1,0:T(8,128)(2,1)S(1)}, u32[]{:S(2)}, u32[]{:S(2)}) collective-permute-start(bf16[96,512]{1,0:T(8,128)(2,1)S(1)} %add_convert_fusion.2), channel_id=1, source_target_pairs={{0,3},{1,2},{2,1},{3,0},{4,7},{5,6},{6,5},{7,4},{8,11},{9,10},{10,... | collective-permute-start | bytes 294920 | tf_op jit(solution)/shard_map/ppermute | solution.py:494
  106.7 6.1 %collective-permute-start.25 = (bf16[96,512]{1,0:T(8,128)(2,1)S(1)}, bf16[96,512]{1,0:T(8,128)(2,1)S(1)}, u32[]{:S(2)}, u32[]{:S(2)}) collective-permute-start(bf16[96,512]{1,0:T(8,128)(2,1)S(1)} %add_convert_fusion.2), channel_id=1, source_target_pairs={{0,2},{1,3},{2,0},{3,1},{4,6},{5,7},{6,4},{7,5},{8,10},{9,11},{10,... | collective-permute-start | bytes 294920 | tf_op jit(solution)/shard_map/ppermute | solution.py:494
  107.6 17.7 %collective-permute-start.26 = (bf16[4,96,512]{2,1,0:T(8,128)(2,1)S(1)}, bf16[4,96,512]{2,1,0:T(8,128)(2,1)}, u32[]{:S(2)}, u32[]{:S(2)}) collective-permute-start(bf16[4,96,512]{2,1,0:T(8,128)(2,1)S(1)} %pad_maximum_fusion.2.refs_1_), channel_id=1, source_target_pairs={{0,4},{1,5},{2,6},{3,7},{4,0},{5,1},{6,2},{7,3},{8,12},{9,13},{10,... | collective-permute-start | bytes 1179656 | tf_op jit(solution)/shard_map/ppermute | solution.py:494
  112.9 12.4 %collective-permute-start.27 = (bf16[4,96,512]{2,1,0:T(8,128)(2,1)S(1)}, bf16[4,96,512]{2,1,0:T(8,128)(2,1)}, u32[]{:S(2)}, u32[]{:S(2)}) collective-permute-start(bf16[4,96,512]{2,1,0:T(8,128)(2,1)S(1)} %pad_maximum_fusion.3.refs_2_), channel_id=1, source_target_pairs={{0,4},{1,5},{2,6},{3,7},{4,0},{5,1},{6,2},{7,3},{8,12},{9,13},{10,... | collective-permute-start | bytes 1179656 | tf_op jit(solution)/shard_map/ppermute | solution.py:494
  114.7 11.6 %collective-permute-start.28 = (bf16[2,192,512]{2,1,0:T(8,128)(2,1)S(1)}, bf16[2,192,512]{2,1,0:T(8,128)(2,1)}, u32[]{:S(2)}, u32[]{:S(2)}) collective-permute-start(bf16[2,192,512]{2,1,0:T(8,128)(2,1)S(1)} %add_convert_fusion.refs_0_), channel_id=1, source_target_pairs={{0,2},{1,3},{2,0},{3,1},{4,6},{5,7},{6,4},{7,5},{8,10},{9,11},{10,... | collective-permute-start | bytes 1179656 | tf_op jit(solution)/shard_map/ppermute | solution.py:494
  117.2 11.4 %collective-permute-start.29 = (bf16[2,192,512]{2,1,0:T(8,128)(2,1)S(1)}, bf16[2,192,512]{2,1,0:T(8,128)(2,1)}, u32[]{:S(2)}, u32[]{:S(2)}) collective-permute-start(bf16[2,192,512]{2,1,0:T(8,128)(2,1)S(1)} %add_convert_fusion.refs_0_), channel_id=1, source_target_pairs={{0,1},{1,0},{2,3},{3,2},{4,5},{5,4},{6,7},{7,6},{8,9},{9,8},{10,11... | collective-permute-start | bytes 1179656 | tf_op jit(solution)/shard_map/ppermute | solution.py:494
  118.4 12.0 %collective-permute-start.30 = (bf16[2,192,512]{2,1,0:T(8,128)(2,1)S(1)}, bf16[2,192,512]{2,1,0:T(8,128)(2,1)}, u32[]{:S(2)}, u32[]{:S(2)}) collective-permute-start(bf16[2,192,512]{2,1,0:T(8,128)(2,1)S(1)} %add_convert_fusion.refs_0_), channel_id=1, source_target_pairs={{0,3},{1,2},{2,1},{3,0},{4,7},{5,6},{6,5},{7,4},{8,11},{9,10},{10,... | collective-permute-start | bytes 1179656 | tf_op jit(solution)/shard_map/ppermute | solution.py:494

commit v2 on v1

--- a/solution.py
+++ b/solution.py
@@ -563,27 +563,30 @@
     got_z = move_x(zsend, 4)
     got_x = move_roles(xo, xp, xq)
     kept = project(attended, out_weight, head, zhere + both[3])
-    got_z = after(got_z, got_x)
+    xsum = add(kept[4:], *after(got_x, gathered))
+    got_z = after(got_z, xsum)
     rows = STEPS * PROBS // 2
     halves = [slice(k, k + rows) for k in (0, rows)]
     zpart = [[add(kept[r][h], got_z[r][h]) for r in roles] for h in halves]
     got_zx = [move_roles(*part[:3]) for part in zpart]
-    got_x = after(got_x, zpart[1][3], gathered)
-    xsum = add(kept[4:], *got_x)
-    got_zx[1] = after(got_zx[1], xsum)
-    zsum = [add(part[3], *got) for part, got in zip(zpart, got_zx)]
 
     pair = add(xsum, move_x(xsum, 4)[::-1])
+    xo = move_x(pair, 2)
+    zsum = [add(zpart[0][3], *got_zx[0])]
+    zsum.append(add(zpart[1][3], *after(got_zx[1], pair, zsum[0])))
     zback = [move_roles(part, part, part) for part in zsum]
-    zback[1] = after(zback[1], pair)
+    zback[1] = after(zback[1], xo)
     zfour = [jnp.stack([zo, zp, zq, part]) for (zp, zq, zo), part in zip(zback, zsum)]
+    pair = after(pair, zfour[0])
+    xp, xq = move_x(pair, 1), move_x(pair, 3)
     zother = [move_x(part, 4) for part in zfour]
-    xp, xq, xo = move_roles(pair, pair, pair)
     joined_keys, joined_values = join(
         (me * share).reshape(1), offsets, lengths, after(gathered, zfour[1])
     )
-    mixed = assemble(head, [both[3], zhere, zhere], after([pair] + zfour, joined_keys))
-    mixed = complete(head, [zthere, zthere] + both[:3], mixed, zother + [xo, xp, xq])
+    mixed = assemble(
+        head, [both[3], both[0], zhere, zhere], after([pair, xo] + zfour, joined_keys)
+    )
+    mixed = complete(head, [zthere, zthere] + both[1:3], mixed, zother + [xp, xq])
     mixed = jnp.transpose(mixed.reshape(STEPS, PROBS, 16 * CHUNK), (1, 0, 2))[None]
     return mixed, joined_keys, joined_values
 

time: 134 us -> 144 us (1.075); the launches traced: 133 us -> 141 us
  starting transfers between devices: 47.9 us -> 54.2 us
  waiting for transfers between devices: 25.2 us -> 22.1 us
  local copies, waits for them, and re-layouts: 1.03 us -> 3.99 us
    ppermute x22, waiting for transfers between devices: 23.8 us -> 16.7 us  [move_x(): return lax.ppermute(value, 'head', [(h, h ^ flip) for h in range(KVH)])]
    ppermute x22, starting transfers between devices: 32.1 us -> 38.2 us  [move_x(): return lax.ppermute(value, 'head', [(h, h ^ flip) for h in range(KVH)])]
    ppermute x2, waiting for transfers between devices: 0.01 us -> 3.99 us  [swap_core(): return lax.ppermute(value, 'branch', [(b, b ^ 1) for b in range(BRANCHES)])]
    unnamed x18, local copies, waits for them, and re-layouts: 1.03 us -> 3.99 us
  transfers between devices with their start and end apart: 32 -> 32, of which waited for: 11 -> 9; matrix products, arithmetic and copies ran while one was open for 7% -> 6% of each run, Pallas kernels for 33% -> 32%
where the time goes in v2:
time: 144 us; the launch traced here: 141 us
  starting transfers between devices  54.2 us (38%)
  Pallas kernels  49.9 us (35%)
  waiting for transfers between devices  22.1 us (15%)
  other arithmetic  10.1 us (7%)
  local copies, waits for them, and re-layouts  3.99 us (3%)
    ppermute x22, starting transfers between devices, move_x(): return lax.ppermute(value, 'head', [(h, h ^ flip) for h in range(KVH)])  38.2 us
    pallas_call x1, Pallas kernels, prompt_part(): pl.pallas_call(functools.partial(prompt_kernel, places, groups, len(stack...  25.5 us
    ppermute x22, waiting for transfers between devices, move_x(): return lax.ppermute(value, 'head', [(h, h ^ flip) for h in range(KVH)])  16.7 us
    ppermute x7, starting transfers between devices, move_chip(): return lax.ppermute(value, 'branch', perm)  10.2 us
    pallas_call x1, Pallas kernels, span_part(): pl.pallas_call(span_kernel, grid_spec=pltpu.PrefetchScalarGridSpec(num_sc...  7.3 us
    convert_element_type x5, other arithmetic, add(): return total.astype(jnp.bfloat16)  5.49 us
    pallas_call x1, Pallas kernels, project(): pl.pallas_call(functools.partial(project_kernel, places), grid_spec=pltpu...  5.46 us
    all_to_all x1, starting transfers between devices, shards(): gathered = lax.all_to_all(sent, 'branch', 0, 0, tiled=True)  5.17 us
  transfers between devices with their start and end apart: 32, of which 9 were waited for; matrix products, arithmetic and copies ran while one was open for 6% of the time, Pallas kernels for 32%

profile of v2, /device:TPU:8, one launch (start us, length us, event | category | flops | bytes accessed | tf_op | source)
XLA Modules:
  0.0 141.3 jit_solution(4056903367801036440)
XLA Ops:
  0.6 1.8 %shard_map.149 = bf16[1024,128]{1,0:T(8,128)(2,1)} custom-call(bf16[512,128]{1,0:T(8,128)(2,1)} %keys_ref.1, bf16[512,128]{1,0:T(8,128)(2,1)} %vals_ref.1), custom_call_target="tpu_custom_call" | custom-call | tf_op jit(solution)/shard_map/pallas_call | solution.py:156
  2.4 2.3 %collective-permute-start.3 = (bf16[1024,128]{1,0:T(8,128)(2,1)}, bf16[1024,128]{1,0:T(8,128)(2,1)S(1)}, u32[]{:S(2)}, u32[]{:S(2)}) collective-permute-start(bf16[1024,128]{1,0:T(8,128)(2,1)} %shard_map.149), channel_id=1, source_target_pairs={{0,32},{8,40},{16,48},{24,56},{32,0},{40,8},{48,16},{56,24},{64,96... | collective-permute-start | bytes 786440 | tf_op jit(solution)/shard_map/ppermute | solution.py:486
  4.7 1.9 %collective-permute-start = (bf16[1024,128]{1,0:T(8,128)(2,1)}, bf16[1024,128]{1,0:T(8,128)(2,1)S(1)}, u32[]{:S(2)}, u32[]{:S(2)}) collective-permute-start(bf16[1024,128]{1,0:T(8,128)(2,1)} %shard_map.149), channel_id=1, source_target_pairs={{0,64},{8,72},{16,80},{24,88},{32,96},{40,104},{48,112},{56,120},{... | collective-permute-start | bytes 786440 | tf_op jit(solution)/shard_map/ppermute | solution.py:486
  6.6 2.0 %collective-permute-start.2 = (bf16[1024,128]{1,0:T(8,128)(2,1)}, bf16[1024,128]{1,0:T(8,128)(2,1)S(1)}, u32[]{:S(2)}, u32[]{:S(2)}) collective-permute-start(bf16[1024,128]{1,0:T(8,128)(2,1)} %shard_map.149), channel_id=1, source_target_pairs={{0,48},{8,56},{16,0},{24,8},{32,16},{40,24},{48,32},{56,40},{64,11... | collective-permute-start | bytes 786440 | tf_op jit(solution)/shard_map/ppermute | solution.py:486
  8.6 0.7 add_bitcast_fusion.1
  9.3 0.7 add_bitcast_fusion
  10.0 1.9 %fusion.6 = (f32[4,64,128]{2,1,0:T(8,128)}, f32[4,64,128]{2,1,0:T(8,128)}) fusion(f32[128]{0:T(128)} %constant.24.clone, f32[128]{0:T(128)} %constant.23.clone, f32[4,64]{1,0:T(4,128)S(1)} %add_convert_fusion.10), kind=kLoop, calls=%fused_computation.24 | loop fusion | flops 65536 | bytes 264192 | tf_op jit(solution)/shard_map/mul | solution.py:46
  11.9 1.4 collective-permute-done.3
  13.3 1.9 %collective-permute-start.6 = (bf16[1024,128]{1,0:T(8,128)(2,1)S(1)}, bf16[1024,128]{1,0:T(8,128)(2,1)S(1)}, u32[]{:S(2)}, u32[]{:S(2)}) collective-permute-start(bf16[1024,128]{1,0:T(8,128)(2,1)S(1)} %collective-permute-done.3), channel_id=1, source_target_pairs={{0,64},{8,72},{16,80},{24,88},{32,96},{40,104},{48,112},{56,120},{... | collective-permute-start | bytes 786440 | tf_op jit(solution)/shard_map/ppermute | solution.py:486
  15.3 1.5 %collective-permute-start.4 = (bf16[1024,128]{1,0:T(8,128)(2,1)S(1)}, bf16[1024,128]{1,0:T(8,128)(2,1)S(1)}, u32[]{:S(2)}, u32[]{:S(2)}) collective-permute-start(bf16[1024,128]{1,0:T(8,128)(2,1)S(1)} %collective-permute-done), channel_id=1, source_target_pairs={{0,16},{8,24},{16,32},{24,40},{32,48},{40,56},{48,0},{56,8},{64,80... | collective-permute-start | bytes 786440 | tf_op jit(solution)/shard_map/ppermute | solution.py:486
  17.3 7.3 %shard_map.148 = (bf16[3,64,1024]{2,1,0:T(8,128)(2,1)}, f32[4,384,128]{2,1,0:T(8,128)}, f32[4,384,256]{2,1,0:T(8,128)}, bf16[64,64,256]{2,1,0:T(8,128)(2,1)}) custom-call(s32[16,64]{1,0:T(8,128)} %bitcast.65, s32[1]{0:T(128)} %bitcast.2.me_ref, bf16[3,64,1024]{2,1,0:T(8,128)(2,1)} %bitcast.73, f32[4,64,128]{2,1,0:T(8,128)} %get-tuple-element.84.cos_ref, ...), custom_call_target="tpu_custom_call" | custom-call | tf_op jit(solution)/shard_map/pallas_call | solution.py:128
  24.8 0.7 copy-done.6
  25.5 1.1 pad_maximum_fusion.refs_0_
  26.6 5.2 %all-to-all-start = ((bf16[16,4,64,256]{3,2,1,0:T(8,128)(2,1)}), bf16[16,4,64,256]{3,2,1,0:T(8,128)(2,1)S(1)}, u32[]{:S(2)}, u32[]{:S(2)}) async-start(bf16[16,4,64,256]{3,2,1,0:T(8,128)(2,1)} %bitcast.69), calls=%async_computation | async-start | bytes 4194304 | tf_op jit(solution)/shard_map/all_to_all | solution.py:551
  32.4 2.3 %collective-permute-done.8.refs_3_ = bf16[4,1024,128]{2,1,0:T(8,128)(2,1)} collective-permute-done((bf16[4,1024,128]{2,1,0:T(8,128)(2,1)S(1)}, bf16[4,1024,128]{2,1,0:T(8,128)(2,1)}, u32[]{:S(2)}, u32[]{:S(2)}) %collective-permute-start.8) | collective-permute-done | bytes 1048608 | tf_op jit(solution)/shard_map/ppermute | solution.py:490
  34.7 1.7 %collective-permute-done.7.refs_1_ = bf16[4,1024,128]{2,1,0:T(8,128)(2,1)} collective-permute-done((bf16[4,1024,128]{2,1,0:T(8,128)(2,1)}, bf16[4,1024,128]{2,1,0:T(8,128)(2,1)}, u32[]{:S(2)}, u32[]{:S(2)}) %collective-permute-start.7) | collective-permute-done | bytes 1048608 | tf_op jit(solution)/shard_map/ppermute | solution.py:490
  36.4 25.5 %shard_map.150 = (bf16[4,192,512]{2,1,0:T(8,128)(2,1)}, bf16[2,192,512]{2,1,0:T(8,128)(2,1)}, bf16[2,192,512]{2,1,0:T(8,128)(2,1)}, bf16[2,192,512]{2,1,0:T(8,128)(2,1)}, bf16[192,1024]{1,0:T(8,128)(2,1)}) custom-call(s32[4,16]{1,0:T(4,128)} %bitcast.91, s32[1]{0:T(128)} %bitcast.2.me_ref, s32[1]{0:T(128)} %bitcast.head_ref, ...), custom_call_target="tpu_custom_call" | custom-call | tf_op jit(solution)/shard_map/pallas_call | solution.py:309
  61.9 2.8 %collective-permute-start.10 = (bf16[2,192,512]{2,1,0:T(8,128)(2,1)}, bf16[2,192,512]{2,1,0:T(8,128)(2,1)S(1)}, u32[]{:S(2)}, u32[]{:S(2)}) collective-permute-start(bf16[2,192,512]{2,1,0:T(8,128)(2,1)} %get-tuple-element.54), channel_id=1, source_target_pairs={{0,3},{1,2},{2,1},{3,0},{4,7},{5,6},{6,5},{7,4},{8,11},{9,10},{10,... | collective-permute-start | bytes 1179656 | tf_op jit(solution)/shard_map/ppermute | solution.py:494
  64.7 0.8 collective-permute-start.11
  66.0 3.6 %collective-permute-start.13 = (bf16[4,192,512]{2,1,0:T(8,128)(2,1)}, bf16[4,192,512]{2,1,0:T(8,128)(2,1)}, u32[]{:S(2)}, u32[]{:S(2)}) collective-permute-start(bf16[4,192,512]{2,1,0:T(8,128)(2,1)} %get-tuple-element.61), channel_id=1, source_target_pairs={{0,4},{1,5},{2,6},{3,7},{4,0},{5,1},{6,2},{7,3},{8,12},{9,13},{10,... | collective-permute-start | bytes 2359304 | tf_op jit(solution)/shard_map/ppermute | solution.py:494
  69.6 1.0 copy-done.2
  70.6 5.5 %shard_map.151 = bf16[6,192,512]{2,1,0:T(8,128)(2,1)S(1)} custom-call(s32[1]{0:T(128)} %bitcast.head_ref, bf16[192,1024]{1,0:T(8,128)(2,1)S(1)} %copy-done.2, bf16[1024,8192]{1,0:T(8,128)(2,1)} %w_ref.1), custom_call_target="tpu_custom_call" | custom-call | tf_op jit(solution)/shard_map/pallas_call | solution.py:359
  76.1 4.9 %collective-permute-done.10 = bf16[2,192,512]{2,1,0:T(8,128)(2,1)S(1)} collective-permute-done((bf16[2,192,512]{2,1,0:T(8,128)(2,1)}, bf16[2,192,512]{2,1,0:T(8,128)(2,1)S(1)}, u32[]{:S(2)}, u32[]{:S(2)}) %collective-permute-start.10) | collective-permute-done | bytes 393248 | tf_op jit(solution)/shard_map/ppermute | solution.py:494
  80.9 0.7 copy-done.7
  81.7 0.7 copy-done.8
  82.4 1.4 %add_convert_fusion.1 = bf16[2,192,512]{2,1,0:T(8,128)(2,1)S(1)} fusion(bf16[2,192,512]{2,1,0:T(8,128)(2,1)} %copy-done.8, bf16[2,192,512]{2,1,0:T(8,128)(2,1)} %copy-done.7, bf16[2,192,512]{2,1,0:T(8,128)(2,1)} %collective-permute-done.9, bf16[6,192,512]{2,1,0:T(8,128)(2,1)S(1)} %shard_map.151), kind=kLoop, calls=%fused_computation.3 | loop fusion | flops 1572864 | bytes 1966080 | tf_op jit(solution)/shard_map/convert_element_type | solution.py:505
  83.9 3.7 %collective-permute-start.12 = (bf16[2,192,512]{2,1,0:T(8,128)(2,1)S(1)}, bf16[2,192,512]{2,1,0:T(8,128)(2,1)S(1)}, u32[]{:S(2)}, u32[]{:S(2)}) collective-permute-start(bf16[2,192,512]{2,1,0:T(8,128)(2,1)S(1)} %add_convert_fusion.1), channel_id=1, source_target_pairs={{0,4},{1,5},{2,6},{3,7},{4,0},{5,1},{6,2},{7,3},{8,12},{9,13},{10,... | collective-permute-start | bytes 1179656 | tf_op jit(solution)/shard_map/ppermute | solution.py:494
  87.5 1.3 fusion.14
  88.8 0.8 collective-permute-start.14
  89.6 2.3 %collective-permute-start.15 = (bf16[96,512]{1,0:T(8,128)(2,1)S(1)}, bf16[96,512]{1,0:T(8,128)(2,1)S(1)}, u32[]{:S(2)}, u32[]{:S(2)}) collective-permute-start(bf16[96,512]{1,0:T(8,128)(2,1)S(1)} %get-tuple-element.81), channel_id=1, source_target_pairs={{0,3},{1,2},{2,1},{3,0},{4,7},{5,6},{6,5},{7,4},{8,11},{9,10},{10,... | collective-permute-start | bytes 294920 | tf_op jit(solution)/shard_map/ppermute | solution.py:494
  91.9 1.2 collective-permute-start.16
  93.7 1.7 %collective-permute-done.12 = bf16[2,192,512]{2,1,0:T(8,128)(2,1)S(1)} collective-permute-done((bf16[2,192,512]{2,1,0:T(8,128)(2,1)S(1)}, bf16[2,192,512]{2,1,0:T(8,128)(2,1)S(1)}, u32[]{:S(2)}, u32[]{:S(2)}) %collective-permute-start.12) | collective-permute-done | bytes 393248 | tf_op jit(solution)/shard_map/ppermute | solution.py:494
  95.4 3.6 %collective-permute-start.22 = (bf16[96,512]{1,0:T(8,128)(2,1)S(1)}, bf16[96,512]{1,0:T(8,128)(2,1)S(1)}, u32[]{:S(2)}, u32[]{:S(2)}) collective-permute-start(bf16[96,512]{1,0:T(8,128)(2,1)S(1)} %get-tuple-element.78), channel_id=1, source_target_pairs={{0,3},{1,2},{2,1},{3,0},{4,7},{5,6},{6,5},{7,4},{8,11},{9,10},{10,... | collective-permute-start | bytes 294920 | tf_op jit(solution)/shard_map/ppermute | solution.py:494
  99.0 0.8 add_convert_fusion.refs_0_
  99.9 3.5 %collective-permute-start.20 = (bf16[2,192,512]{2,1,0:T(8,128)(2,1)}, bf16[2,192,512]{2,1,0:T(8,128)(2,1)S(1)}, u32[]{:S(2)}, u32[]{:S(2)}) collective-permute-start(bf16[2,192,512]{2,1,0:T(8,128)(2,1)} %add_convert_fusion.refs_0_), channel_id=1, source_target_pairs={{0,2},{1,3},{2,0},{3,1},{4,6},{5,7},{6,4},{7,5},{8,10},{9,11},{10,... | collective-permute-start | bytes 1179656 | tf_op jit(solution)/shard_map/ppermute | solution.py:494
  103.4 1.0 fusion.5
  104.5 0.8 collective-permute-start.18
  105.3 7.7 %collective-permute-done.22 = bf16[96,512]{1,0:T(8,128)(2,1)S(1)} collective-permute-done((bf16[96,512]{1,0:T(8,128)(2,1)S(1)}, bf16[96,512]{1,0:T(8,128)(2,1)S(1)}, u32[]{:S(2)}, u32[]{:S(2)}) %collective-permute-start.22) | collective-permute-done | bytes 98336 | tf_op jit(solution)/shard_map/ppermute | solution.py:494
  113.0 4.2 %collective-permute-start.19 = (bf16[96,512]{1,0:T(8,128)(2,1)S(1)}, bf16[96,512]{1,0:T(8,128)(2,1)S(1)}, u32[]{:S(2)}, u32[]{:S(2)}) collective-permute-start(bf16[96,512]{1,0:T(8,128)(2,1)S(1)} %fusion.5), channel_id=1, source_target_pairs={{0,3},{1,2},{2,1},{3,0},{4,7},{5,6},{6,5},{7,4},{8,11},{9,10},{10,... | collective-permute-start | bytes 294920 | tf_op jit(solution)/shard_map/ppermute | solution.py:494
  117.2 1.0 fusion.2
  118.4 4.0 %collective-permute-start.26 = (bf16[96,512]{1,0:T(8,128)(2,1)S(1)}, bf16[96,512]{1,0:T(8,128)(2,1)S(1)}, u32[]{:S(2)}, u32[]{:S(2)}) collective-permute-start(bf16[96,512]{1,0:T(8,128)(2,1)S(1)} %fusion.2), channel_id=1, source_target_pairs={{0,2},{1,3},{2,0},{3,1},{4,6},{5,7},{6,4},{7,5},{8,10},{9,11},{10,... | collective-permute-start | bytes 294920 | tf_op jit(solution)/shard_map/ppermute | solution.py:494
  122.4 2.7 %collective-permute-start.27 = (bf16[4,96,512]{2,1,0:T(8,128)(2,1)S(1)}, bf16[4,96,512]{2,1,0:T(8,128)(2,1)S(1)}, u32[]{:S(2)}, u32[]{:S(2)}) collective-permute-start(bf16[4,96,512]{2,1,0:T(8,128)(2,1)S(1)} %pad_maximum_fusion.2.refs_2_), channel_id=1, source_target_pairs={{0,4},{1,5},{2,6},{3,7},{4,0},{5,1},{6,2},{7,3},{8,12},{9,13},{10,... | collective-permute-start | bytes 1179656 | tf_op jit(solution)/shard_map/ppermute | solution.py:494
  126.1 0.7 copy-done
  126.9 2.7 %collective-permute-start.28 = (bf16[4,96,512]{2,1,0:T(8,128)(2,1)S(1)}, bf16[4,96,512]{2,1,0:T(8,128)(2,1)}, u32[]{:S(2)}, u32[]{:S(2)}) collective-permute-start(bf16[4,96,512]{2,1,0:T(8,128)(2,1)S(1)} %pad_maximum_fusion.3.refs_3_), channel_id=1, source_target_pairs={{0,4},{1,5},{2,6},{3,7},{4,0},{5,1},{6,2},{7,3},{8,12},{9,13},{10,... | collective-permute-start | bytes 1179656 | tf_op jit(solution)/shard_map/ppermute | solution.py:494
  129.6 4.7 %shard_map.152 = (bf16[4,1024,128]{2,1,0:T(8,128)(2,1)}, bf16[4,1024,128]{2,1,0:T(8,128)(2,1)}) custom-call(s32[1]{0:T(128)} %bitcast.39.first_ref, s32[16,64]{1,0:T(8,128)S(1)} %bitcast.67, s32[16,64]{1,0:T(8,128)S(1)} %bitcast.66, bf16[16,4,64,256]{3,2,1,0:T(8,128)(2,1)S(1)} %all-to-all-done.source), custom_call_target="tpu_custom_call" | custom-call | tf_op jit(solution)/shard_map/pallas_call | solution.py:466
  134.3 2.8 %shard_map.153.earlier = bf16[192,8192]{1,0:T(8,128)(2,1)} custom-call(s32[1]{0:T(128)} %bitcast.head_ref, bf16[2,192,512]{2,1,0:T(8,128)(2,1)} %add_convert_fusion.refs_0_, bf16[2,192,512]{2,1,0:T(8,128)(2,1)S(1)} %copy-done.1, bf16[4,96,512]{2,1,0:T(8,128)(2,1)S(1)} %pad_maximum_fusion.2.refs_2_, bf16[4,96,512]{2,1,0:T(8,128)(2,1)S(1)} %pad_maximum_fusion.3.refs_3_), custom_call_target="tpu_custom_call" | custom-call | tf_op jit(solution)/shard_map/pallas_call | solution.py:396
  137.1 1.6 %collective-permute-done.28.refs_1_ = bf16[4,96,512]{2,1,0:T(8,128)(2,1)} collective-permute-done((bf16[4,96,512]{2,1,0:T(8,128)(2,1)S(1)}, bf16[4,96,512]{2,1,0:T(8,128)(2,1)}, u32[]{:S(2)}, u32[]{:S(2)}) %collective-permute-start.28) | collective-permute-done | bytes 393248 | tf_op jit(solution)/shard_map/ppermute | solution.py:494
  138.7 2.5 %shard_map.154 = bf16[192,8192]{1,0:T(8,128)(2,1)} custom-call(s32[1]{0:T(128)} %bitcast.head_ref, bf16[192,8192]{1,0:T(8,128)(2,1)} %shard_map.153.earlier, bf16[4,96,512]{2,1,0:T(8,128)(2,1)S(1)} %collective-permute-done.27.refs_0_, bf16[4,96,512]{2,1,0:T(8,128)(2,1)} %collective-permute-done.28.refs_1_, ...), custom_call_target="tpu_custom_call", output_to_operand_aliasing={{}: (1, {})} | custom-call | tf_op jit(solution)/shard_map/pallas_call | solution.py:425
  (55 shorter events, 3.9 us)
Async XLA Ops:
  2.4 11.0 %collective-permute-start.3 = (bf16[1024,128]{1,0:T(8,128)(2,1)}, bf16[1024,128]{1,0:T(8,128)(2,1)S(1)}, u32[]{:S(2)}, u32[]{:S(2)}) collective-permute-start(bf16[1024,128]{1,0:T(8,128)(2,1)} %shard_map.149), channel_id=1, source_target_pairs={{0,32},{8,40},{16,48},{24,56},{32,0},{40,8},{48,16},{56,24},{64,96... | collective-permute-start | bytes 786440 | tf_op jit(solution)/shard_map/ppermute | solution.py:486
  4.7 10.6 %collective-permute-start = (bf16[1024,128]{1,0:T(8,128)(2,1)}, bf16[1024,128]{1,0:T(8,128)(2,1)S(1)}, u32[]{:S(2)}, u32[]{:S(2)}) collective-permute-start(bf16[1024,128]{1,0:T(8,128)(2,1)} %shard_map.149), channel_id=1, source_target_pairs={{0,64},{8,72},{16,80},{24,88},{32,96},{40,104},{48,112},{56,120},{... | collective-permute-start | bytes 786440 | tf_op jit(solution)/shard_map/ppermute | solution.py:486
  6.6 18.0 %collective-permute-start.1 = (bf16[1024,128]{1,0:T(8,128)(2,1)}, bf16[1024,128]{1,0:T(8,128)(2,1)S(1)}, u32[]{:S(2)}, u32[]{:S(2)}) collective-permute-start(bf16[1024,128]{1,0:T(8,128)(2,1)} %shard_map.149), channel_id=1, source_target_pairs={{0,16},{8,24},{16,32},{24,40},{32,48},{40,56},{48,0},{56,8},{64,80... | collective-permute-start | bytes 786440 | tf_op jit(solution)/shard_map/ppermute | solution.py:486
  6.6 18.0 %collective-permute-start.2 = (bf16[1024,128]{1,0:T(8,128)(2,1)}, bf16[1024,128]{1,0:T(8,128)(2,1)S(1)}, u32[]{:S(2)}, u32[]{:S(2)}) collective-permute-start(bf16[1024,128]{1,0:T(8,128)(2,1)} %shard_map.149), channel_id=1, source_target_pairs={{0,48},{8,56},{16,0},{24,8},{32,16},{40,24},{48,32},{56,40},{64,11... | collective-permute-start | bytes 786440 | tf_op jit(solution)/shard_map/ppermute | solution.py:486
  13.3 11.3 %collective-permute-start.6 = (bf16[1024,128]{1,0:T(8,128)(2,1)S(1)}, bf16[1024,128]{1,0:T(8,128)(2,1)S(1)}, u32[]{:S(2)}, u32[]{:S(2)}) collective-permute-start(bf16[1024,128]{1,0:T(8,128)(2,1)S(1)} %collective-permute-done.3), channel_id=1, source_target_pairs={{0,64},{8,72},{16,80},{24,88},{32,96},{40,104},{48,112},{56,120},{... | collective-permute-start | bytes 786440 | tf_op jit(solution)/shard_map/ppermute | solution.py:486
  15.3 9.4 %collective-permute-start.4 = (bf16[1024,128]{1,0:T(8,128)(2,1)S(1)}, bf16[1024,128]{1,0:T(8,128)(2,1)S(1)}, u32[]{:S(2)}, u32[]{:S(2)}) collective-permute-start(bf16[1024,128]{1,0:T(8,128)(2,1)S(1)} %collective-permute-done), channel_id=1, source_target_pairs={{0,16},{8,24},{16,32},{24,40},{32,48},{40,56},{48,0},{56,8},{64,80... | collective-permute-start | bytes 786440 | tf_op jit(solution)/shard_map/ppermute | solution.py:486
  16.8 7.8 %collective-permute-start.5 = (bf16[1024,128]{1,0:T(8,128)(2,1)S(1)}, bf16[1024,128]{1,0:T(8,128)(2,1)S(1)}, u32[]{:S(2)}, u32[]{:S(2)}) collective-permute-start(bf16[1024,128]{1,0:T(8,128)(2,1)S(1)} %collective-permute-done), channel_id=1, source_target_pairs={{0,48},{8,56},{16,0},{24,8},{32,16},{40,24},{48,32},{56,40},{64,11... | collective-permute-start | bytes 786440 | tf_op jit(solution)/shard_map/ppermute | solution.py:486
  24.6 0.9 copy-start.6
  24.8 7.0 %copy-start.5 = (bf16[4,1024,128]{2,1,0:T(8,128)(2,1)}, bf16[4,1024,128]{2,1,0:T(8,128)(2,1)S(1)}, u32[]{:S(2)}) copy-start(bf16[4,1024,128]{2,1,0:T(8,128)(2,1)S(1)} %pad_maximum_fusion.1.refs_2_) | copy-start | bytes 3145732
  26.6 55.8 %all-to-all-start = ((bf16[16,4,64,256]{3,2,1,0:T(8,128)(2,1)}), bf16[16,4,64,256]{3,2,1,0:T(8,128)(2,1)S(1)}, u32[]{:S(2)}, u32[]{:S(2)}) async-start(bf16[16,4,64,256]{3,2,1,0:T(8,128)(2,1)} %bitcast.69), calls=%async_computation | async-start | bytes 4194304 | tf_op jit(solution)/shard_map/all_to_all | solution.py:551
  31.8 2.9 %collective-permute-start.8 = (bf16[4,1024,128]{2,1,0:T(8,128)(2,1)S(1)}, bf16[4,1024,128]{2,1,0:T(8,128)(2,1)}, u32[]{:S(2)}, u32[]{:S(2)}) collective-permute-start(bf16[4,1024,128]{2,1,0:T(8,128)(2,1)S(1)} %pad_maximum_fusion.1.refs_2_), channel_id=1, source_target_pairs={{0,8},{8,0},{16,24},{24,16},{32,40},{40,32},{48,56},{56,48},{64,72... | collective-permute-start | bytes 3145736 | tf_op jit(solution)/shard_map/ppermute | solution.py:490
  32.1 4.4 %collective-permute-start.7 = (bf16[4,1024,128]{2,1,0:T(8,128)(2,1)}, bf16[4,1024,128]{2,1,0:T(8,128)(2,1)}, u32[]{:S(2)}, u32[]{:S(2)}) collective-permute-start(bf16[4,1024,128]{2,1,0:T(8,128)(2,1)} %pad_maximum_fusion.refs_0_), channel_id=1, source_target_pairs={{0,8},{8,0},{16,24},{24,16},{32,40},{40,32},{48,56},{56,48},{64,72... | collective-permute-start | bytes 3145736 | tf_op jit(solution)/shard_map/ppermute | solution.py:490
  61.9 19.1 %collective-permute-start.10 = (bf16[2,192,512]{2,1,0:T(8,128)(2,1)}, bf16[2,192,512]{2,1,0:T(8,128)(2,1)S(1)}, u32[]{:S(2)}, u32[]{:S(2)}) collective-permute-start(bf16[2,192,512]{2,1,0:T(8,128)(2,1)} %get-tuple-element.54), channel_id=1, source_target_pairs={{0,3},{1,2},{2,1},{3,0},{4,7},{5,6},{6,5},{7,4},{8,11},{9,10},{10,... | collective-permute-start | bytes 1179656 | tf_op jit(solution)/shard_map/ppermute | solution.py:494
  64.7 16.2 %collective-permute-start.11 = (bf16[2,192,512]{2,1,0:T(8,128)(2,1)}, bf16[2,192,512]{2,1,0:T(8,128)(2,1)S(1)}, u32[]{:S(2)}, u32[]{:S(2)}) collective-permute-start(bf16[2,192,512]{2,1,0:T(8,128)(2,1)} %get-tuple-element.55), channel_id=1, source_target_pairs={{0,2},{1,3},{2,0},{3,1},{4,6},{5,7},{6,4},{7,5},{8,10},{9,11},{10,... | collective-permute-start | bytes 1179656 | tf_op jit(solution)/shard_map/ppermute | solution.py:494
  65.5 16.9 %collective-permute-start.9 = (bf16[2,192,512]{2,1,0:T(8,128)(2,1)}, bf16[2,192,512]{2,1,0:T(8,128)(2,1)}, u32[]{:S(2)}, u32[]{:S(2)}) collective-permute-start(bf16[2,192,512]{2,1,0:T(8,128)(2,1)} %get-tuple-element.53), channel_id=1, source_target_pairs={{0,1},{1,0},{2,3},{3,2},{4,5},{5,4},{6,7},{7,6},{8,9},{9,8},{10,11... | collective-permute-start | bytes 1179656 | tf_op jit(solution)/shard_map/ppermute | solution.py:494
  66.0 21.5 %collective-permute-start.13 = (bf16[4,192,512]{2,1,0:T(8,128)(2,1)}, bf16[4,192,512]{2,1,0:T(8,128)(2,1)}, u32[]{:S(2)}, u32[]{:S(2)}) collective-permute-start(bf16[4,192,512]{2,1,0:T(8,128)(2,1)} %get-tuple-element.61), channel_id=1, source_target_pairs={{0,4},{1,5},{2,6},{3,7},{4,0},{5,1},{6,2},{7,3},{8,12},{9,13},{10,... | collective-permute-start | bytes 2359304 | tf_op jit(solution)/shard_map/ppermute | solution.py:494
  69.6 1.0 copy-start.2
  80.9 0.7 copy-start.7
  81.7 0.7 copy-start.8
  83.9 11.6 %collective-permute-start.12 = (bf16[2,192,512]{2,1,0:T(8,128)(2,1)S(1)}, bf16[2,192,512]{2,1,0:T(8,128)(2,1)S(1)}, u32[]{:S(2)}, u32[]{:S(2)}) collective-permute-start(bf16[2,192,512]{2,1,0:T(8,128)(2,1)S(1)} %add_convert_fusion.1), channel_id=1, source_target_pairs={{0,4},{1,5},{2,6},{3,7},{4,0},{5,1},{6,2},{7,3},{8,12},{9,13},{10,... | collective-permute-start | bytes 1179656 | tf_op jit(solution)/shard_map/ppermute | solution.py:494
  88.8 11.0 %collective-permute-start.14 = (bf16[96,512]{1,0:T(8,128)(2,1)S(1)}, bf16[96,512]{1,0:T(8,128)(2,1)S(1)}, u32[]{:S(2)}, u32[]{:S(2)}) collective-permute-start(bf16[96,512]{1,0:T(8,128)(2,1)S(1)} %get-tuple-element.82), channel_id=1, source_target_pairs={{0,1},{1,0},{2,3},{3,2},{4,5},{5,4},{6,7},{7,6},{8,9},{9,8},{10,11... | collective-permute-start | bytes 294920 | tf_op jit(solution)/shard_map/ppermute | solution.py:494
  89.6 10.2 %collective-permute-start.15 = (bf16[96,512]{1,0:T(8,128)(2,1)S(1)}, bf16[96,512]{1,0:T(8,128)(2,1)S(1)}, u32[]{:S(2)}, u32[]{:S(2)}) collective-permute-start(bf16[96,512]{1,0:T(8,128)(2,1)S(1)} %get-tuple-element.81), channel_id=1, source_target_pairs={{0,3},{1,2},{2,1},{3,0},{4,7},{5,6},{6,5},{7,4},{8,11},{9,10},{10,... | collective-permute-start | bytes 294920 | tf_op jit(solution)/shard_map/ppermute | solution.py:494
  91.9 11.5 %collective-permute-start.16 = (bf16[96,512]{1,0:T(8,128)(2,1)S(1)}, bf16[96,512]{1,0:T(8,128)(2,1)S(1)}, u32[]{:S(2)}, u32[]{:S(2)}) collective-permute-start(bf16[96,512]{1,0:T(8,128)(2,1)S(1)} %get-tuple-element.80), channel_id=1, source_target_pairs={{0,2},{1,3},{2,0},{3,1},{4,6},{5,7},{6,4},{7,5},{8,10},{9,11},{10,... | collective-permute-start | bytes 294920 | tf_op jit(solution)/shard_map/ppermute | solution.py:494
  93.1 11.4 %collective-permute-start.21 = (bf16[96,512]{1,0:T(8,128)(2,1)S(1)}, bf16[96,512]{1,0:T(8,128)(2,1)S(1)}, u32[]{:S(2)}, u32[]{:S(2)}) collective-permute-start(bf16[96,512]{1,0:T(8,128)(2,1)S(1)} %get-tuple-element.79), channel_id=1, source_target_pairs={{0,1},{1,0},{2,3},{3,2},{4,5},{5,4},{6,7},{7,6},{8,9},{9,8},{10,11... | collective-permute-start | bytes 294920 | tf_op jit(solution)/shard_map/ppermute | solution.py:494
  95.4 17.6 %collective-permute-start.22 = (bf16[96,512]{1,0:T(8,128)(2,1)S(1)}, bf16[96,512]{1,0:T(8,128)(2,1)S(1)}, u32[]{:S(2)}, u32[]{:S(2)}) collective-permute-start(bf16[96,512]{1,0:T(8,128)(2,1)S(1)} %get-tuple-element.78), channel_id=1, source_target_pairs={{0,3},{1,2},{2,1},{3,0},{4,7},{5,6},{6,5},{7,4},{8,11},{9,10},{10,... | collective-permute-start | bytes 294920 | tf_op jit(solution)/shard_map/ppermute | solution.py:494
  99.8 29.7 %copy-start.3 = (s32[64,16]{0,1:T(8,128)S(1)}, s32[64,16]{0,1:T(8,128)}, u32[]{:S(2)}) copy-start(s32[64,16]{0,1:T(8,128)} %param.20) | copy-start | bytes 12292
  99.8 29.7 %copy-start.4 = (s32[64,16]{0,1:T(8,128)S(1)}, s32[64,16]{0,1:T(8,128)}, u32[]{:S(2)}) copy-start(s32[64,16]{0,1:T(8,128)} %param.21) | copy-start | bytes 12292
  99.9 17.4 %collective-permute-start.23 = (bf16[96,512]{1,0:T(8,128)(2,1)S(1)}, bf16[96,512]{1,0:T(8,128)(2,1)S(1)}, u32[]{:S(2)}, u32[]{:S(2)}) collective-permute-start(bf16[96,512]{1,0:T(8,128)(2,1)S(1)} %get-tuple-element.77), channel_id=1, source_target_pairs={{0,2},{1,3},{2,0},{3,1},{4,6},{5,7},{6,4},{7,5},{8,10},{9,11},{10,... | collective-permute-start | bytes 294920 | tf_op jit(solution)/shard_map/ppermute | solution.py:494
  99.9 26.2 %collective-permute-start.20 = (bf16[2,192,512]{2,1,0:T(8,128)(2,1)}, bf16[2,192,512]{2,1,0:T(8,128)(2,1)S(1)}, u32[]{:S(2)}, u32[]{:S(2)}) collective-permute-start(bf16[2,192,512]{2,1,0:T(8,128)(2,1)} %add_convert_fusion.refs_0_), channel_id=1, source_target_pairs={{0,2},{1,3},{2,0},{3,1},{4,6},{5,7},{6,4},{7,5},{8,10},{9,11},{10,... | collective-permute-start | bytes 1179656 | tf_op jit(solution)/shard_map/ppermute | solution.py:494
  104.4 13.9 %collective-permute-start.17 = (bf16[96,512]{1,0:T(8,128)(2,1)S(1)}, bf16[96,512]{1,0:T(8,128)(2,1)S(1)}, u32[]{:S(2)}, u32[]{:S(2)}) collective-permute-start(bf16[96,512]{1,0:T(8,128)(2,1)S(1)} %fusion.5), channel_id=1, source_target_pairs={{0,2},{1,3},{2,0},{3,1},{4,6},{5,7},{6,4},{7,5},{8,10},{9,11},{10,... | collective-permute-start | bytes 294920 | tf_op jit(solution)/shard_map/ppermute | solution.py:494
  104.5 13.9 %collective-permute-start.18 = (bf16[96,512]{1,0:T(8,128)(2,1)S(1)}, bf16[96,512]{1,0:T(8,128)(2,1)S(1)}, u32[]{:S(2)}, u32[]{:S(2)}) collective-permute-start(bf16[96,512]{1,0:T(8,128)(2,1)S(1)} %fusion.5), channel_id=1, source_target_pairs={{0,1},{1,0},{2,3},{3,2},{4,5},{5,4},{6,7},{7,6},{8,9},{9,8},{10,11... | collective-permute-start | bytes 294920 | tf_op jit(solution)/shard_map/ppermute | solution.py:494
  113.0 9.3 %collective-permute-start.19 = (bf16[96,512]{1,0:T(8,128)(2,1)S(1)}, bf16[96,512]{1,0:T(8,128)(2,1)S(1)}, u32[]{:S(2)}, u32[]{:S(2)}) collective-permute-start(bf16[96,512]{1,0:T(8,128)(2,1)S(1)} %fusion.5), channel_id=1, source_target_pairs={{0,3},{1,2},{2,1},{3,0},{4,7},{5,6},{6,5},{7,4},{8,11},{9,10},{10,... | collective-permute-start | bytes 294920 | tf_op jit(solution)/shard_map/ppermute | solution.py:494
  118.2 6.9 %collective-permute-start.24 = (bf16[96,512]{1,0:T(8,128)(2,1)S(1)}, bf16[96,512]{1,0:T(8,128)(2,1)S(1)}, u32[]{:S(2)}, u32[]{:S(2)}) collective-permute-start(bf16[96,512]{1,0:T(8,128)(2,1)S(1)} %fusion.2), channel_id=1, source_target_pairs={{0,1},{1,0},{2,3},{3,2},{4,5},{5,4},{6,7},{7,6},{8,9},{9,8},{10,11... | collective-permute-start | bytes 294920 | tf_op jit(solution)/shard_map/ppermute | solution.py:494
  118.3 7.6 %collective-permute-start.25 = (bf16[96,512]{1,0:T(8,128)(2,1)S(1)}, bf16[96,512]{1,0:T(8,128)(2,1)S(1)}, u32[]{:S(2)}, u32[]{:S(2)}) collective-permute-start(bf16[96,512]{1,0:T(8,128)(2,1)S(1)} %fusion.2), channel_id=1, source_target_pairs={{0,3},{1,2},{2,1},{3,0},{4,7},{5,6},{6,5},{7,4},{8,11},{9,10},{10,... | collective-permute-start | bytes 294920 | tf_op jit(solution)/shard_map/ppermute | solution.py:494
  118.4 7.7 %collective-permute-start.26 = (bf16[96,512]{1,0:T(8,128)(2,1)S(1)}, bf16[96,512]{1,0:T(8,128)(2,1)S(1)}, u32[]{:S(2)}, u32[]{:S(2)}) collective-permute-start(bf16[96,512]{1,0:T(8,128)(2,1)S(1)} %fusion.2), channel_id=1, source_target_pairs={{0,2},{1,3},{2,0},{3,1},{4,6},{5,7},{6,4},{7,5},{8,10},{9,11},{10,... | collective-permute-start | bytes 294920 | tf_op jit(solution)/shard_map/ppermute | solution.py:494
  122.4 14.6 %collective-permute-start.27 = (bf16[4,96,512]{2,1,0:T(8,128)(2,1)S(1)}, bf16[4,96,512]{2,1,0:T(8,128)(2,1)S(1)}, u32[]{:S(2)}, u32[]{:S(2)}) collective-permute-start(bf16[4,96,512]{2,1,0:T(8,128)(2,1)S(1)} %pad_maximum_fusion.2.refs_2_), channel_id=1, source_target_pairs={{0,4},{1,5},{2,6},{3,7},{4,0},{5,1},{6,2},{7,3},{8,12},{9,13},{10,... | collective-permute-start | bytes 1179656 | tf_op jit(solution)/shard_map/ppermute | solution.py:494
  125.1 11.9 %collective-permute-start.29 = (bf16[2,192,512]{2,1,0:T(8,128)(2,1)}, bf16[2,192,512]{2,1,0:T(8,128)(2,1)}, u32[]{:S(2)}, u32[]{:S(2)}) collective-permute-start(bf16[2,192,512]{2,1,0:T(8,128)(2,1)} %add_convert_fusion.refs_0_), channel_id=1, source_target_pairs={{0,1},{1,0},{2,3},{3,2},{4,5},{5,4},{6,7},{7,6},{8,9},{9,8},{10,11... | collective-permute-start | bytes 1179656 | tf_op jit(solution)/shard_map/ppermute | solution.py:494
  125.8 11.2 %collective-permute-start.30 = (bf16[2,192,512]{2,1,0:T(8,128)(2,1)}, bf16[2,192,512]{2,1,0:T(8,128)(2,1)}, u32[]{:S(2)}, u32[]{:S(2)}) collective-permute-start(bf16[2,192,512]{2,1,0:T(8,128)(2,1)} %add_convert_fusion.refs_0_), channel_id=1, source_target_pairs={{0,3},{1,2},{2,1},{3,0},{4,7},{5,6},{6,5},{7,4},{8,11},{9,10},{10,... | collective-permute-start | bytes 1179656 | tf_op jit(solution)/shard_map/ppermute | solution.py:494
  126.1 0.7 copy-start
  126.9 11.8 %collective-permute-start.28 = (bf16[4,96,512]{2,1,0:T(8,128)(2,1)S(1)}, bf16[4,96,512]{2,1,0:T(8,128)(2,1)}, u32[]{:S(2)}, u32[]{:S(2)}) collective-permute-start(bf16[4,96,512]{2,1,0:T(8,128)(2,1)S(1)} %pad_maximum_fusion.3.refs_3_), channel_id=1, source_target_pairs={{0,4},{1,5},{2,6},{3,7},{4,0},{5,1},{6,2},{7,3},{8,12},{9,13},{10,... | collective-permute-start | bytes 1179656 | tf_op jit(solution)/shard_map/ppermute | solution.py:494
  129.6 4.7 %copy-start.1 = (bf16[2,192,512]{2,1,0:T(8,128)(2,1)S(1)}, bf16[2,192,512]{2,1,0:T(8,128)(2,1)}, u32[]{:S(2)}) copy-start(bf16[2,192,512]{2,1,0:T(8,128)(2,1)} %copy-done) | copy-start | bytes 1179652

commit v3 on v1

--- a/solution.py
+++ b/solution.py
@@ -531,11 +531,14 @@
     shift = lax.dynamic_slice_in_dim(offsets, me, 1, 0) - prompt_len
     steps = jnp.arange(STEPS, dtype=jnp.int32)[:, None]
     cosine, sine = tables(jnp.concatenate([prompt_len + live + steps, shift]))
+    near = after(near, cosine)
+    near_stack = jnp.stack(near)
+    near_other = swap_core(near_stack)
     far.append(move_chip(after(far[0], cosine), 1, 0))
     query, top, accum, sent = span_part(
         lengths,
         one,
-        jnp.transpose(queries[0], (1, 0, 2)),
+        after(jnp.transpose(queries[0], (1, 0, 2)), near_stack),
         cosine,
         sine,
         jnp.transpose(new_keys[0], (1, 0, 2)),
@@ -544,10 +547,9 @@
         span_values[0],
     )
 
-    near, far = after((near, far), query)
-    near_stack, far_stack = jnp.stack(near), jnp.stack(far)
-    near_other, far_other = swap_core(near_stack), swap_core(far_stack)
-    sent = after(sent, near_stack, far_stack).reshape(BRANCHES, share, SPAN, 2 * HD)
+    far_stack = jnp.stack(after(far, query))
+    far_other = swap_core(far_stack)
+    sent = after(sent, far_stack).reshape(BRANCHES, share, SPAN, 2 * HD)
     gathered = lax.all_to_all(sent, "branch", 0, 0, tiled=True)
     places = [(dz, dy, c) for at in (near_at, far_at) for c in (0, 1) for dz, dy in at]
     stacks = [near_stack, near_other, far_stack, far_other]

time: 134 us -> 140 us (1.045)
  waiting for transfers between devices: 25.2 us -> 30.1 us
    ppermute x7, waiting for transfers between devices: 1.41 us -> 7.99 us  [move_chip(): return lax.ppermute(value, 'branch', perm)]
    ppermute x22, starting transfers between devices: 32.1 us -> 34 us  [move_x(): return lax.ppermute(value, 'head', [(h, h ^ flip) for h in range(KVH)])]
    ppermute x22, waiting for transfers between devices: 23.8 us -> 22.1 us  [move_x(): return lax.ppermute(value, 'head', [(h, h ^ flip) for h in range(KVH)])]
    ppermute x7, starting transfers between devices: 10.2 us -> 8.55 us  [move_chip(): return lax.ppermute(value, 'branch', perm)]
  transfers between devices with their start and end apart: 32 -> 32, of which waited for: 11 -> 10; matrix products, arithmetic and copies ran while one was open for 7% -> 7% of each run, Pallas kernels for 33% -> 31%
where the time goes in v3:
time: 140 us; the launch traced here: 139 us
  starting transfers between devices  48.7 us (35%)
  Pallas kernels  47.8 us (34%)
  waiting for transfers between devices  30.1 us (22%)
  other arithmetic  10.3 us (7%)
    ppermute x22, starting transfers between devices, move_x(): return lax.ppermute(value, 'head', [(h, h ^ flip) for h in range(KVH)])  34 us
    pallas_call x1, Pallas kernels, prompt_part(): pl.pallas_call(functools.partial(prompt_kernel, places, groups, len(stack...  23.9 us
    ppermute x22, waiting for transfers between devices, move_x(): return lax.ppermute(value, 'head', [(h, h ^ flip) for h in range(KVH)])  22.1 us
    ppermute x7, starting transfers between devices, move_chip(): return lax.ppermute(value, 'branch', perm)  8.55 us
    ppermute x7, waiting for transfers between devices, move_chip(): return lax.ppermute(value, 'branch', perm)  7.99 us
    pallas_call x1, Pallas kernels, span_part(): pl.pallas_call(span_kernel, grid_spec=pltpu.PrefetchScalarGridSpec(num_sc...  7.32 us
    all_to_all x1, starting transfers between devices, shards(): gathered = lax.all_to_all(sent, 'branch', 0, 0, tiled=True)  5.61 us
    pallas_call x1, Pallas kernels, project(): pl.pallas_call(functools.partial(project_kernel, places), grid_spec=pltpu...  5.47 us
  transfers between devices with their start and end apart: 32, of which 10 were waited for; matrix products, arithmetic and copies ran while one was open for 7% of the time, Pallas kernels for 31%

profile of v3, /device:TPU:8, one launch (start us, length us, event | category | flops | bytes accessed | tf_op | source)
XLA Modules:
  0.0 138.9 jit_solution(2209354300547071490)
XLA Ops:
  0.6 1.8 %shard_map.148 = bf16[1024,128]{1,0:T(8,128)(2,1)} custom-call(bf16[512,128]{1,0:T(8,128)(2,1)} %keys_ref.1, bf16[512,128]{1,0:T(8,128)(2,1)} %vals_ref.1), custom_call_target="tpu_custom_call" | custom-call | tf_op jit(solution)/shard_map/pallas_call | solution.py:156
  2.4 1.9 %collective-permute-start = (bf16[1024,128]{1,0:T(8,128)(2,1)}, bf16[1024,128]{1,0:T(8,128)(2,1)S(1)}, u32[]{:S(2)}, u32[]{:S(2)}) collective-permute-start(bf16[1024,128]{1,0:T(8,128)(2,1)} %shard_map.148), channel_id=1, source_target_pairs={{0,64},{8,72},{16,80},{24,88},{32,96},{40,104},{48,112},{56,120},{... | collective-permute-start | bytes 786440 | tf_op jit(solution)/shard_map/ppermute | solution.py:486
  4.3 1.6 %collective-permute-start.1 = (bf16[1024,128]{1,0:T(8,128)(2,1)}, bf16[1024,128]{1,0:T(8,128)(2,1)S(1)}, u32[]{:S(2)}, u32[]{:S(2)}) collective-permute-start(bf16[1024,128]{1,0:T(8,128)(2,1)} %shard_map.148), channel_id=1, source_target_pairs={{0,16},{8,24},{16,32},{24,40},{32,48},{40,56},{48,0},{56,8},{64,80... | collective-permute-start | bytes 786440 | tf_op jit(solution)/shard_map/ppermute | solution.py:486
  6.3 2.3 %collective-permute-start.4 = (bf16[1024,128]{1,0:T(8,128)(2,1)}, bf16[1024,128]{1,0:T(8,128)(2,1)S(1)}, u32[]{:S(2)}, u32[]{:S(2)}) collective-permute-start(bf16[1024,128]{1,0:T(8,128)(2,1)} %shard_map.148), channel_id=1, source_target_pairs={{0,32},{8,40},{16,48},{24,56},{32,0},{40,8},{48,16},{56,24},{64,96... | collective-permute-start | bytes 786440 | tf_op jit(solution)/shard_map/ppermute | solution.py:486
  8.6 0.7 add_bitcast_fusion.1
  9.3 0.7 add_bitcast_fusion
  10.0 1.9 %fusion.3 = (f32[4,64,128]{2,1,0:T(8,128)}, f32[4,64,128]{2,1,0:T(8,128)}) fusion(f32[128]{0:T(128)} %constant.24.clone, f32[128]{0:T(128)} %constant.23.clone, f32[4,64]{1,0:T(4,128)S(1)} %add_convert_fusion.11), kind=kLoop, calls=%fused_computation.21 | loop fusion | flops 65536 | bytes 264192 | tf_op jit(solution)/shard_map/mul | solution.py:46
  11.9 8.0 %collective-permute-done.4 = bf16[1024,128]{1,0:T(8,128)(2,1)S(1)} collective-permute-done((bf16[1024,128]{1,0:T(8,128)(2,1)}, bf16[1024,128]{1,0:T(8,128)(2,1)S(1)}, u32[]{:S(2)}, u32[]{:S(2)}) %collective-permute-start.4) | collective-permute-done | bytes 262176 | tf_op jit(solution)/shard_map/ppermute | solution.py:486
  20.2 2.0 %collective-permute-start.6 = (bf16[1024,128]{1,0:T(8,128)(2,1)S(1)}, bf16[1024,128]{1,0:T(8,128)(2,1)S(1)}, u32[]{:S(2)}, u32[]{:S(2)}) collective-permute-start(bf16[1024,128]{1,0:T(8,128)(2,1)S(1)} %collective-permute-done), channel_id=1, source_target_pairs={{0,48},{8,56},{16,0},{24,8},{32,16},{40,24},{48,32},{56,40},{64,11... | collective-permute-start | bytes 786440 | tf_op jit(solution)/shard_map/ppermute | solution.py:486
  22.2 1.1 pad_maximum_fusion.refs_0_
  23.4 7.3 %shard_map.149 = (bf16[3,64,1024]{2,1,0:T(8,128)(2,1)}, f32[4,384,128]{2,1,0:T(8,128)}, f32[4,384,256]{2,1,0:T(8,128)}, bf16[64,64,256]{2,1,0:T(8,128)(2,1)}) custom-call(s32[16,64]{1,0:T(8,128)} %bitcast.62, s32[1]{0:T(128)} %bitcast.2.me_ref, bf16[3,64,1024]{2,1,0:T(8,128)(2,1)} %bitcast.70, f32[4,64,128]{2,1,0:T(8,128)} %get-tuple-element.83.cos_ref, ...), custom_call_target="tpu_custom_call" | custom-call | tf_op jit(solution)/shard_map/pallas_call | solution.py:128
  30.8 1.1 pad_maximum_fusion.1.refs_2_
  32.4 5.6 %all-to-all-start = ((bf16[16,4,64,256]{3,2,1,0:T(8,128)(2,1)}), bf16[16,4,64,256]{3,2,1,0:T(8,128)(2,1)S(1)}, u32[]{:S(2)}, u32[]{:S(2)}) async-start(bf16[16,4,64,256]{3,2,1,0:T(8,128)(2,1)} %bitcast.66), calls=%async_computation | async-start | bytes 4194304 | tf_op jit(solution)/shard_map/all_to_all | solution.py:553
  38.0 23.9 %shard_map.150 = (bf16[4,192,512]{2,1,0:T(8,128)(2,1)}, bf16[2,192,512]{2,1,0:T(8,128)(2,1)}, bf16[2,192,512]{2,1,0:T(8,128)(2,1)}, bf16[2,192,512]{2,1,0:T(8,128)(2,1)}, bf16[192,1024]{1,0:T(8,128)(2,1)}) custom-call(s32[4,16]{1,0:T(4,128)} %bitcast.88, s32[1]{0:T(128)} %bitcast.2.me_ref, s32[1]{0:T(128)} %bitcast.head_ref, ...), custom_call_target="tpu_custom_call" | custom-call | tf_op jit(solution)/shard_map/pallas_call | solution.py:309
  61.9 3.8 %collective-permute-start.12 = (bf16[4,192,512]{2,1,0:T(8,128)(2,1)}, bf16[4,192,512]{2,1,0:T(8,128)(2,1)S(1)}, u32[]{:S(2)}, u32[]{:S(2)}) collective-permute-start(bf16[4,192,512]{2,1,0:T(8,128)(2,1)} %get-tuple-element.56), channel_id=1, source_target_pairs={{0,4},{1,5},{2,6},{3,7},{4,0},{5,1},{6,2},{7,3},{8,12},{9,13},{10,... | collective-permute-start | bytes 2359304 | tf_op jit(solution)/shard_map/ppermute | solution.py:494
  65.8 2.7 %collective-permute-start.10 = (bf16[2,192,512]{2,1,0:T(8,128)(2,1)}, bf16[2,192,512]{2,1,0:T(8,128)(2,1)S(1)}, u32[]{:S(2)}, u32[]{:S(2)}) collective-permute-start(bf16[2,192,512]{2,1,0:T(8,128)(2,1)} %get-tuple-element.54), channel_id=1, source_target_pairs={{0,3},{1,2},{2,1},{3,0},{4,7},{5,6},{6,5},{7,4},{8,11},{9,10},{10,... | collective-permute-start | bytes 1179656 | tf_op jit(solution)/shard_map/ppermute | solution.py:494
  68.5 0.8 collective-permute-start.11
  69.9 1.0 copy-done
  70.9 5.5 %shard_map.151 = bf16[6,192,512]{2,1,0:T(8,128)(2,1)S(1)} custom-call(s32[1]{0:T(128)} %bitcast.head_ref, bf16[192,1024]{1,0:T(8,128)(2,1)S(1)} %copy-done, bf16[1024,8192]{1,0:T(8,128)(2,1)} %w_ref.1), custom_call_target="tpu_custom_call" | custom-call | tf_op jit(solution)/shard_map/pallas_call | solution.py:359
  76.3 10.1 %collective-permute-done.10 = bf16[2,192,512]{2,1,0:T(8,128)(2,1)S(1)} collective-permute-done((bf16[2,192,512]{2,1,0:T(8,128)(2,1)}, bf16[2,192,512]{2,1,0:T(8,128)(2,1)S(1)}, u32[]{:S(2)}, u32[]{:S(2)}) %collective-permute-start.10) | collective-permute-done | bytes 393248 | tf_op jit(solution)/shard_map/ppermute | solution.py:494
  86.5 0.6 collective-permute-done.9
  87.1 1.1 fusion.11
  88.2 1.5 %collective-permute-start.20 = (bf16[96,512]{1,0:T(8,128)(2,1)}, bf16[96,512]{1,0:T(8,128)(2,1)}, u32[]{:S(2)}, u32[]{:S(2)}) collective-permute-start(bf16[96,512]{1,0:T(8,128)(2,1)} %get-tuple-element.77), channel_id=1, source_target_pairs={{0,1},{1,0},{2,3},{3,2},{4,5},{5,4},{6,7},{7,6},{8,9},{9,8},{10,11... | collective-permute-start | bytes 294920 | tf_op jit(solution)/shard_map/ppermute | solution.py:494
  89.7 2.1 %collective-permute-start.21 = (bf16[96,512]{1,0:T(8,128)(2,1)}, bf16[96,512]{1,0:T(8,128)(2,1)}, u32[]{:S(2)}, u32[]{:S(2)}) collective-permute-start(bf16[96,512]{1,0:T(8,128)(2,1)} %get-tuple-element.76), channel_id=1, source_target_pairs={{0,3},{1,2},{2,1},{3,0},{4,7},{5,6},{6,5},{7,4},{8,11},{9,10},{10,... | collective-permute-start | bytes 294920 | tf_op jit(solution)/shard_map/ppermute | solution.py:494
  92.4 0.6 collective-permute-start.15
  93.0 3.0 %collective-permute-start.16 = (bf16[96,512]{1,0:T(8,128)(2,1)}, bf16[96,512]{1,0:T(8,128)(2,1)}, u32[]{:S(2)}, u32[]{:S(2)}) collective-permute-start(bf16[96,512]{1,0:T(8,128)(2,1)} %get-tuple-element.78), channel_id=1, source_target_pairs={{0,2},{1,3},{2,0},{3,1},{4,6},{5,7},{6,4},{7,5},{8,10},{9,11},{10,... | collective-permute-start | bytes 294920 | tf_op jit(solution)/shard_map/ppermute | solution.py:494
  96.0 1.4 %add_convert_fusion.1 = bf16[2,192,512]{2,1,0:T(8,128)(2,1)S(1)} fusion(bf16[2,192,512]{2,1,0:T(8,128)(2,1)} %copy-done.6, bf16[2,192,512]{2,1,0:T(8,128)(2,1)} %copy-done.5, bf16[2,192,512]{2,1,0:T(8,128)(2,1)} %copy-done.7, bf16[6,192,512]{2,1,0:T(8,128)(2,1)S(1)} %shard_map.151), kind=kLoop, calls=%fused_computation.3 | loop fusion | flops 1572864 | bytes 1966080 | tf_op jit(solution)/shard_map/convert_element_type | solution.py:505
  97.5 0.7 collective-permute-start.22
  98.2 2.7 %collective-permute-done.15 = bf16[96,512]{1,0:T(8,128)(2,1)} collective-permute-done((bf16[96,512]{1,0:T(8,128)(2,1)}, bf16[96,512]{1,0:T(8,128)(2,1)}, u32[]{:S(2)}, u32[]{:S(2)}) %collective-permute-start.15) | collective-permute-done | bytes 98336 | tf_op jit(solution)/shard_map/ppermute | solution.py:494
  101.5 1.1 fusion.2
  102.6 1.0 collective-permute-start.17
  103.6 0.8 collective-permute-start.18
  104.4 2.4 %collective-permute-start.19 = (bf16[96,512]{1,0:T(8,128)(2,1)S(1)}, bf16[96,512]{1,0:T(8,128)(2,1)S(1)}, u32[]{:S(2)}, u32[]{:S(2)}) collective-permute-start(bf16[96,512]{1,0:T(8,128)(2,1)S(1)} %fusion.2), channel_id=1, source_target_pairs={{0,3},{1,2},{2,1},{3,0},{4,7},{5,6},{6,5},{7,4},{8,11},{9,10},{10,... | collective-permute-start | bytes 294920 | tf_op jit(solution)/shard_map/ppermute | solution.py:494
  106.8 1.0 add_convert_fusion.2
  108.2 1.2 collective-permute-done.17
  109.3 1.1 collective-permute-start.24
  110.4 1.6 %collective-permute-start.25 = (bf16[96,512]{1,0:T(8,128)(2,1)S(1)}, bf16[96,512]{1,0:T(8,128)(2,1)S(1)}, u32[]{:S(2)}, u32[]{:S(2)}) collective-permute-start(bf16[96,512]{1,0:T(8,128)(2,1)S(1)} %add_convert_fusion.2), channel_id=1, source_target_pairs={{0,2},{1,3},{2,0},{3,1},{4,6},{5,7},{6,4},{7,5},{8,10},{9,11},{10,... | collective-permute-start | bytes 294920 | tf_op jit(solution)/shard_map/ppermute | solution.py:494
  112.3 2.8 %collective-permute-start.26 = (bf16[4,96,512]{2,1,0:T(8,128)(2,1)S(1)}, bf16[4,96,512]{2,1,0:T(8,128)(2,1)}, u32[]{:S(2)}, u32[]{:S(2)}) collective-permute-start(bf16[4,96,512]{2,1,0:T(8,128)(2,1)S(1)} %pad_maximum_fusion.2.refs_1_), channel_id=1, source_target_pairs={{0,4},{1,5},{2,6},{3,7},{4,0},{5,1},{6,2},{7,3},{8,12},{9,13},{10,... | collective-permute-start | bytes 1179656 | tf_op jit(solution)/shard_map/ppermute | solution.py:494
  115.2 1.3 collective-permute-done.25
  116.6 2.7 %collective-permute-start.27 = (bf16[4,96,512]{2,1,0:T(8,128)(2,1)S(1)}, bf16[4,96,512]{2,1,0:T(8,128)(2,1)}, u32[]{:S(2)}, u32[]{:S(2)}) collective-permute-start(bf16[4,96,512]{2,1,0:T(8,128)(2,1)S(1)} %pad_maximum_fusion.3.refs_2_), channel_id=1, source_target_pairs={{0,4},{1,5},{2,6},{3,7},{4,0},{5,1},{6,2},{7,3},{8,12},{9,13},{10,... | collective-permute-start | bytes 1179656 | tf_op jit(solution)/shard_map/ppermute | solution.py:494
  119.2 3.1 %collective-permute-start.28 = (bf16[2,192,512]{2,1,0:T(8,128)(2,1)S(1)}, bf16[2,192,512]{2,1,0:T(8,128)(2,1)}, u32[]{:S(2)}, u32[]{:S(2)}) collective-permute-start(bf16[2,192,512]{2,1,0:T(8,128)(2,1)S(1)} %add_convert_fusion.refs_0_), channel_id=1, source_target_pairs={{0,2},{1,3},{2,0},{3,1},{4,6},{5,7},{6,4},{7,5},{8,10},{9,11},{10,... | collective-permute-start | bytes 1179656 | tf_op jit(solution)/shard_map/ppermute | solution.py:494
  122.3 1.3 collective-permute-start.29
  123.6 4.7 %shard_map.152 = (bf16[4,1024,128]{2,1,0:T(8,128)(2,1)}, bf16[4,1024,128]{2,1,0:T(8,128)(2,1)}) custom-call(s32[1]{0:T(128)} %bitcast.39.first_ref, s32[16,64]{1,0:T(8,128)S(1)} %bitcast.64, s32[16,64]{1,0:T(8,128)S(1)} %bitcast.63, bf16[16,4,64,256]{3,2,1,0:T(8,128)(2,1)S(1)} %all-to-all-done.source), custom_call_target="tpu_custom_call" | custom-call | tf_op jit(solution)/shard_map/pallas_call | solution.py:466
  128.3 1.8 %shard_map.153.earlier = bf16[192,8192]{1,0:T(8,128)(2,1)} custom-call(s32[1]{0:T(128)} %bitcast.head_ref, bf16[2,192,512]{2,1,0:T(8,128)(2,1)S(1)} %add_convert_fusion.refs_0_, bf16[4,96,512]{2,1,0:T(8,128)(2,1)S(1)} %pad_maximum_fusion.2.refs_1_, bf16[4,96,512]{2,1,0:T(8,128)(2,1)S(1)} %pad_maximum_fusion.3.refs_2_), custom_call_target="tpu_custom_call" | custom-call | tf_op jit(solution)/shard_map/pallas_call | solution.py:396
  130.1 1.8 %collective-permute-done.28.refs_2_ = bf16[2,192,512]{2,1,0:T(8,128)(2,1)} collective-permute-done((bf16[2,192,512]{2,1,0:T(8,128)(2,1)S(1)}, bf16[2,192,512]{2,1,0:T(8,128)(2,1)}, u32[]{:S(2)}, u32[]{:S(2)}) %collective-permute-start.28) | collective-permute-done | bytes 393248 | tf_op jit(solution)/shard_map/ppermute | solution.py:494
  131.9 1.9 %collective-permute-done.29.refs_3_ = bf16[2,192,512]{2,1,0:T(8,128)(2,1)} collective-permute-done((bf16[2,192,512]{2,1,0:T(8,128)(2,1)S(1)}, bf16[2,192,512]{2,1,0:T(8,128)(2,1)}, u32[]{:S(2)}, u32[]{:S(2)}) %collective-permute-start.29) | collective-permute-done | bytes 393248 | tf_op jit(solution)/shard_map/ppermute | solution.py:494
  133.7 2.2 %collective-permute-done.30.refs_4_ = bf16[2,192,512]{2,1,0:T(8,128)(2,1)} collective-permute-done((bf16[2,192,512]{2,1,0:T(8,128)(2,1)S(1)}, bf16[2,192,512]{2,1,0:T(8,128)(2,1)}, u32[]{:S(2)}, u32[]{:S(2)}) %collective-permute-start.30) | collective-permute-done | bytes 393248 | tf_op jit(solution)/shard_map/ppermute | solution.py:494
  135.9 2.8 %shard_map.154 = bf16[192,8192]{1,0:T(8,128)(2,1)} custom-call(s32[1]{0:T(128)} %bitcast.head_ref, bf16[192,8192]{1,0:T(8,128)(2,1)} %shard_map.153.earlier, bf16[4,96,512]{2,1,0:T(8,128)(2,1)} %collective-permute-done.26.refs_0_, bf16[4,96,512]{2,1,0:T(8,128)(2,1)} %collective-permute-done.27.refs_1_, ...), custom_call_target="tpu_custom_call", output_to_operand_aliasing={{}: (1, {})} | custom-call | tf_op jit(solution)/shard_map/pallas_call | solution.py:425
  (53 shorter events, 4.0 us)
Async XLA Ops:
  2.4 17.8 %collective-permute-start = (bf16[1024,128]{1,0:T(8,128)(2,1)}, bf16[1024,128]{1,0:T(8,128)(2,1)S(1)}, u32[]{:S(2)}, u32[]{:S(2)}) collective-permute-start(bf16[1024,128]{1,0:T(8,128)(2,1)} %shard_map.148), channel_id=1, source_target_pairs={{0,64},{8,72},{16,80},{24,88},{32,96},{40,104},{48,112},{56,120},{... | collective-permute-start | bytes 786440 | tf_op jit(solution)/shard_map/ppermute | solution.py:486
  4.3 17.9 %collective-permute-start.1 = (bf16[1024,128]{1,0:T(8,128)(2,1)}, bf16[1024,128]{1,0:T(8,128)(2,1)S(1)}, u32[]{:S(2)}, u32[]{:S(2)}) collective-permute-start(bf16[1024,128]{1,0:T(8,128)(2,1)} %shard_map.148), channel_id=1, source_target_pairs={{0,16},{8,24},{16,32},{24,40},{32,48},{40,56},{48,0},{56,8},{64,80... | collective-permute-start | bytes 786440 | tf_op jit(solution)/shard_map/ppermute | solution.py:486
  5.9 16.4 %collective-permute-start.2 = (bf16[1024,128]{1,0:T(8,128)(2,1)}, bf16[1024,128]{1,0:T(8,128)(2,1)S(1)}, u32[]{:S(2)}, u32[]{:S(2)}) collective-permute-start(bf16[1024,128]{1,0:T(8,128)(2,1)} %shard_map.148), channel_id=1, source_target_pairs={{0,48},{8,56},{16,0},{24,8},{32,16},{40,24},{48,32},{56,40},{64,11... | collective-permute-start | bytes 786440 | tf_op jit(solution)/shard_map/ppermute | solution.py:486
  6.3 13.6 %collective-permute-start.4 = (bf16[1024,128]{1,0:T(8,128)(2,1)}, bf16[1024,128]{1,0:T(8,128)(2,1)S(1)}, u32[]{:S(2)}, u32[]{:S(2)}) collective-permute-start(bf16[1024,128]{1,0:T(8,128)(2,1)} %shard_map.148), channel_id=1, source_target_pairs={{0,32},{8,40},{16,48},{24,56},{32,0},{40,8},{48,16},{56,24},{64,96... | collective-permute-start | bytes 786440 | tf_op jit(solution)/shard_map/ppermute | solution.py:486
  19.9 10.8 %collective-permute-start.7 = (bf16[1024,128]{1,0:T(8,128)(2,1)S(1)}, bf16[1024,128]{1,0:T(8,128)(2,1)S(1)}, u32[]{:S(2)}, u32[]{:S(2)}) collective-permute-start(bf16[1024,128]{1,0:T(8,128)(2,1)S(1)} %collective-permute-done.4), channel_id=1, source_target_pairs={{0,64},{8,72},{16,80},{24,88},{32,96},{40,104},{48,112},{56,120},{... | collective-permute-start | bytes 786440 | tf_op jit(solution)/shard_map/ppermute | solution.py:486
  20.2 10.6 %collective-permute-start.5 = (bf16[1024,128]{1,0:T(8,128)(2,1)S(1)}, bf16[1024,128]{1,0:T(8,128)(2,1)S(1)}, u32[]{:S(2)}, u32[]{:S(2)}) collective-permute-start(bf16[1024,128]{1,0:T(8,128)(2,1)S(1)} %collective-permute-done), channel_id=1, source_target_pairs={{0,16},{8,24},{16,32},{24,40},{32,48},{40,56},{48,0},{56,8},{64,80... | collective-permute-start | bytes 786440 | tf_op jit(solution)/shard_map/ppermute | solution.py:486
  20.2 10.6 %collective-permute-start.6 = (bf16[1024,128]{1,0:T(8,128)(2,1)S(1)}, bf16[1024,128]{1,0:T(8,128)(2,1)S(1)}, u32[]{:S(2)}, u32[]{:S(2)}) collective-permute-start(bf16[1024,128]{1,0:T(8,128)(2,1)S(1)} %collective-permute-done), channel_id=1, source_target_pairs={{0,48},{8,56},{16,0},{24,8},{32,16},{40,24},{48,32},{56,40},{64,11... | collective-permute-start | bytes 786440 | tf_op jit(solution)/shard_map/ppermute | solution.py:486
  23.3 8.6 %copy-start.3 = (bf16[4,1024,128]{2,1,0:T(8,128)(2,1)}, bf16[4,1024,128]{2,1,0:T(8,128)(2,1)S(1)}, u32[]{:S(2)}) copy-start(bf16[4,1024,128]{2,1,0:T(8,128)(2,1)S(1)} %pad_maximum_fusion.refs_0_) | copy-start | bytes 3145732
  23.3 14.6 %collective-permute-start.3 = (bf16[4,1024,128]{2,1,0:T(8,128)(2,1)S(1)}, bf16[4,1024,128]{2,1,0:T(8,128)(2,1)}, u32[]{:S(2)}, u32[]{:S(2)}) collective-permute-start(bf16[4,1024,128]{2,1,0:T(8,128)(2,1)S(1)} %pad_maximum_fusion.refs_0_), channel_id=1, source_target_pairs={{0,8},{8,0},{16,24},{24,16},{32,40},{40,32},{48,56},{56,48},{64,72... | collective-permute-start | bytes 3145736 | tf_op jit(solution)/shard_map/ppermute | solution.py:490
  31.9 6.1 %collective-permute-start.8 = (bf16[4,1024,128]{2,1,0:T(8,128)(2,1)}, bf16[4,1024,128]{2,1,0:T(8,128)(2,1)}, u32[]{:S(2)}, u32[]{:S(2)}) collective-permute-start(bf16[4,1024,128]{2,1,0:T(8,128)(2,1)} %pad_maximum_fusion.1.refs_2_), channel_id=1, source_target_pairs={{0,8},{8,0},{16,24},{24,16},{32,40},{40,32},{48,56},{56,48},{64,72... | collective-permute-start | bytes 3145736 | tf_op jit(solution)/shard_map/ppermute | solution.py:490
  32.4 63.6 %all-to-all-start = ((bf16[16,4,64,256]{3,2,1,0:T(8,128)(2,1)}), bf16[16,4,64,256]{3,2,1,0:T(8,128)(2,1)S(1)}, u32[]{:S(2)}, u32[]{:S(2)}) async-start(bf16[16,4,64,256]{3,2,1,0:T(8,128)(2,1)} %bitcast.66), calls=%async_computation | async-start | bytes 4194304 | tf_op jit(solution)/shard_map/all_to_all | solution.py:553
  61.9 25.2 %collective-permute-start.12 = (bf16[4,192,512]{2,1,0:T(8,128)(2,1)}, bf16[4,192,512]{2,1,0:T(8,128)(2,1)S(1)}, u32[]{:S(2)}, u32[]{:S(2)}) collective-permute-start(bf16[4,192,512]{2,1,0:T(8,128)(2,1)} %get-tuple-element.56), channel_id=1, source_target_pairs={{0,4},{1,5},{2,6},{3,7},{4,0},{5,1},{6,2},{7,3},{8,12},{9,13},{10,... | collective-permute-start | bytes 2359304 | tf_op jit(solution)/shard_map/ppermute | solution.py:494
  65.8 20.7 %collective-permute-start.10 = (bf16[2,192,512]{2,1,0:T(8,128)(2,1)}, bf16[2,192,512]{2,1,0:T(8,128)(2,1)S(1)}, u32[]{:S(2)}, u32[]{:S(2)}) collective-permute-start(bf16[2,192,512]{2,1,0:T(8,128)(2,1)} %get-tuple-element.54), channel_id=1, source_target_pairs={{0,3},{1,2},{2,1},{3,0},{4,7},{5,6},{6,5},{7,4},{8,11},{9,10},{10,... | collective-permute-start | bytes 1179656 | tf_op jit(solution)/shard_map/ppermute | solution.py:494
  68.5 18.0 %collective-permute-start.11 = (bf16[2,192,512]{2,1,0:T(8,128)(2,1)}, bf16[2,192,512]{2,1,0:T(8,128)(2,1)S(1)}, u32[]{:S(2)}, u32[]{:S(2)}) collective-permute-start(bf16[2,192,512]{2,1,0:T(8,128)(2,1)} %get-tuple-element.55), channel_id=1, source_target_pairs={{0,2},{1,3},{2,0},{3,1},{4,6},{5,7},{6,4},{7,5},{8,10},{9,11},{10,... | collective-permute-start | bytes 1179656 | tf_op jit(solution)/shard_map/ppermute | solution.py:494
  69.3 17.8 %collective-permute-start.9 = (bf16[2,192,512]{2,1,0:T(8,128)(2,1)}, bf16[2,192,512]{2,1,0:T(8,128)(2,1)S(1)}, u32[]{:S(2)}, u32[]{:S(2)}) collective-permute-start(bf16[2,192,512]{2,1,0:T(8,128)(2,1)} %get-tuple-element.53), channel_id=1, source_target_pairs={{0,1},{1,0},{2,3},{3,2},{4,5},{5,4},{6,7},{7,6},{8,9},{9,8},{10,11... | collective-permute-start | bytes 1179656 | tf_op jit(solution)/shard_map/ppermute | solution.py:494
  69.9 1.0 copy-start
  86.5 6.5 %copy-start.5 = (bf16[2,192,512]{2,1,0:T(8,128)(2,1)}, bf16[2,192,512]{2,1,0:T(8,128)(2,1)S(1)}, u32[]{:S(2)}) copy-start(bf16[2,192,512]{2,1,0:T(8,128)(2,1)S(1)} %collective-permute-done.10) | copy-start | bytes 1179652
  86.5 6.5 %copy-start.6 = (bf16[2,192,512]{2,1,0:T(8,128)(2,1)}, bf16[2,192,512]{2,1,0:T(8,128)(2,1)S(1)}, u32[]{:S(2)}) copy-start(bf16[2,192,512]{2,1,0:T(8,128)(2,1)S(1)} %collective-permute-done.11) | copy-start | bytes 1179652
  87.1 5.9 %copy-start.7 = (bf16[2,192,512]{2,1,0:T(8,128)(2,1)}, bf16[2,192,512]{2,1,0:T(8,128)(2,1)S(1)}, u32[]{:S(2)}) copy-start(bf16[2,192,512]{2,1,0:T(8,128)(2,1)S(1)} %collective-permute-done.9) | copy-start | bytes 1179652
  87.1 5.9 %copy-start.4 = (bf16[4,192,512]{2,1,0:T(8,128)(2,1)}, bf16[4,192,512]{2,1,0:T(8,128)(2,1)S(1)}, u32[]{:S(2)}) copy-start(bf16[4,192,512]{2,1,0:T(8,128)(2,1)S(1)} %collective-permute-done.12) | copy-start | bytes 2359300
  88.2 15.4 %collective-permute-start.20 = (bf16[96,512]{1,0:T(8,128)(2,1)}, bf16[96,512]{1,0:T(8,128)(2,1)}, u32[]{:S(2)}, u32[]{:S(2)}) collective-permute-start(bf16[96,512]{1,0:T(8,128)(2,1)} %get-tuple-element.77), channel_id=1, source_target_pairs={{0,1},{1,0},{2,3},{3,2},{4,5},{5,4},{6,7},{7,6},{8,9},{9,8},{10,11... | collective-permute-start | bytes 294920 | tf_op jit(solution)/shard_map/ppermute | solution.py:494
  89.7 14.7 %collective-permute-start.21 = (bf16[96,512]{1,0:T(8,128)(2,1)}, bf16[96,512]{1,0:T(8,128)(2,1)}, u32[]{:S(2)}, u32[]{:S(2)}) collective-permute-start(bf16[96,512]{1,0:T(8,128)(2,1)} %get-tuple-element.76), channel_id=1, source_target_pairs={{0,3},{1,2},{2,1},{3,0},{4,7},{5,6},{6,5},{7,4},{8,11},{9,10},{10,... | collective-permute-start | bytes 294920 | tf_op jit(solution)/shard_map/ppermute | solution.py:494
  91.8 5.7 %collective-permute-start.14 = (bf16[96,512]{1,0:T(8,128)(2,1)}, bf16[96,512]{1,0:T(8,128)(2,1)}, u32[]{:S(2)}, u32[]{:S(2)}) collective-permute-start(bf16[96,512]{1,0:T(8,128)(2,1)} %get-tuple-element.80), channel_id=1, source_target_pairs={{0,1},{1,0},{2,3},{3,2},{4,5},{5,4},{6,7},{7,6},{8,9},{9,8},{10,11... | collective-permute-start | bytes 294920 | tf_op jit(solution)/shard_map/ppermute | solution.py:494
  92.4 8.5 %collective-permute-start.15 = (bf16[96,512]{1,0:T(8,128)(2,1)}, bf16[96,512]{1,0:T(8,128)(2,1)}, u32[]{:S(2)}, u32[]{:S(2)}) collective-permute-start(bf16[96,512]{1,0:T(8,128)(2,1)} %get-tuple-element.79), channel_id=1, source_target_pairs={{0,3},{1,2},{2,1},{3,0},{4,7},{5,6},{6,5},{7,4},{8,11},{9,10},{10,... | collective-permute-start | bytes 294920 | tf_op jit(solution)/shard_map/ppermute | solution.py:494
  93.0 8.5 %collective-permute-start.16 = (bf16[96,512]{1,0:T(8,128)(2,1)}, bf16[96,512]{1,0:T(8,128)(2,1)}, u32[]{:S(2)}, u32[]{:S(2)}) collective-permute-start(bf16[96,512]{1,0:T(8,128)(2,1)} %get-tuple-element.78), channel_id=1, source_target_pairs={{0,2},{1,3},{2,0},{3,1},{4,6},{5,7},{6,4},{7,5},{8,10},{9,11},{10,... | collective-permute-start | bytes 294920 | tf_op jit(solution)/shard_map/ppermute | solution.py:494
  97.4 26.2 %copy-start.1 = (s32[64,16]{0,1:T(8,128)S(1)}, s32[64,16]{0,1:T(8,128)}, u32[]{:S(2)}) copy-start(s32[64,16]{0,1:T(8,128)} %param.20) | copy-start | bytes 12292
  97.4 26.2 %copy-start.2 = (s32[64,16]{0,1:T(8,128)S(1)}, s32[64,16]{0,1:T(8,128)}, u32[]{:S(2)}) copy-start(s32[64,16]{0,1:T(8,128)} %param.21) | copy-start | bytes 12292
  97.5 9.3 %collective-permute-start.22 = (bf16[96,512]{1,0:T(8,128)(2,1)S(1)}, bf16[96,512]{1,0:T(8,128)(2,1)S(1)}, u32[]{:S(2)}, u32[]{:S(2)}) collective-permute-start(bf16[96,512]{1,0:T(8,128)(2,1)S(1)} %get-tuple-element.75), channel_id=1, source_target_pairs={{0,2},{1,3},{2,0},{3,1},{4,6},{5,7},{6,4},{7,5},{8,10},{9,11},{10,... | collective-permute-start | bytes 294920 | tf_op jit(solution)/shard_map/ppermute | solution.py:494
  100.9 14.1 %collective-permute-start.13 = (bf16[2,192,512]{2,1,0:T(8,128)(2,1)S(1)}, bf16[2,192,512]{2,1,0:T(8,128)(2,1)S(1)}, u32[]{:S(2)}, u32[]{:S(2)}) collective-permute-start(bf16[2,192,512]{2,1,0:T(8,128)(2,1)S(1)} %add_convert_fusion.1), channel_id=1, source_target_pairs={{0,4},{1,5},{2,6},{3,7},{4,0},{5,1},{6,2},{7,3},{8,12},{9,13},{10,... | collective-permute-start | bytes 1179656 | tf_op jit(solution)/shard_map/ppermute | solution.py:494
  102.6 6.7 %collective-permute-start.17 = (bf16[96,512]{1,0:T(8,128)(2,1)S(1)}, bf16[96,512]{1,0:T(8,128)(2,1)S(1)}, u32[]{:S(2)}, u32[]{:S(2)}) collective-permute-start(bf16[96,512]{1,0:T(8,128)(2,1)S(1)} %fusion.2), channel_id=1, source_target_pairs={{0,2},{1,3},{2,0},{3,1},{4,6},{5,7},{6,4},{7,5},{8,10},{9,11},{10,... | collective-permute-start | bytes 294920 | tf_op jit(solution)/shard_map/ppermute | solution.py:494
  103.6 6.8 %collective-permute-start.18 = (bf16[96,512]{1,0:T(8,128)(2,1)S(1)}, bf16[96,512]{1,0:T(8,128)(2,1)S(1)}, u32[]{:S(2)}, u32[]{:S(2)}) collective-permute-start(bf16[96,512]{1,0:T(8,128)(2,1)S(1)} %fusion.2), channel_id=1, source_target_pairs={{0,1},{1,0},{2,3},{3,2},{4,5},{5,4},{6,7},{7,6},{8,9},{9,8},{10,11... | collective-permute-start | bytes 294920 | tf_op jit(solution)/shard_map/ppermute | solution.py:494
  104.4 7.8 %collective-permute-start.19 = (bf16[96,512]{1,0:T(8,128)(2,1)S(1)}, bf16[96,512]{1,0:T(8,128)(2,1)S(1)}, u32[]{:S(2)}, u32[]{:S(2)}) collective-permute-start(bf16[96,512]{1,0:T(8,128)(2,1)S(1)} %fusion.2), channel_id=1, source_target_pairs={{0,3},{1,2},{2,1},{3,0},{4,7},{5,6},{6,5},{7,4},{8,11},{9,10},{10,... | collective-permute-start | bytes 294920 | tf_op jit(solution)/shard_map/ppermute | solution.py:494
  107.8 7.4 %collective-permute-start.23 = (bf16[96,512]{1,0:T(8,128)(2,1)S(1)}, bf16[96,512]{1,0:T(8,128)(2,1)S(1)}, u32[]{:S(2)}, u32[]{:S(2)}) collective-permute-start(bf16[96,512]{1,0:T(8,128)(2,1)S(1)} %add_convert_fusion.2), channel_id=1, source_target_pairs={{0,1},{1,0},{2,3},{3,2},{4,5},{5,4},{6,7},{7,6},{8,9},{9,8},{10,11... | collective-permute-start | bytes 294920 | tf_op jit(solution)/shard_map/ppermute | solution.py:494
  109.3 5.9 %collective-permute-start.24 = (bf16[96,512]{1,0:T(8,128)(2,1)S(1)}, bf16[96,512]{1,0:T(8,128)(2,1)S(1)}, u32[]{:S(2)}, u32[]{:S(2)}) collective-permute-start(bf16[96,512]{1,0:T(8,128)(2,1)S(1)} %add_convert_fusion.2), channel_id=1, source_target_pairs={{0,3},{1,2},{2,1},{3,0},{4,7},{5,6},{6,5},{7,4},{8,11},{9,10},{10,... | collective-permute-start | bytes 294920 | tf_op jit(solution)/shard_map/ppermute | solution.py:494
  110.4 6.1 %collective-permute-start.25 = (bf16[96,512]{1,0:T(8,128)(2,1)S(1)}, bf16[96,512]{1,0:T(8,128)(2,1)S(1)}, u32[]{:S(2)}, u32[]{:S(2)}) collective-permute-start(bf16[96,512]{1,0:T(8,128)(2,1)S(1)} %add_convert_fusion.2), channel_id=1, source_target_pairs={{0,2},{1,3},{2,0},{3,1},{4,6},{5,7},{6,4},{7,5},{8,10},{9,11},{10,... | collective-permute-start | bytes 294920 | tf_op jit(solution)/shard_map/ppermute | solution.py:494
  112.3 17.8 %collective-permute-start.26 = (bf16[4,96,512]{2,1,0:T(8,128)(2,1)S(1)}, bf16[4,96,512]{2,1,0:T(8,128)(2,1)}, u32[]{:S(2)}, u32[]{:S(2)}) collective-permute-start(bf16[4,96,512]{2,1,0:T(8,128)(2,1)S(1)} %pad_maximum_fusion.2.refs_1_), channel_id=1, source_target_pairs={{0,4},{1,5},{2,6},{3,7},{4,0},{5,1},{6,2},{7,3},{8,12},{9,13},{10,... | collective-permute-start | bytes 1179656 | tf_op jit(solution)/shard_map/ppermute | solution.py:494
  116.6 13.5 %collective-permute-start.27 = (bf16[4,96,512]{2,1,0:T(8,128)(2,1)S(1)}, bf16[4,96,512]{2,1,0:T(8,128)(2,1)}, u32[]{:S(2)}, u32[]{:S(2)}) collective-permute-start(bf16[4,96,512]{2,1,0:T(8,128)(2,1)S(1)} %pad_maximum_fusion.3.refs_2_), channel_id=1, source_target_pairs={{0,4},{1,5},{2,6},{3,7},{4,0},{5,1},{6,2},{7,3},{8,12},{9,13},{10,... | collective-permute-start | bytes 1179656 | tf_op jit(solution)/shard_map/ppermute | solution.py:494
  119.2 12.6 %collective-permute-start.28 = (bf16[2,192,512]{2,1,0:T(8,128)(2,1)S(1)}, bf16[2,192,512]{2,1,0:T(8,128)(2,1)}, u32[]{:S(2)}, u32[]{:S(2)}) collective-permute-start(bf16[2,192,512]{2,1,0:T(8,128)(2,1)S(1)} %add_convert_fusion.refs_0_), channel_id=1, source_target_pairs={{0,2},{1,3},{2,0},{3,1},{4,6},{5,7},{6,4},{7,5},{8,10},{9,11},{10,... | collective-permute-start | bytes 1179656 | tf_op jit(solution)/shard_map/ppermute | solution.py:494
  122.3 11.4 %collective-permute-start.29 = (bf16[2,192,512]{2,1,0:T(8,128)(2,1)S(1)}, bf16[2,192,512]{2,1,0:T(8,128)(2,1)}, u32[]{:S(2)}, u32[]{:S(2)}) collective-permute-start(bf16[2,192,512]{2,1,0:T(8,128)(2,1)S(1)} %add_convert_fusion.refs_0_), channel_id=1, source_target_pairs={{0,1},{1,0},{2,3},{3,2},{4,5},{5,4},{6,7},{7,6},{8,9},{9,8},{10,11... | collective-permute-start | bytes 1179656 | tf_op jit(solution)/shard_map/ppermute | solution.py:494
  123.6 12.3 %collective-permute-start.30 = (bf16[2,192,512]{2,1,0:T(8,128)(2,1)S(1)}, bf16[2,192,512]{2,1,0:T(8,128)(2,1)}, u32[]{:S(2)}, u32[]{:S(2)}) collective-permute-start(bf16[2,192,512]{2,1,0:T(8,128)(2,1)S(1)} %add_convert_fusion.refs_0_), channel_id=1, source_target_pairs={{0,3},{1,2},{2,1},{3,0},{4,7},{5,6},{6,5},{7,4},{8,11},{9,10},{10,... | collective-permute-start | bytes 1179656 | tf_op jit(solution)/shard_map/ppermute | solution.py:494

commit v4 on v1

--- a/solution.py
+++ b/solution.py
@@ -570,8 +570,8 @@
     got_zx = [move_roles(*part[:3]) for part in zpart]
     got_x = after(got_x, zpart[1][3], gathered)
     xsum = add(kept[4:], *got_x)
-    got_zx[1] = after(got_zx[1], xsum)
-    zsum = [add(part[3], *got) for part, got in zip(zpart, got_zx)]
+    zsum = [add(zpart[0][3], *got_zx[0])]
+    zsum.append(add(zpart[1][3], *after(got_zx[1], xsum, zsum[0])))
 
     pair = add(xsum, move_x(xsum, 4)[::-1])
     zback = [move_roles(part, part, part) for part in zsum]

time: 134 us -> 132 us (0.985)
  the two profiles are of different devices: /device:TPU:8 before, /device:TPU:0 now
where the time goes in v4:
time: 132 us; the launch traced here: 131 us
  starting transfers between devices  53.1 us (40%)
  Pallas kernels  47.4 us (36%)
  waiting for transfers between devices  19.5 us (15%)
  other arithmetic  9.47 us (7%)
    ppermute x22, starting transfers between devices, move_x(): return lax.ppermute(value, 'head', [(h, h ^ flip) for h in range(KVH)])  36 us
    pallas_call x1, Pallas kernels, prompt_part(): pl.pallas_call(functools.partial(prompt_kernel, places, groups, len(stack...  23.4 us
    ppermute x22, waiting for transfers between devices, move_x(): return lax.ppermute(value, 'head', [(h, h ^ flip) for h in range(KVH)])  19.4 us
    ppermute x7, starting transfers between devices, move_chip(): return lax.ppermute(value, 'branch', perm)  12.9 us
    pallas_call x1, Pallas kernels, span_part(): pl.pallas_call(span_kernel, grid_spec=pltpu.PrefetchScalarGridSpec(num_sc...  7.44 us
    pallas_call x1, Pallas kernels, project(): pl.pallas_call(functools.partial(project_kernel, places), grid_spec=pltpu...  5.46 us
    convert_element_type x5, other arithmetic, add(): return total.astype(jnp.bfloat16)  4.72 us
    pallas_call x1, Pallas kernels, join(): pl.pallas_call(join_kernel, grid_spec=pltpu.PrefetchScalarGridSpec(num_sc...  4.69 us
  transfers between devices with their start and end apart: 32, of which 9 were waited for; matrix products, arithmetic and copies ran while one was open for 7% of the time, Pallas kernels for 33%

profile of v4, /device:TPU:0, one launch (start us, length us, event | category | flops | bytes accessed | tf_op | source)
XLA Modules:
  0.0 131.5 jit_solution(391950741352184469)
XLA Ops:
  0.6 1.8 %shard_map.149 = bf16[1024,128]{1,0:T(8,128)(2,1)} custom-call(bf16[512,128]{1,0:T(8,128)(2,1)} %keys_ref.1, bf16[512,128]{1,0:T(8,128)(2,1)} %vals_ref.1), custom_call_target="tpu_custom_call" | custom-call | tf_op jit(solution)/shard_map/pallas_call | solution.py:156
  2.4 3.3 %collective-permute-start.3 = (bf16[1024,128]{1,0:T(8,128)(2,1)}, bf16[1024,128]{1,0:T(8,128)(2,1)S(1)}, u32[]{:S(2)}, u32[]{:S(2)}) collective-permute-start(bf16[1024,128]{1,0:T(8,128)(2,1)} %shard_map.149), channel_id=1, source_target_pairs={{0,32},{8,40},{16,48},{24,56},{32,0},{40,8},{48,16},{56,24},{64,96... | collective-permute-start | bytes 786440 | tf_op jit(solution)/shard_map/ppermute | solution.py:486
  5.7 1.9 %collective-permute-start = (bf16[1024,128]{1,0:T(8,128)(2,1)}, bf16[1024,128]{1,0:T(8,128)(2,1)S(1)}, u32[]{:S(2)}, u32[]{:S(2)}) collective-permute-start(bf16[1024,128]{1,0:T(8,128)(2,1)} %shard_map.149), channel_id=1, source_target_pairs={{0,64},{8,72},{16,80},{24,88},{32,96},{40,104},{48,112},{56,120},{... | collective-permute-start | bytes 786440 | tf_op jit(solution)/shard_map/ppermute | solution.py:486
  7.6 0.7 collective-permute-start.1
  8.3 2.6 %collective-permute-start.2 = (bf16[1024,128]{1,0:T(8,128)(2,1)}, bf16[1024,128]{1,0:T(8,128)(2,1)S(1)}, u32[]{:S(2)}, u32[]{:S(2)}) collective-permute-start(bf16[1024,128]{1,0:T(8,128)(2,1)} %shard_map.149), channel_id=1, source_target_pairs={{0,48},{8,56},{16,0},{24,8},{32,16},{40,24},{48,32},{56,40},{64,11... | collective-permute-start | bytes 786440 | tf_op jit(solution)/shard_map/ppermute | solution.py:486
  10.8 0.7 add_bitcast_fusion.1
  11.5 0.7 add_bitcast_fusion
  12.2 1.9 %fusion.3 = (f32[4,64,128]{2,1,0:T(8,128)}, f32[4,64,128]{2,1,0:T(8,128)}) fusion(f32[128]{0:T(128)} %constant.24.clone, f32[128]{0:T(128)} %constant.23.clone, f32[4,64]{1,0:T(4,128)S(1)} %add_convert_fusion.11), kind=kLoop, calls=%fused_computation.21 | loop fusion | flops 65536 | bytes 264192 | tf_op jit(solution)/shard_map/mul | solution.py:46
  14.1 1.2 collective-permute-start.6
  15.3 1.6 %collective-permute-start.4 = (bf16[1024,128]{1,0:T(8,128)(2,1)S(1)}, bf16[1024,128]{1,0:T(8,128)(2,1)S(1)}, u32[]{:S(2)}, u32[]{:S(2)}) collective-permute-start(bf16[1024,128]{1,0:T(8,128)(2,1)S(1)} %collective-permute-done), channel_id=1, source_target_pairs={{0,16},{8,24},{16,32},{24,40},{32,48},{40,56},{48,0},{56,8},{64,80... | collective-permute-start | bytes 786440 | tf_op jit(solution)/shard_map/ppermute | solution.py:486
  16.9 1.7 %collective-permute-start.5 = (bf16[1024,128]{1,0:T(8,128)(2,1)S(1)}, bf16[1024,128]{1,0:T(8,128)(2,1)S(1)}, u32[]{:S(2)}, u32[]{:S(2)}) collective-permute-start(bf16[1024,128]{1,0:T(8,128)(2,1)S(1)} %collective-permute-done), channel_id=1, source_target_pairs={{0,48},{8,56},{16,0},{24,8},{32,16},{40,24},{48,32},{56,40},{64,11... | collective-permute-start | bytes 786440 | tf_op jit(solution)/shard_map/ppermute | solution.py:486
  18.6 7.4 %shard_map.148 = (bf16[3,64,1024]{2,1,0:T(8,128)(2,1)}, f32[4,384,128]{2,1,0:T(8,128)}, f32[4,384,256]{2,1,0:T(8,128)}, bf16[64,64,256]{2,1,0:T(8,128)(2,1)}) custom-call(s32[16,64]{1,0:T(8,128)} %bitcast.62, s32[1]{0:T(128)} %bitcast.2.me_ref, bf16[3,64,1024]{2,1,0:T(8,128)(2,1)} %bitcast.70, f32[4,64,128]{2,1,0:T(8,128)} %get-tuple-element.81.cos_ref, ...), custom_call_target="tpu_custom_call" | custom-call | tf_op jit(solution)/shard_map/pallas_call | solution.py:128
  26.3 1.2 pad_maximum_fusion.refs_0_
  27.9 3.7 %all-to-all-start = ((bf16[16,4,64,256]{3,2,1,0:T(8,128)(2,1)}), bf16[16,4,64,256]{3,2,1,0:T(8,128)(2,1)S(1)}, u32[]{:S(2)}, u32[]{:S(2)}) async-start(bf16[16,4,64,256]{3,2,1,0:T(8,128)(2,1)} %bitcast.66), calls=%async_computation | async-start | bytes 4194304 | tf_op jit(solution)/shard_map/all_to_all | solution.py:551
  31.7 23.4 %shard_map.150 = (bf16[4,192,512]{2,1,0:T(8,128)(2,1)}, bf16[2,192,512]{2,1,0:T(8,128)(2,1)}, bf16[2,192,512]{2,1,0:T(8,128)(2,1)}, bf16[2,192,512]{2,1,0:T(8,128)(2,1)}, bf16[192,1024]{1,0:T(8,128)(2,1)}) custom-call(s32[4,16]{1,0:T(4,128)} %bitcast.88, s32[1]{0:T(128)} %bitcast.2.me_ref, s32[1]{0:T(128)} %bitcast.head_ref, ...), custom_call_target="tpu_custom_call" | custom-call | tf_op jit(solution)/shard_map/pallas_call | solution.py:309
  55.1 3.7 %collective-permute-start.12 = (bf16[4,192,512]{2,1,0:T(8,128)(2,1)}, bf16[4,192,512]{2,1,0:T(8,128)(2,1)S(1)}, u32[]{:S(2)}, u32[]{:S(2)}) collective-permute-start(bf16[4,192,512]{2,1,0:T(8,128)(2,1)} %get-tuple-element.54), channel_id=1, source_target_pairs={{0,4},{1,5},{2,6},{3,7},{4,0},{5,1},{6,2},{7,3},{8,12},{9,13},{10,... | collective-permute-start | bytes 2359304 | tf_op jit(solution)/shard_map/ppermute | solution.py:494
  58.8 2.8 %collective-permute-start.10 = (bf16[2,192,512]{2,1,0:T(8,128)(2,1)}, bf16[2,192,512]{2,1,0:T(8,128)(2,1)S(1)}, u32[]{:S(2)}, u32[]{:S(2)}) collective-permute-start(bf16[2,192,512]{2,1,0:T(8,128)(2,1)} %get-tuple-element.52), channel_id=1, source_target_pairs={{0,3},{1,2},{2,1},{3,0},{4,7},{5,6},{6,5},{7,4},{8,11},{9,10},{10,... | collective-permute-start | bytes 1179656 | tf_op jit(solution)/shard_map/ppermute | solution.py:494
  61.5 0.8 collective-permute-start.11
  62.9 1.0 copy-done
  63.8 5.5 %shard_map.151 = bf16[6,192,512]{2,1,0:T(8,128)(2,1)S(1)} custom-call(s32[1]{0:T(128)} %bitcast.head_ref, bf16[192,1024]{1,0:T(8,128)(2,1)S(1)} %copy-done, bf16[1024,8192]{1,0:T(8,128)(2,1)} %w_ref.1), custom_call_target="tpu_custom_call" | custom-call | tf_op jit(solution)/shard_map/pallas_call | solution.py:359
  69.3 10.9 %collective-permute-done.10 = bf16[2,192,512]{2,1,0:T(8,128)(2,1)S(1)} collective-permute-done((bf16[2,192,512]{2,1,0:T(8,128)(2,1)}, bf16[2,192,512]{2,1,0:T(8,128)(2,1)S(1)}, u32[]{:S(2)}, u32[]{:S(2)}) %collective-permute-start.10) | collective-permute-done | bytes 393248 | tf_op jit(solution)/shard_map/ppermute | solution.py:494
  80.2 1.1 collective-permute-done.9
  81.3 1.1 fusion.11
  82.4 1.5 %collective-permute-start.14 = (bf16[96,512]{1,0:T(8,128)(2,1)}, bf16[96,512]{1,0:T(8,128)(2,1)}, u32[]{:S(2)}, u32[]{:S(2)}) collective-permute-start(bf16[96,512]{1,0:T(8,128)(2,1)} %get-tuple-element.78), channel_id=1, source_target_pairs={{0,1},{1,0},{2,3},{3,2},{4,5},{5,4},{6,7},{7,6},{8,9},{9,8},{10,11... | collective-permute-start | bytes 294920 | tf_op jit(solution)/shard_map/ppermute | solution.py:494
  83.9 2.1 %collective-permute-start.15 = (bf16[96,512]{1,0:T(8,128)(2,1)}, bf16[96,512]{1,0:T(8,128)(2,1)}, u32[]{:S(2)}, u32[]{:S(2)}) collective-permute-start(bf16[96,512]{1,0:T(8,128)(2,1)} %get-tuple-element.77), channel_id=1, source_target_pairs={{0,3},{1,2},{2,1},{3,0},{4,7},{5,6},{6,5},{7,4},{8,11},{9,10},{10,... | collective-permute-start | bytes 294920 | tf_op jit(solution)/shard_map/ppermute | solution.py:494
  86.6 1.4 %collective-permute-start.20 = (bf16[96,512]{1,0:T(8,128)(2,1)}, bf16[96,512]{1,0:T(8,128)(2,1)}, u32[]{:S(2)}, u32[]{:S(2)}) collective-permute-start(bf16[96,512]{1,0:T(8,128)(2,1)} %get-tuple-element.75), channel_id=1, source_target_pairs={{0,1},{1,0},{2,3},{3,2},{4,5},{5,4},{6,7},{7,6},{8,9},{9,8},{10,11... | collective-permute-start | bytes 294920 | tf_op jit(solution)/shard_map/ppermute | solution.py:494
  88.0 2.2 %collective-permute-start.21 = (bf16[96,512]{1,0:T(8,128)(2,1)}, bf16[96,512]{1,0:T(8,128)(2,1)}, u32[]{:S(2)}, u32[]{:S(2)}) collective-permute-start(bf16[96,512]{1,0:T(8,128)(2,1)} %get-tuple-element.74), channel_id=1, source_target_pairs={{0,3},{1,2},{2,1},{3,0},{4,7},{5,6},{6,5},{7,4},{8,11},{9,10},{10,... | collective-permute-start | bytes 294920 | tf_op jit(solution)/shard_map/ppermute | solution.py:494
  90.2 1.4 %add_convert_fusion.1 = bf16[2,192,512]{2,1,0:T(8,128)(2,1)S(1)} fusion(bf16[2,192,512]{2,1,0:T(8,128)(2,1)} %copy-done.7, bf16[2,192,512]{2,1,0:T(8,128)(2,1)} %copy-done.6, bf16[2,192,512]{2,1,0:T(8,128)(2,1)} %copy-done.8, bf16[6,192,512]{2,1,0:T(8,128)(2,1)S(1)} %shard_map.151), kind=kLoop, calls=%fused_computation.3 | loop fusion | flops 1572864 | bytes 1966080 | tf_op jit(solution)/shard_map/convert_element_type | solution.py:505
  91.6 0.7 collective-permute-start.22
  92.4 0.8 collective-permute-done.16
  93.2 1.1 fusion.2
  94.3 2.2 %collective-permute-start.17 = (bf16[96,512]{1,0:T(8,128)(2,1)S(1)}, bf16[96,512]{1,0:T(8,128)(2,1)S(1)}, u32[]{:S(2)}, u32[]{:S(2)}) collective-permute-start(bf16[96,512]{1,0:T(8,128)(2,1)S(1)} %fusion.2), channel_id=1, source_target_pairs={{0,2},{1,3},{2,0},{3,1},{4,6},{5,7},{6,4},{7,5},{8,10},{9,11},{10,... | collective-permute-start | bytes 294920 | tf_op jit(solution)/shard_map/ppermute | solution.py:494
  97.0 1.4 %collective-permute-start.19 = (bf16[96,512]{1,0:T(8,128)(2,1)S(1)}, bf16[96,512]{1,0:T(8,128)(2,1)S(1)}, u32[]{:S(2)}, u32[]{:S(2)}) collective-permute-start(bf16[96,512]{1,0:T(8,128)(2,1)S(1)} %fusion.2), channel_id=1, source_target_pairs={{0,3},{1,2},{2,1},{3,0},{4,7},{5,6},{6,5},{7,4},{8,11},{9,10},{10,... | collective-permute-start | bytes 294920 | tf_op jit(solution)/shard_map/ppermute | solution.py:494
  98.8 1.0 add_convert_fusion.2
  99.8 0.7 collective-permute-start.23
  100.7 2.0 %collective-permute-start.24 = (bf16[96,512]{1,0:T(8,128)(2,1)S(1)}, bf16[96,512]{1,0:T(8,128)(2,1)S(1)}, u32[]{:S(2)}, u32[]{:S(2)}) collective-permute-start(bf16[96,512]{1,0:T(8,128)(2,1)S(1)} %add_convert_fusion.2), channel_id=1, source_target_pairs={{0,3},{1,2},{2,1},{3,0},{4,7},{5,6},{6,5},{7,4},{8,11},{9,10},{10,... | collective-permute-start | bytes 294920 | tf_op jit(solution)/shard_map/ppermute | solution.py:494
  102.8 1.5 %collective-permute-start.25 = (bf16[96,512]{1,0:T(8,128)(2,1)S(1)}, bf16[96,512]{1,0:T(8,128)(2,1)S(1)}, u32[]{:S(2)}, u32[]{:S(2)}) collective-permute-start(bf16[96,512]{1,0:T(8,128)(2,1)S(1)} %add_convert_fusion.2), channel_id=1, source_target_pairs={{0,2},{1,3},{2,0},{3,1},{4,6},{5,7},{6,4},{7,5},{8,10},{9,11},{10,... | collective-permute-start | bytes 294920 | tf_op jit(solution)/shard_map/ppermute | solution.py:494
  104.4 3.0 %collective-permute-start.26 = (bf16[4,96,512]{2,1,0:T(8,128)(2,1)S(1)}, bf16[4,96,512]{2,1,0:T(8,128)(2,1)}, u32[]{:S(2)}, u32[]{:S(2)}) collective-permute-start(bf16[4,96,512]{2,1,0:T(8,128)(2,1)S(1)} %pad_maximum_fusion.2.refs_1_), channel_id=1, source_target_pairs={{0,4},{1,5},{2,6},{3,7},{4,0},{5,1},{6,2},{7,3},{8,12},{9,13},{10,... | collective-permute-start | bytes 1179656 | tf_op jit(solution)/shard_map/ppermute | solution.py:494
  107.5 1.3 %collective-permute-done.25 = bf16[96,512]{1,0:T(8,128)(2,1)S(1)} collective-permute-done((bf16[96,512]{1,0:T(8,128)(2,1)S(1)}, bf16[96,512]{1,0:T(8,128)(2,1)S(1)}, u32[]{:S(2)}, u32[]{:S(2)}) %collective-permute-start.25) | collective-permute-done | bytes 98336 | tf_op jit(solution)/shard_map/ppermute | solution.py:494
  108.9 4.1 %collective-permute-start.27 = (bf16[4,96,512]{2,1,0:T(8,128)(2,1)S(1)}, bf16[4,96,512]{2,1,0:T(8,128)(2,1)}, u32[]{:S(2)}, u32[]{:S(2)}) collective-permute-start(bf16[4,96,512]{2,1,0:T(8,128)(2,1)S(1)} %pad_maximum_fusion.3.refs_2_), channel_id=1, source_target_pairs={{0,4},{1,5},{2,6},{3,7},{4,0},{5,1},{6,2},{7,3},{8,12},{9,13},{10,... | collective-permute-start | bytes 1179656 | tf_op jit(solution)/shard_map/ppermute | solution.py:494
  113.5 0.9 collective-permute-start.29
  114.5 2.7 %collective-permute-start.30 = (bf16[2,192,512]{2,1,0:T(8,128)(2,1)S(1)}, bf16[2,192,512]{2,1,0:T(8,128)(2,1)}, u32[]{:S(2)}, u32[]{:S(2)}) collective-permute-start(bf16[2,192,512]{2,1,0:T(8,128)(2,1)S(1)} %add_convert_fusion.refs_0_), channel_id=1, source_target_pairs={{0,3},{1,2},{2,1},{3,0},{4,7},{5,6},{6,5},{7,4},{8,11},{9,10},{10,... | collective-permute-start | bytes 1179656 | tf_op jit(solution)/shard_map/ppermute | solution.py:494
  117.2 4.7 %shard_map.152 = (bf16[4,1024,128]{2,1,0:T(8,128)(2,1)}, bf16[4,1024,128]{2,1,0:T(8,128)(2,1)}) custom-call(s32[1]{0:T(128)} %bitcast.39.first_ref, s32[16,64]{1,0:T(8,128)S(1)} %bitcast.64, s32[16,64]{1,0:T(8,128)S(1)} %bitcast.63, bf16[16,4,64,256]{3,2,1,0:T(8,128)(2,1)S(1)} %all-to-all-done.source), custom_call_target="tpu_custom_call" | custom-call | tf_op jit(solution)/shard_map/pallas_call | solution.py:466
  121.9 1.8 %shard_map.153.earlier = bf16[192,8192]{1,0:T(8,128)(2,1)} custom-call(s32[1]{0:T(128)} %bitcast.head_ref, bf16[2,192,512]{2,1,0:T(8,128)(2,1)S(1)} %add_convert_fusion.refs_0_, bf16[4,96,512]{2,1,0:T(8,128)(2,1)S(1)} %pad_maximum_fusion.2.refs_1_, bf16[4,96,512]{2,1,0:T(8,128)(2,1)S(1)} %pad_maximum_fusion.3.refs_2_), custom_call_target="tpu_custom_call" | custom-call | tf_op jit(solution)/shard_map/pallas_call | solution.py:396
  123.6 0.8 collective-permute-done.28.refs_2_
  124.4 3.2 %collective-permute-done.29.refs_3_ = bf16[2,192,512]{2,1,0:T(8,128)(2,1)} collective-permute-done((bf16[2,192,512]{2,1,0:T(8,128)(2,1)S(1)}, bf16[2,192,512]{2,1,0:T(8,128)(2,1)}, u32[]{:S(2)}, u32[]{:S(2)}) %collective-permute-start.29) | collective-permute-done | bytes 393248 | tf_op jit(solution)/shard_map/ppermute | solution.py:494
  127.6 0.8 collective-permute-done.30.refs_4_
  128.4 2.8 %shard_map.154 = bf16[192,8192]{1,0:T(8,128)(2,1)} custom-call(s32[1]{0:T(128)} %bitcast.head_ref, bf16[192,8192]{1,0:T(8,128)(2,1)} %shard_map.153.earlier, bf16[4,96,512]{2,1,0:T(8,128)(2,1)} %collective-permute-done.26.refs_0_, bf16[4,96,512]{2,1,0:T(8,128)(2,1)} %collective-permute-done.27.refs_1_, ...), custom_call_target="tpu_custom_call", output_to_operand_aliasing={{}: (1, {})} | custom-call | tf_op jit(solution)/shard_map/pallas_call | solution.py:425
  (55 shorter events, 3.7 us)
Async XLA Ops:
  2.4 11.8 %collective-permute-start.3 = (bf16[1024,128]{1,0:T(8,128)(2,1)}, bf16[1024,128]{1,0:T(8,128)(2,1)S(1)}, u32[]{:S(2)}, u32[]{:S(2)}) collective-permute-start(bf16[1024,128]{1,0:T(8,128)(2,1)} %shard_map.149), channel_id=1, source_target_pairs={{0,32},{8,40},{16,48},{24,56},{32,0},{40,8},{48,16},{56,24},{64,96... | collective-permute-start | bytes 786440 | tf_op jit(solution)/shard_map/ppermute | solution.py:486
  5.7 9.7 %collective-permute-start = (bf16[1024,128]{1,0:T(8,128)(2,1)}, bf16[1024,128]{1,0:T(8,128)(2,1)S(1)}, u32[]{:S(2)}, u32[]{:S(2)}) collective-permute-start(bf16[1024,128]{1,0:T(8,128)(2,1)} %shard_map.149), channel_id=1, source_target_pairs={{0,64},{8,72},{16,80},{24,88},{32,96},{40,104},{48,112},{56,120},{... | collective-permute-start | bytes 786440 | tf_op jit(solution)/shard_map/ppermute | solution.py:486
  7.6 18.4 %collective-permute-start.1 = (bf16[1024,128]{1,0:T(8,128)(2,1)}, bf16[1024,128]{1,0:T(8,128)(2,1)S(1)}, u32[]{:S(2)}, u32[]{:S(2)}) collective-permute-start(bf16[1024,128]{1,0:T(8,128)(2,1)} %shard_map.149), channel_id=1, source_target_pairs={{0,16},{8,24},{16,32},{24,40},{32,48},{40,56},{48,0},{56,8},{64,80... | collective-permute-start | bytes 786440 | tf_op jit(solution)/shard_map/ppermute | solution.py:486
  8.3 17.8 %collective-permute-start.2 = (bf16[1024,128]{1,0:T(8,128)(2,1)}, bf16[1024,128]{1,0:T(8,128)(2,1)S(1)}, u32[]{:S(2)}, u32[]{:S(2)}) collective-permute-start(bf16[1024,128]{1,0:T(8,128)(2,1)} %shard_map.149), channel_id=1, source_target_pairs={{0,48},{8,56},{16,0},{24,8},{32,16},{40,24},{48,32},{56,40},{64,11... | collective-permute-start | bytes 786440 | tf_op jit(solution)/shard_map/ppermute | solution.py:486
  14.1 11.9 %collective-permute-start.6 = (bf16[1024,128]{1,0:T(8,128)(2,1)S(1)}, bf16[1024,128]{1,0:T(8,128)(2,1)S(1)}, u32[]{:S(2)}, u32[]{:S(2)}) collective-permute-start(bf16[1024,128]{1,0:T(8,128)(2,1)S(1)} %collective-permute-done.3), channel_id=1, source_target_pairs={{0,64},{8,72},{16,80},{24,88},{32,96},{40,104},{48,112},{56,120},{... | collective-permute-start | bytes 786440 | tf_op jit(solution)/shard_map/ppermute | solution.py:486
  15.3 10.7 %collective-permute-start.4 = (bf16[1024,128]{1,0:T(8,128)(2,1)S(1)}, bf16[1024,128]{1,0:T(8,128)(2,1)S(1)}, u32[]{:S(2)}, u32[]{:S(2)}) collective-permute-start(bf16[1024,128]{1,0:T(8,128)(2,1)S(1)} %collective-permute-done), channel_id=1, source_target_pairs={{0,16},{8,24},{16,32},{24,40},{32,48},{40,56},{48,0},{56,8},{64,80... | collective-permute-start | bytes 786440 | tf_op jit(solution)/shard_map/ppermute | solution.py:486
  16.9 9.1 %collective-permute-start.5 = (bf16[1024,128]{1,0:T(8,128)(2,1)S(1)}, bf16[1024,128]{1,0:T(8,128)(2,1)S(1)}, u32[]{:S(2)}, u32[]{:S(2)}) collective-permute-start(bf16[1024,128]{1,0:T(8,128)(2,1)S(1)} %collective-permute-done), channel_id=1, source_target_pairs={{0,48},{8,56},{16,0},{24,8},{32,16},{40,24},{48,32},{56,40},{64,11... | collective-permute-start | bytes 786440 | tf_op jit(solution)/shard_map/ppermute | solution.py:486
  18.6 7.7 %copy-start.4 = (bf16[1024,128]{1,0:T(8,128)(2,1)S(1)}, bf16[1024,128]{1,0:T(8,128)(2,1)}, u32[]{:S(2)}) copy-start(bf16[1024,128]{1,0:T(8,128)(2,1)} %shard_map.149) | copy-start | bytes 786436
  26.2 1.7 %copy-start.3 = (bf16[4,1024,128]{2,1,0:T(8,128)(2,1)}, bf16[4,1024,128]{2,1,0:T(8,128)(2,1)S(1)}, u32[]{:S(2)}) copy-start(bf16[4,1024,128]{2,1,0:T(8,128)(2,1)S(1)} %pad_maximum_fusion.1.refs_2_) | copy-start | bytes 3145732
  26.2 5.4 %collective-permute-start.8 = (bf16[4,1024,128]{2,1,0:T(8,128)(2,1)S(1)}, bf16[4,1024,128]{2,1,0:T(8,128)(2,1)}, u32[]{:S(2)}, u32[]{:S(2)}) collective-permute-start(bf16[4,1024,128]{2,1,0:T(8,128)(2,1)S(1)} %pad_maximum_fusion.1.refs_2_), channel_id=1, source_target_pairs={{0,8},{8,0},{16,24},{24,16},{32,40},{40,32},{48,56},{56,48},{64,72... | collective-permute-start | bytes 3145736 | tf_op jit(solution)/shard_map/ppermute | solution.py:490
  27.5 4.1 %collective-permute-start.7 = (bf16[4,1024,128]{2,1,0:T(8,128)(2,1)}, bf16[4,1024,128]{2,1,0:T(8,128)(2,1)}, u32[]{:S(2)}, u32[]{:S(2)}) collective-permute-start(bf16[4,1024,128]{2,1,0:T(8,128)(2,1)} %pad_maximum_fusion.refs_0_), channel_id=1, source_target_pairs={{0,8},{8,0},{16,24},{24,16},{32,40},{40,32},{48,56},{56,48},{64,72... | collective-permute-start | bytes 3145736 | tf_op jit(solution)/shard_map/ppermute | solution.py:490
  27.9 62.2 %all-to-all-start = ((bf16[16,4,64,256]{3,2,1,0:T(8,128)(2,1)}), bf16[16,4,64,256]{3,2,1,0:T(8,128)(2,1)S(1)}, u32[]{:S(2)}, u32[]{:S(2)}) async-start(bf16[16,4,64,256]{3,2,1,0:T(8,128)(2,1)} %bitcast.66), calls=%async_computation | async-start | bytes 4194304 | tf_op jit(solution)/shard_map/all_to_all | solution.py:551
  55.1 26.2 %collective-permute-start.12 = (bf16[4,192,512]{2,1,0:T(8,128)(2,1)}, bf16[4,192,512]{2,1,0:T(8,128)(2,1)S(1)}, u32[]{:S(2)}, u32[]{:S(2)}) collective-permute-start(bf16[4,192,512]{2,1,0:T(8,128)(2,1)} %get-tuple-element.54), channel_id=1, source_target_pairs={{0,4},{1,5},{2,6},{3,7},{4,0},{5,1},{6,2},{7,3},{8,12},{9,13},{10,... | collective-permute-start | bytes 2359304 | tf_op jit(solution)/shard_map/ppermute | solution.py:494
  58.8 21.4 %collective-permute-start.10 = (bf16[2,192,512]{2,1,0:T(8,128)(2,1)}, bf16[2,192,512]{2,1,0:T(8,128)(2,1)S(1)}, u32[]{:S(2)}, u32[]{:S(2)}) collective-permute-start(bf16[2,192,512]{2,1,0:T(8,128)(2,1)} %get-tuple-element.52), channel_id=1, source_target_pairs={{0,3},{1,2},{2,1},{3,0},{4,7},{5,6},{6,5},{7,4},{8,11},{9,10},{10,... | collective-permute-start | bytes 1179656 | tf_op jit(solution)/shard_map/ppermute | solution.py:494
  61.5 18.7 %collective-permute-start.11 = (bf16[2,192,512]{2,1,0:T(8,128)(2,1)}, bf16[2,192,512]{2,1,0:T(8,128)(2,1)S(1)}, u32[]{:S(2)}, u32[]{:S(2)}) collective-permute-start(bf16[2,192,512]{2,1,0:T(8,128)(2,1)} %get-tuple-element.53), channel_id=1, source_target_pairs={{0,2},{1,3},{2,0},{3,1},{4,6},{5,7},{6,4},{7,5},{8,10},{9,11},{10,... | collective-permute-start | bytes 1179656 | tf_op jit(solution)/shard_map/ppermute | solution.py:494
  62.3 19.0 %collective-permute-start.9 = (bf16[2,192,512]{2,1,0:T(8,128)(2,1)}, bf16[2,192,512]{2,1,0:T(8,128)(2,1)S(1)}, u32[]{:S(2)}, u32[]{:S(2)}) collective-permute-start(bf16[2,192,512]{2,1,0:T(8,128)(2,1)} %get-tuple-element.51), channel_id=1, source_target_pairs={{0,1},{1,0},{2,3},{3,2},{4,5},{5,4},{6,7},{7,6},{8,9},{9,8},{10,11... | collective-permute-start | bytes 1179656 | tf_op jit(solution)/shard_map/ppermute | solution.py:494
  62.9 1.0 copy-start
  80.2 7.8 %copy-start.6 = (bf16[2,192,512]{2,1,0:T(8,128)(2,1)}, bf16[2,192,512]{2,1,0:T(8,128)(2,1)S(1)}, u32[]{:S(2)}) copy-start(bf16[2,192,512]{2,1,0:T(8,128)(2,1)S(1)} %collective-permute-done.10) | copy-start | bytes 1179652
  80.2 7.8 %copy-start.7 = (bf16[2,192,512]{2,1,0:T(8,128)(2,1)}, bf16[2,192,512]{2,1,0:T(8,128)(2,1)S(1)}, u32[]{:S(2)}) copy-start(bf16[2,192,512]{2,1,0:T(8,128)(2,1)S(1)} %collective-permute-done.11) | copy-start | bytes 1179652
  81.3 6.7 %copy-start.8 = (bf16[2,192,512]{2,1,0:T(8,128)(2,1)}, bf16[2,192,512]{2,1,0:T(8,128)(2,1)S(1)}, u32[]{:S(2)}) copy-start(bf16[2,192,512]{2,1,0:T(8,128)(2,1)S(1)} %collective-permute-done.9) | copy-start | bytes 1179652
  81.3 6.7 %copy-start.5 = (bf16[4,192,512]{2,1,0:T(8,128)(2,1)}, bf16[4,192,512]{2,1,0:T(8,128)(2,1)S(1)}, u32[]{:S(2)}) copy-start(bf16[4,192,512]{2,1,0:T(8,128)(2,1)S(1)} %collective-permute-done.12) | copy-start | bytes 2359300
  82.4 9.2 %collective-permute-start.14 = (bf16[96,512]{1,0:T(8,128)(2,1)}, bf16[96,512]{1,0:T(8,128)(2,1)}, u32[]{:S(2)}, u32[]{:S(2)}) collective-permute-start(bf16[96,512]{1,0:T(8,128)(2,1)} %get-tuple-element.78), channel_id=1, source_target_pairs={{0,1},{1,0},{2,3},{3,2},{4,5},{5,4},{6,7},{7,6},{8,9},{9,8},{10,11... | collective-permute-start | bytes 294920 | tf_op jit(solution)/shard_map/ppermute | solution.py:494
  83.9 8.5 %collective-permute-start.15 = (bf16[96,512]{1,0:T(8,128)(2,1)}, bf16[96,512]{1,0:T(8,128)(2,1)}, u32[]{:S(2)}, u32[]{:S(2)}) collective-permute-start(bf16[96,512]{1,0:T(8,128)(2,1)} %get-tuple-element.77), channel_id=1, source_target_pairs={{0,3},{1,2},{2,1},{3,0},{4,7},{5,6},{6,5},{7,4},{8,11},{9,10},{10,... | collective-permute-start | bytes 294920 | tf_op jit(solution)/shard_map/ppermute | solution.py:494
  86.0 7.2 %collective-permute-start.16 = (bf16[96,512]{1,0:T(8,128)(2,1)}, bf16[96,512]{1,0:T(8,128)(2,1)}, u32[]{:S(2)}, u32[]{:S(2)}) collective-permute-start(bf16[96,512]{1,0:T(8,128)(2,1)} %get-tuple-element.76), channel_id=1, source_target_pairs={{0,2},{1,3},{2,0},{3,1},{4,6},{5,7},{6,4},{7,5},{8,10},{9,11},{10,... | collective-permute-start | bytes 294920 | tf_op jit(solution)/shard_map/ppermute | solution.py:494
  86.6 9.8 %collective-permute-start.20 = (bf16[96,512]{1,0:T(8,128)(2,1)}, bf16[96,512]{1,0:T(8,128)(2,1)}, u32[]{:S(2)}, u32[]{:S(2)}) collective-permute-start(bf16[96,512]{1,0:T(8,128)(2,1)} %get-tuple-element.75), channel_id=1, source_target_pairs={{0,1},{1,0},{2,3},{3,2},{4,5},{5,4},{6,7},{7,6},{8,9},{9,8},{10,11... | collective-permute-start | bytes 294920 | tf_op jit(solution)/shard_map/ppermute | solution.py:494
  88.0 9.1 %collective-permute-start.21 = (bf16[96,512]{1,0:T(8,128)(2,1)}, bf16[96,512]{1,0:T(8,128)(2,1)}, u32[]{:S(2)}, u32[]{:S(2)}) collective-permute-start(bf16[96,512]{1,0:T(8,128)(2,1)} %get-tuple-element.74), channel_id=1, source_target_pairs={{0,3},{1,2},{2,1},{3,0},{4,7},{5,6},{6,5},{7,4},{8,11},{9,10},{10,... | collective-permute-start | bytes 294920 | tf_op jit(solution)/shard_map/ppermute | solution.py:494
  91.6 25.6 %copy-start.1 = (s32[64,16]{0,1:T(8,128)S(1)}, s32[64,16]{0,1:T(8,128)}, u32[]{:S(2)}) copy-start(s32[64,16]{0,1:T(8,128)} %param.20) | copy-start | bytes 12292
  91.6 25.6 %copy-start.2 = (s32[64,16]{0,1:T(8,128)S(1)}, s32[64,16]{0,1:T(8,128)}, u32[]{:S(2)}) copy-start(s32[64,16]{0,1:T(8,128)} %param.21) | copy-start | bytes 12292
  91.6 7.2 %collective-permute-start.22 = (bf16[96,512]{1,0:T(8,128)(2,1)S(1)}, bf16[96,512]{1,0:T(8,128)(2,1)S(1)}, u32[]{:S(2)}, u32[]{:S(2)}) collective-permute-start(bf16[96,512]{1,0:T(8,128)(2,1)S(1)} %get-tuple-element.73), channel_id=1, source_target_pairs={{0,2},{1,3},{2,0},{3,1},{4,6},{5,7},{6,4},{7,5},{8,10},{9,11},{10,... | collective-permute-start | bytes 294920 | tf_op jit(solution)/shard_map/ppermute | solution.py:494
  92.4 15.0 %collective-permute-start.13 = (bf16[2,192,512]{2,1,0:T(8,128)(2,1)S(1)}, bf16[2,192,512]{2,1,0:T(8,128)(2,1)S(1)}, u32[]{:S(2)}, u32[]{:S(2)}) collective-permute-start(bf16[2,192,512]{2,1,0:T(8,128)(2,1)S(1)} %add_convert_fusion.1), channel_id=1, source_target_pairs={{0,4},{1,5},{2,6},{3,7},{4,0},{5,1},{6,2},{7,3},{8,12},{9,13},{10,... | collective-permute-start | bytes 1179656 | tf_op jit(solution)/shard_map/ppermute | solution.py:494
  94.3 6.4 %collective-permute-start.17 = (bf16[96,512]{1,0:T(8,128)(2,1)S(1)}, bf16[96,512]{1,0:T(8,128)(2,1)S(1)}, u32[]{:S(2)}, u32[]{:S(2)}) collective-permute-start(bf16[96,512]{1,0:T(8,128)(2,1)S(1)} %fusion.2), channel_id=1, source_target_pairs={{0,2},{1,3},{2,0},{3,1},{4,6},{5,7},{6,4},{7,5},{8,10},{9,11},{10,... | collective-permute-start | bytes 294920 | tf_op jit(solution)/shard_map/ppermute | solution.py:494
  96.4 6.3 %collective-permute-start.18 = (bf16[96,512]{1,0:T(8,128)(2,1)S(1)}, bf16[96,512]{1,0:T(8,128)(2,1)S(1)}, u32[]{:S(2)}, u32[]{:S(2)}) collective-permute-start(bf16[96,512]{1,0:T(8,128)(2,1)S(1)} %fusion.2), channel_id=1, source_target_pairs={{0,1},{1,0},{2,3},{3,2},{4,5},{5,4},{6,7},{7,6},{8,9},{9,8},{10,11... | collective-permute-start | bytes 294920 | tf_op jit(solution)/shard_map/ppermute | solution.py:494
  97.0 7.3 %collective-permute-start.19 = (bf16[96,512]{1,0:T(8,128)(2,1)S(1)}, bf16[96,512]{1,0:T(8,128)(2,1)S(1)}, u32[]{:S(2)}, u32[]{:S(2)}) collective-permute-start(bf16[96,512]{1,0:T(8,128)(2,1)S(1)} %fusion.2), channel_id=1, source_target_pairs={{0,3},{1,2},{2,1},{3,0},{4,7},{5,6},{6,5},{7,4},{8,11},{9,10},{10,... | collective-permute-start | bytes 294920 | tf_op jit(solution)/shard_map/ppermute | solution.py:494
  99.8 7.7 %collective-permute-start.23 = (bf16[96,512]{1,0:T(8,128)(2,1)S(1)}, bf16[96,512]{1,0:T(8,128)(2,1)S(1)}, u32[]{:S(2)}, u32[]{:S(2)}) collective-permute-start(bf16[96,512]{1,0:T(8,128)(2,1)S(1)} %add_convert_fusion.2), channel_id=1, source_target_pairs={{0,1},{1,0},{2,3},{3,2},{4,5},{5,4},{6,7},{7,6},{8,9},{9,8},{10,11... | collective-permute-start | bytes 294920 | tf_op jit(solution)/shard_map/ppermute | solution.py:494
  100.7 6.8 %collective-permute-start.24 = (bf16[96,512]{1,0:T(8,128)(2,1)S(1)}, bf16[96,512]{1,0:T(8,128)(2,1)S(1)}, u32[]{:S(2)}, u32[]{:S(2)}) collective-permute-start(bf16[96,512]{1,0:T(8,128)(2,1)S(1)} %add_convert_fusion.2), channel_id=1, source_target_pairs={{0,3},{1,2},{2,1},{3,0},{4,7},{5,6},{6,5},{7,4},{8,11},{9,10},{10,... | collective-permute-start | bytes 294920 | tf_op jit(solution)/shard_map/ppermute | solution.py:494
  102.8 6.1 %collective-permute-start.25 = (bf16[96,512]{1,0:T(8,128)(2,1)S(1)}, bf16[96,512]{1,0:T(8,128)(2,1)S(1)}, u32[]{:S(2)}, u32[]{:S(2)}) collective-permute-start(bf16[96,512]{1,0:T(8,128)(2,1)S(1)} %add_convert_fusion.2), channel_id=1, source_target_pairs={{0,2},{1,3},{2,0},{3,1},{4,6},{5,7},{6,4},{7,5},{8,10},{9,11},{10,... | collective-permute-start | bytes 294920 | tf_op jit(solution)/shard_map/ppermute | solution.py:494
  104.4 19.3 %collective-permute-start.26 = (bf16[4,96,512]{2,1,0:T(8,128)(2,1)S(1)}, bf16[4,96,512]{2,1,0:T(8,128)(2,1)}, u32[]{:S(2)}, u32[]{:S(2)}) collective-permute-start(bf16[4,96,512]{2,1,0:T(8,128)(2,1)S(1)} %pad_maximum_fusion.2.refs_1_), channel_id=1, source_target_pairs={{0,4},{1,5},{2,6},{3,7},{4,0},{5,1},{6,2},{7,3},{8,12},{9,13},{10,... | collective-permute-start | bytes 1179656 | tf_op jit(solution)/shard_map/ppermute | solution.py:494
  108.9 14.7 %collective-permute-start.27 = (bf16[4,96,512]{2,1,0:T(8,128)(2,1)S(1)}, bf16[4,96,512]{2,1,0:T(8,128)(2,1)}, u32[]{:S(2)}, u32[]{:S(2)}) collective-permute-start(bf16[4,96,512]{2,1,0:T(8,128)(2,1)S(1)} %pad_maximum_fusion.3.refs_2_), channel_id=1, source_target_pairs={{0,4},{1,5},{2,6},{3,7},{4,0},{5,1},{6,2},{7,3},{8,12},{9,13},{10,... | collective-permute-start | bytes 1179656 | tf_op jit(solution)/shard_map/ppermute | solution.py:494
  113.1 11.3 %collective-permute-start.28 = (bf16[2,192,512]{2,1,0:T(8,128)(2,1)S(1)}, bf16[2,192,512]{2,1,0:T(8,128)(2,1)}, u32[]{:S(2)}, u32[]{:S(2)}) collective-permute-start(bf16[2,192,512]{2,1,0:T(8,128)(2,1)S(1)} %add_convert_fusion.refs_0_), channel_id=1, source_target_pairs={{0,2},{1,3},{2,0},{3,1},{4,6},{5,7},{6,4},{7,5},{8,10},{9,11},{10,... | collective-permute-start | bytes 1179656 | tf_op jit(solution)/shard_map/ppermute | solution.py:494
  113.5 14.1 %collective-permute-start.29 = (bf16[2,192,512]{2,1,0:T(8,128)(2,1)S(1)}, bf16[2,192,512]{2,1,0:T(8,128)(2,1)}, u32[]{:S(2)}, u32[]{:S(2)}) collective-permute-start(bf16[2,192,512]{2,1,0:T(8,128)(2,1)S(1)} %add_convert_fusion.refs_0_), channel_id=1, source_target_pairs={{0,1},{1,0},{2,3},{3,2},{4,5},{5,4},{6,7},{7,6},{8,9},{9,8},{10,11... | collective-permute-start | bytes 1179656 | tf_op jit(solution)/shard_map/ppermute | solution.py:494
  114.5 14.0 %collective-permute-start.30 = (bf16[2,192,512]{2,1,0:T(8,128)(2,1)S(1)}, bf16[2,192,512]{2,1,0:T(8,128)(2,1)}, u32[]{:S(2)}, u32[]{:S(2)}) collective-permute-start(bf16[2,192,512]{2,1,0:T(8,128)(2,1)S(1)} %add_convert_fusion.refs_0_), channel_id=1, source_target_pairs={{0,3},{1,2},{2,1},{3,0},{4,7},{5,6},{6,5},{7,4},{8,11},{9,10},{10,... | collective-permute-start | bytes 1179656 | tf_op jit(solution)/shard_map/ppermute | solution.py:494
